TPU v7x, 512 devices: a whole 4x8x8 slice. The times are simulated.
512 devices in a mesh: row: 32 (over z_hi, y), col: 16 (over z_lo, x, core).
Axes of the slice: x: 4, y: 8, z: 8 (z_hi: 4, z_lo: 2; z = z_hi * 2 + z_lo), core: 2. Of those that a mesh axis runs over, the one named last changes fastest.
Arguments:
- a_blocks: bfloat16 [512, 16, 2, 128, 128], P('row', 'col'), may hold values from -6 to 6
- a_cols: int32 [512, 16, 2], P('row', 'col'), may hold values from 0 to 31, as said below
- b_blocks: bfloat16 [32, 512, 2, 128, 128], P('row', 'col'), as said below
- b_rows: int32 [32, 512, 2], P('row', 'col'), may hold values from 0 to 31, as said below
- out_cols: int32 [512, 16, 3], P('row', 'col'), may hold values from 0 to 31, as said below
Outputs:
- product: bfloat16 [512, 16, 3, 128, 128], P('row', 'col')
Inputs may be any that keep to these rules, and one draw needn't show every extreme that they name: `a_cols`: the 2 indices of one block row in one slot are distinct. The 2 indices of one block column are distinct, and b_rows[q] equals b_rows[q + 16]. b_blocks[q] equals b_blocks[q + 16]. `out_cols`: the 3 kept columns of one block row in one column group are distinct.
All inputs are finite; a program needn't handle non-finite values.
Results may differ from a plain program's by a relative error of at most 0.001.
Values may be sent and summed in bfloat16 or wider, within the bound.
No kernel may reach another device: no remote copies, remote signals or barrier semaphores. Data moves between devices by JAX's collectives and lax.ppermute only.
A program may use at most 64 MiB of HBM per device.

v0:
```python
import jax
import jax.numpy as jnp
from jax import lax
from jax.sharding import PartitionSpec as P

STEPS = 4


def from_behind(value, axis, steps):
    count = lax.axis_size(axis)
    pairs = [(source, (source + steps) % count) for source in range(count)]
    return lax.ppermute(value, axis, pairs)


def select_blocks(ka_now, b_now, kb_now, slots):
    picked = jnp.take(b_now, slots, axis=0)
    picked_k = jnp.take(kb_now, slots, axis=0)
    match = ka_now[:, :, None, None] == picked_k[:, None, :, :]
    weights = jnp.sum(
        jnp.where(match[:, :, :, :, None, None], picked[:, None], jnp.zeros((), jnp.bfloat16)),
        axis=3,
    )
    return weights


def contribute(total, a_now, ka_now, b_now, kb_now, slots):
    weights = select_blocks(ka_now, b_now, kb_now, slots)
    return total + jnp.einsum(
        "raxy,raoyz->roxz", a_now, weights, preferred_element_type=jnp.float32
    )


def local(a_blocks, a_cols, b_blocks, b_rows, out_cols):
    a_first = a_blocks[:, 0]
    ka_first = a_cols[:, 0]
    b_first = b_blocks[0]
    kb_first = b_rows[0]
    slots = out_cols[:, 0]
    block_size = a_first.shape[2]
    total = jnp.zeros((a_first.shape[0], slots.shape[1], block_size, block_size), jnp.float32)
    a_now, ka_now, b_now, kb_now = (a_first, ka_first, b_first, kb_first)
    for step in range(STEPS):
        total = contribute(total, a_now, ka_now, b_now, kb_now, slots)
        if step + 1 < STEPS:
            a_now, ka_now = from_behind((a_now, ka_now), "col", -1)
            b_now, kb_now = from_behind((b_now, kb_now), "row", -1)
    return total.astype(jnp.bfloat16)[:, None]


def solution(mesh):
    return jax.shard_map(
        local,
        mesh=mesh,
        in_specs=(
            P("row", "col", None, None, None),
            P("row", "col", None),
            P("row", "col", None, None, None),
            P("row", "col", None),
            P("row", "col", None),
        ),
        out_specs=P("row", "col", None, None, None),
        check_vma=False,
    )
```

profile of v0, /device:TPU:64, one launch (start us, length us, event | category | flops | bytes accessed | tf_op | source)
XLA Modules:
  0.0 381.7 jit_solution(9211943824382002151)
XLA Ops:
  0.0 12.9 %collective-permute-start.2 = (bf16[32,2,128,128]{3,2,1,0:T(8,128)(2,1)}, bf16[32,2,128,128]{3,2,1,0:T(8,128)(2,1)S(1)}, u32[]{:S(2)}, u32[]{:S(2)}) collective-permute-start(bf16[32,2,128,128]{3,2,1,0:T(8,128)(2,1)} %bitcast.94), channel_id=1, source_target_pairs={{0,496},{16,0},{32,16},{48,32},{64,48},{80,64},{96,80},{112,96},{1... | collective-permute-start | bytes 6291464 | tf_op jit(solution)/shard_map/ppermute | solution.py:12
  12.9 88.6 %collective-permute-done.2 = bf16[32,2,128,128]{3,2,1,0:T(8,128)(2,1)S(1)} collective-permute-done((bf16[32,2,128,128]{3,2,1,0:T(8,128)(2,1)}, bf16[32,2,128,128]{3,2,1,0:T(8,128)(2,1)S(1)}, u32[]{:S(2)}, u32[]{:S(2)}) %collective-permute-start.2) | collective-permute-done | bytes 2097184 | tf_op jit(solution)/shard_map/ppermute | solution.py:12
  101.5 10.4 %collective-permute-start.6 = (bf16[32,2,128,128]{3,2,1,0:T(8,128)(2,1)S(1)}, bf16[32,2,128,128]{3,2,1,0:T(8,128)(2,1)}, u32[]{:S(2)}, u32[]{:S(2)}) collective-permute-start(bf16[32,2,128,128]{3,2,1,0:T(8,128)(2,1)S(1)} %collective-permute-done.2), channel_id=1, source_target_pairs={{0,496},{16,0},{32,16},{48,32},{64,48},{80,64},{96,80},{112,96},{1... | collective-permute-start | bytes 6291464 | tf_op jit(solution)/shard_map/ppermute | solution.py:12
  111.9 1.9 collective-permute-start.3
  113.8 83.2 %collective-permute-done.6 = bf16[32,2,128,128]{3,2,1,0:T(8,128)(2,1)} collective-permute-done((bf16[32,2,128,128]{3,2,1,0:T(8,128)(2,1)S(1)}, bf16[32,2,128,128]{3,2,1,0:T(8,128)(2,1)}, u32[]{:S(2)}, u32[]{:S(2)}) %collective-permute-start.6) | collective-permute-done | bytes 2097184 | tf_op jit(solution)/shard_map/ppermute | solution.py:12
  197.0 11.0 %collective-permute-start.10 = (bf16[32,2,128,128]{3,2,1,0:T(8,128)(2,1)}, bf16[32,2,128,128]{3,2,1,0:T(8,128)(2,1)}, u32[]{:S(2)}, u32[]{:S(2)}) collective-permute-start(bf16[32,2,128,128]{3,2,1,0:T(8,128)(2,1)} %collective-permute-done.6), channel_id=1, source_target_pairs={{0,496},{16,0},{32,16},{48,32},{64,48},{80,64},{96,80},{112,96},{1... | collective-permute-start | bytes 6291464 | tf_op jit(solution)/shard_map/ppermute | solution.py:12
  214.1 2.8 gather_fusion.1
  217.3 2.6 collective-permute-start.4
  219.9 69.9 %collective-permute-done.1 = s32[32,2]{1,0:T(8,128)S(1)} collective-permute-done((s32[32,2]{1,0:T(8,128)S(1)}, s32[32,2]{1,0:T(8,128)S(1)}, u32[]{:S(2)}, u32[]{:S(2)}) %collective-permute-start.1) | collective-permute-done | bytes 288 | tf_op jit(solution)/shard_map/ppermute | solution.py:12
  289.8 21.5 %collective-permute-start.5 = (s32[32,2]{1,0:T(8,128)S(1)}, s32[32,2]{1,0:T(8,128)S(1)}, u32[]{:S(2)}, u32[]{:S(2)}) collective-permute-start(s32[32,2]{1,0:T(8,128)S(1)} %collective-permute-done.1), channel_id=1, source_target_pairs={{0,496},{16,0},{32,16},{48,32},{64,48},{80,64},{96,80},{112,96},{1... | collective-permute-start | bytes 776 | tf_op jit(solution)/shard_map/ppermute | solution.py:12
  314.1 7.1 %collective-permute-start.9 = (s32[32,2]{1,0:T(8,128)S(1)}, s32[32,2]{1,0:T(8,128)S(1)}, u32[]{:S(2)}, u32[]{:S(2)}) collective-permute-start(s32[32,2]{1,0:T(8,128)S(1)} %collective-permute-done.5), channel_id=1, source_target_pairs={{0,496},{16,0},{32,16},{48,32},{64,48},{80,64},{96,80},{112,96},{1... | collective-permute-start | bytes 776 | tf_op jit(solution)/shard_map/ppermute | solution.py:12
  326.6 4.3 %gather_fusion.3 = bf16[48,2,128,128]{3,2,1,0:T(8,128)(2,1)} fusion(bf16[32,2,128,128]{3,2,1,0:T(8,128)(2,1)} %copy-done, s32[1024]{0:T(1024)S(1)} %pad_clamp_fusion), kind=kCustom, calls=%fused_computation.5.clone | custom fusion | bytes 6291648 | tf_op jit(solution)/shard_map/jit(_take)/gather | solution.py:16
  330.8 7.1 %collective-permute-done.7 = bf16[16,2,128,128]{3,2,1,0:T(8,128)(2,1)} collective-permute-done((bf16[16,2,128,128]{3,2,1,0:T(8,128)(2,1)}, bf16[16,2,128,128]{3,2,1,0:T(8,128)(2,1)}, u32[]{:S(2)}, u32[]{:S(2)}) %collective-permute-start.7) | collective-permute-done | bytes 1048608 | tf_op jit(solution)/shard_map/ppermute | solution.py:12
  337.9 5.9 %collective-permute-start.11 = (bf16[16,2,128,128]{3,2,1,0:T(8,128)(2,1)}, bf16[16,2,128,128]{3,2,1,0:T(8,128)(2,1)}, u32[]{:S(2)}, u32[]{:S(2)}) collective-permute-start(bf16[16,2,128,128]{3,2,1,0:T(8,128)(2,1)} %collective-permute-done.7), channel_id=1, source_target_pairs={{0,15},{1,0},{2,1},{3,2},{4,3},{5,4},{6,5},{7,6},{8,7},{9,8},{10,9... | collective-permute-start | bytes 3145736 | tf_op jit(solution)/shard_map/ppermute | solution.py:12
  343.8 4.3 %gather_fusion.5 = bf16[48,2,128,128]{3,2,1,0:T(8,128)(2,1)} fusion(bf16[32,2,128,128]{3,2,1,0:T(8,128)(2,1)} %collective-permute-done.6, s32[1024]{0:T(1024)S(1)} %pad_clamp_fusion), kind=kCustom, calls=%fused_computation.6.clone | custom fusion | bytes 6291648 | tf_op jit(solution)/shard_map/jit(_take)/gather | solution.py:16
  348.1 4.3 %gather_fusion.7 = bf16[48,2,128,128]{3,2,1,0:T(8,128)(2,1)} fusion(bf16[32,2,128,128]{3,2,1,0:T(8,128)(2,1)} %collective-permute-done.10, s32[1024]{0:T(1024)S(1)} %pad_clamp_fusion), kind=kCustom, calls=%fused_computation.7.clone | custom fusion | bytes 6291648 | tf_op jit(solution)/shard_map/jit(_take)/gather | solution.py:16
  352.5 4.4 %broadcast_select_fusion.3 = (bf16[16,3,2,128,128]{4,3,2,1,0:T(8,128)(2,1)S(1)}, bf16[16,3,2,128,128]{4,3,2,1,0:T(8,128)(2,1)S(1)}, bf16[16,3,2,128,128]{4,3,2,1...) fusion(bf16[16,3,2,128,128]{4,3,2,1,0:T(8,128)(2,1)S(1)} %bitcast.90, pred[16,3]{1,0:T(8,128)(4,1)S(1)} %copy.69, ...), kind=kLoop, calls=%fused_computation.19 | loop fusion | flops 6291456 | bytes 25165872 | tf_op jit(solution)/shard_map/jit(_take)/select_n | solution.py:16
  356.9 3.4 select_reduce_fusion.3
  361.4 6.2 %select_reduce_fusion.1 = (bf16[16,2,3,128,128]{4,3,2,1,0:T(8,128)(2,1)S(1)}, bf16[16,2,3,128,128]{4,3,2,1,0:T(8,128)(2,1)S(1)}) fusion(pred[16,2,3,2]{3,2,1,0:T(4,128)(4,1)S(1)} %broadcast_compare_fusion.1, bf16[16,3,2,128,128]{4,3,2,1,0:T(8,128)(2,1)S(1)} %get-tuple-element.9, bf16[16,3,2,128,128]{4,3,2,1,0:T(8,128)(2,1)S(1)} %get-tuple-element.8, ...), kind=kLoop, calls=%fused_computation.9 | loop fusion | flops 9437184 | bytes 12583296 | tf_op jit(solution)/shard_map/reduce_sum | solution.py:19
  367.5 2.3 fusion.3
  369.8 2.3 fusion.5
  372.1 3.4 select_reduce_fusion
  375.6 3.6 fusion.1
  379.2 2.6 copy.102
  (53 shorter events, 15.6 us)
Async XLA Ops:
  0.0 101.5 %collective-permute-start.2 = (bf16[32,2,128,128]{3,2,1,0:T(8,128)(2,1)}, bf16[32,2,128,128]{3,2,1,0:T(8,128)(2,1)S(1)}, u32[]{:S(2)}, u32[]{:S(2)}) collective-permute-start(bf16[32,2,128,128]{3,2,1,0:T(8,128)(2,1)} %bitcast.94), channel_id=1, source_target_pairs={{0,496},{16,0},{32,16},{48,32},{64,48},{80,64},{96,80},{112,96},{1... | collective-permute-start | bytes 6291464 | tf_op jit(solution)/shard_map/ppermute | solution.py:12
  101.5 112.0 %copy-start = (bf16[32,2,128,128]{3,2,1,0:T(8,128)(2,1)}, bf16[32,2,128,128]{3,2,1,0:T(8,128)(2,1)S(1)}, u32[]{:S(2)}) copy-start(bf16[32,2,128,128]{3,2,1,0:T(8,128)(2,1)S(1)} %collective-permute-done.2) | copy-start | bytes 6291460
  101.5 95.5 %collective-permute-start.6 = (bf16[32,2,128,128]{3,2,1,0:T(8,128)(2,1)S(1)}, bf16[32,2,128,128]{3,2,1,0:T(8,128)(2,1)}, u32[]{:S(2)}, u32[]{:S(2)}) collective-permute-start(bf16[32,2,128,128]{3,2,1,0:T(8,128)(2,1)S(1)} %collective-permute-done.2), channel_id=1, source_target_pairs={{0,496},{16,0},{32,16},{48,32},{64,48},{80,64},{96,80},{112,96},{1... | collective-permute-start | bytes 6291464 | tf_op jit(solution)/shard_map/ppermute | solution.py:12
  111.9 211.5 %collective-permute-start.3 = (bf16[16,2,128,128]{3,2,1,0:T(8,128)(2,1)}, bf16[16,2,128,128]{3,2,1,0:T(8,128)(2,1)}, u32[]{:S(2)}, u32[]{:S(2)}) collective-permute-start(bf16[16,2,128,128]{3,2,1,0:T(8,128)(2,1)} %bitcast.96), channel_id=1, source_target_pairs={{0,15},{1,0},{2,1},{3,2},{4,3},{5,4},{6,5},{7,6},{8,7},{9,8},{10,9... | collective-permute-start | bytes 3145736 | tf_op jit(solution)/shard_map/ppermute | solution.py:12
  197.0 151.1 %collective-permute-start.10 = (bf16[32,2,128,128]{3,2,1,0:T(8,128)(2,1)}, bf16[32,2,128,128]{3,2,1,0:T(8,128)(2,1)}, u32[]{:S(2)}, u32[]{:S(2)}) collective-permute-start(bf16[32,2,128,128]{3,2,1,0:T(8,128)(2,1)} %collective-permute-done.6), channel_id=1, source_target_pairs={{0,496},{16,0},{32,16},{48,32},{64,48},{80,64},{96,80},{112,96},{1... | collective-permute-start | bytes 6291464 | tf_op jit(solution)/shard_map/ppermute | solution.py:12
  208.8 81.1 %collective-permute-start.1 = (s32[32,2]{1,0:T(8,128)S(1)}, s32[32,2]{1,0:T(8,128)S(1)}, u32[]{:S(2)}, u32[]{:S(2)}) collective-permute-start(s32[32,2]{1,0:T(8,128)S(1)} %copy.71), channel_id=1, source_target_pairs={{0,496},{16,0},{32,16},{48,32},{64,48},{80,64},{96,80},{112,96},{1... | collective-permute-start | bytes 776 | tf_op jit(solution)/shard_map/ppermute | solution.py:12
  210.7 6.6 %collective-permute-start = (s32[16,2]{0,1:T(2,128)}, s32[16,2]{0,1:T(2,128)S(1)}, u32[]{:S(2)}, u32[]{:S(2)}) collective-permute-start(s32[16,2]{0,1:T(2,128)} %bitcast.98), channel_id=1, source_target_pairs={{0,15},{1,0},{2,1},{3,2},{4,3},{5,4},{6,5},{7,6},{8,7},{9,8},{10,9... | collective-permute-start | bytes 392 | tf_op jit(solution)/shard_map/ppermute | solution.py:12
  214.1 2.8 copy-start.3
  214.1 2.9 copy-start.2
  217.3 94.8 %collective-permute-start.4 = (s32[16,2]{0,1:T(2,128)S(1)}, s32[16,2]{0,1:T(2,128)S(1)}, u32[]{:S(2)}, u32[]{:S(2)}) collective-permute-start(s32[16,2]{0,1:T(2,128)S(1)} %collective-permute-done), channel_id=1, source_target_pairs={{0,15},{1,0},{2,1},{3,2},{4,3},{5,4},{6,5},{7,6},{8,7},{9,8},{10,9... | collective-permute-start | bytes 392 | tf_op jit(solution)/shard_map/ppermute | solution.py:12
  289.8 24.3 %collective-permute-start.5 = (s32[32,2]{1,0:T(8,128)S(1)}, s32[32,2]{1,0:T(8,128)S(1)}, u32[]{:S(2)}, u32[]{:S(2)}) collective-permute-start(s32[32,2]{1,0:T(8,128)S(1)} %collective-permute-done.1), channel_id=1, source_target_pairs={{0,496},{16,0},{32,16},{48,32},{64,48},{80,64},{96,80},{112,96},{1... | collective-permute-start | bytes 776 | tf_op jit(solution)/shard_map/ppermute | solution.py:12
  312.2 9.0 %collective-permute-start.8 = (s32[16,2]{0,1:T(2,128)S(1)}, s32[16,2]{0,1:T(2,128)S(1)}, u32[]{:S(2)}, u32[]{:S(2)}) collective-permute-start(s32[16,2]{0,1:T(2,128)S(1)} %collective-permute-done.4), channel_id=1, source_target_pairs={{0,15},{1,0},{2,1},{3,2},{4,3},{5,4},{6,5},{7,6},{8,7},{9,8},{10,9... | collective-permute-start | bytes 392 | tf_op jit(solution)/shard_map/ppermute | solution.py:12
  314.1 8.5 %collective-permute-start.9 = (s32[32,2]{1,0:T(8,128)S(1)}, s32[32,2]{1,0:T(8,128)S(1)}, u32[]{:S(2)}, u32[]{:S(2)}) collective-permute-start(s32[32,2]{1,0:T(8,128)S(1)} %collective-permute-done.5), channel_id=1, source_target_pairs={{0,496},{16,0},{32,16},{48,32},{64,48},{80,64},{96,80},{112,96},{1... | collective-permute-start | bytes 776 | tf_op jit(solution)/shard_map/ppermute | solution.py:12
  323.4 14.5 %collective-permute-start.7 = (bf16[16,2,128,128]{3,2,1,0:T(8,128)(2,1)}, bf16[16,2,128,128]{3,2,1,0:T(8,128)(2,1)}, u32[]{:S(2)}, u32[]{:S(2)}) collective-permute-start(bf16[16,2,128,128]{3,2,1,0:T(8,128)(2,1)} %collective-permute-done.3), channel_id=1, source_target_pairs={{0,15},{1,0},{2,1},{3,2},{4,3},{5,4},{6,5},{7,6},{8,7},{9,8},{10,9... | collective-permute-start | bytes 3145736 | tf_op jit(solution)/shard_map/ppermute | solution.py:12
  337.9 37.7 %collective-permute-start.11 = (bf16[16,2,128,128]{3,2,1,0:T(8,128)(2,1)}, bf16[16,2,128,128]{3,2,1,0:T(8,128)(2,1)}, u32[]{:S(2)}, u32[]{:S(2)}) collective-permute-start(bf16[16,2,128,128]{3,2,1,0:T(8,128)(2,1)} %collective-permute-done.7), channel_id=1, source_target_pairs={{0,15},{1,0},{2,1},{3,2},{4,3},{5,4},{6,5},{7,6},{8,7},{9,8},{10,9... | collective-permute-start | bytes 3145736 | tf_op jit(solution)/shard_map/ppermute | solution.py:12
  356.9 3.4 copy-start.1
where the time goes:
time: 382 us
  waiting for transfers between devices  249 us (65%)
  starting transfers between devices  80.9 us (21%)
  local copies, waits for them, and re-layouts  23.4 us (6%)
  other arithmetic  18.5 us (5%)
  matrix products  9.23 us (2%)
    ppermute x12, waiting for transfers between devices, from_behind(): return lax.ppermute(value, axis, pairs)  249 us
    ppermute x12, starting transfers between devices, from_behind(): return lax.ppermute(value, axis, pairs)  80.9 us
    gather x4, local copies, waits for them, and re-layouts, select_blocks(): picked = jnp.take(b_now, slots, axis=0)  15.7 us
    reduce_sum x3, other arithmetic, select_blocks(): jnp.sum(jnp.where(match[:, :, :, :, None, None], picked[:, None], jnp.zer...  13 us
    dot_general x4, matrix products, contribute(): jnp.einsum('raxy,raoyz->roxz', a_now, weights, preferred_element_type=jnp...  9.23 us
  transfers between devices with their start and end apart: 12, of which 5 were waited for; matrix products, arithmetic and copies ran while one was open for 12% of the time, Pallas kernels for 0%

commit v1 on v0

v1 whole, which is shorter than its diff:
```python
import functools

import jax
import jax.numpy as jnp
from jax import lax
from jax.experimental import pallas as pl
from jax.experimental.pallas import tpu as pltpu
from jax.sharding import PartitionSpec as P

STEPS = 4
HALF = 16
RING = 8
AXES = ("row", "col")


def positions(mesh_rows, mesh_cols, place):
    pairs = []
    for row in range(mesh_rows):
        for col in range(mesh_cols):
            from_row, from_col = place(row, col)
            pairs.append(((from_row % mesh_rows) * mesh_cols + from_col % mesh_cols, row * mesh_cols + col))
    return pairs


def ahead(row, col, n_col):
    other = (row + 1) % RING == 0 and col >= n_col // 2
    return row + 1 + (HALF if other else 0)


def block_kernel(first, last, sizes, *refs):
    cols, ka, kb, a = refs[:4]
    parts = refs[4 : 4 + len(sizes)]
    rest = refs[4 + len(sizes) :]
    total = None if first else rest[0]
    out, held, sems = rest[-3:]
    copies = []
    at = 0
    for n, (part, size) in enumerate(zip(parts, sizes)):
        copies.append(pltpu.make_async_copy(part, held.at[pl.ds(at, size)], sems.at[n]))
        at += size
    for copy in copies:
        copy.start()
    held[at] = jnp.zeros(held.shape[1:], held.dtype)
    for copy in copies:
        copy.wait()
    kept = cols.shape[1]

    @pl.loop(0, a.shape[0], unroll=4)
    def _(i):
        left = jnp.concatenate([a[i, 0], a[i, 1]], axis=1)
        right = []
        for o in range(kept):
            j = cols[i, o]
            low, high = kb[j, 0], kb[j, 1]
            column = []
            for k in range(2):
                want = ka[i, k]
                place = jnp.where(low == want, 2 * j, jnp.where(high == want, 2 * j + 1, at))
                column.append(held[place])
            right.append(jnp.concatenate(column, axis=0))
        made = jnp.dot(left, jnp.concatenate(right, axis=1), preferred_element_type=jnp.float32)
        for o in range(kept):
            value = made[:, o * 128 : (o + 1) * 128]
            if not first:
                value = value + total[i, o]
            out[i, o] = value.astype(out.dtype)


def contribute(total, cols, ka, kb, a, parts, last):
    rows, kept = cols.shape
    size = a.shape[2]
    sizes = tuple(p.shape[0] for p in parts)
    first = total is None
    smem = pl.BlockSpec(memory_space=pltpu.SMEM)
    vmem = pl.BlockSpec(memory_space=pltpu.VMEM)
    whole = pl.BlockSpec(memory_space=pl.ANY)
    blocks = sum(sizes)
    return pl.pallas_call(
        functools.partial(block_kernel, first, last, sizes),
        out_shape=jax.ShapeDtypeStruct((rows, kept, size, size), jnp.bfloat16 if last else jnp.float32),
        in_specs=[smem] * 3 + [vmem] + [whole] * len(parts) + ([] if first else [vmem]),
        out_specs=vmem,
        scratch_shapes=[
            pltpu.VMEM((blocks + 1, size, size), jnp.bfloat16),
            pltpu.SemaphoreType.DMA((len(parts),)),
        ],
        compiler_params=pltpu.CompilerParams(vmem_limit_bytes=24 * 2**20),
        cost_estimate=pl.CostEstimate(
            flops=rows * kept * 4 * size**3, bytes_accessed=10 * 2**20, transcendentals=0
        ),
    )(cols, ka, kb, a, *parts, *(() if first else (total,)))


def local(n_row, n_col, a_blocks, a_cols, b_blocks, b_rows, out_cols):
    cols = out_cols[:, 0]
    ka = [a_cols[:, 0]]
    kb = [b_rows[0]]
    a_now = a_blocks[:, 0]
    blocks = b_blocks.shape[1] * b_blocks.shape[2]
    b_now = b_blocks[0].reshape((blocks,) + b_blocks.shape[3:])
    down = positions(n_row, n_col, lambda row, col: (ahead(row, col, n_col), col))
    near = positions(n_row, n_col, lambda row, col: (row + 1, col))
    side = positions(n_row, n_col, lambda row, col: (row, col + 1))
    parts = [b_now]
    total = None
    for step in range(STEPS):
        total = contribute(total, cols, ka[-1], kb[-1], a_now, parts, step + 1 == STEPS)
        if step + 1 < STEPS:
            parts = [lax.ppermute(parts[0], AXES, down)]
            a_now = lax.ppermute(a_now, AXES, side)
            ka.append(lax.ppermute(ka[-1], AXES, side))
            kb.append(lax.ppermute(kb[-1], AXES, near))
    return total[:, None]


def solution(mesh):
    n_row, n_col = mesh.shape["row"], mesh.shape["col"]
    return jax.shard_map(
        functools.partial(local, n_row, n_col),
        mesh=mesh,
        in_specs=(
            P("row", "col", None, None, None),
            P("row", "col", None),
            P("row", "col", None, None, None),
            P("row", "col", None),
            P("row", "col", None),
        ),
        out_specs=P("row", "col", None, None, None),
        check_vma=False,
    )
```

time: 382 us -> 238 us (0.62)
  the two profiles are of different devices: /device:TPU:64 before, /device:TPU:73 now
where the time goes in v1:
time: 238 us; the launch traced here: 237 us
  starting transfers between devices  137 us (58%)
  waiting for transfers between devices  79.8 us (34%)
  Pallas kernels  12.5 us (5%)
  local copies, waits for them, and re-layouts  7.38 us (3%)
    ppermute x3, starting transfers between devices, local(): kb.append(lax.ppermute(kb[-1], AXES, near))  92.5 us
    ppermute x3, waiting for transfers between devices, local(): parts = [lax.ppermute(parts[0], AXES, down)]  64.3 us
    ppermute x3, starting transfers between devices, local(): parts = [lax.ppermute(parts[0], AXES, down)]  15.8 us
    ppermute x3, starting transfers between devices, local(): ka.append(lax.ppermute(ka[-1], AXES, side))  15.2 us
    ppermute x3, waiting for transfers between devices, local(): a_now = lax.ppermute(a_now, AXES, side)  14.1 us
    ppermute x3, starting transfers between devices, local(): a_now = lax.ppermute(a_now, AXES, side)  13.8 us
    pallas_call x4, Pallas kernels, contribute(): pl.pallas_call(functools.partial(block_kernel, first, last, sizes), out_s...  12.5 us
    unnamed x12, local copies, waits for them, and re-layouts  5.1 us
  transfers between devices with their start and end apart: 12, of which 4 were waited for; matrix products, arithmetic and copies ran while one was open for 1% of the time, Pallas kernels for 3%

profile of v1, /device:TPU:73, one launch (start us, length us, event | category | flops | bytes accessed | tf_op | source)
XLA Modules:
  0.0 237.2 jit_solution(6677225137553438524)
XLA Ops:
  0.0 2.1 collective-permute-start.9
  2.1 46.5 %collective-permute-done.9.refs_4_ = bf16[64,128,128]{2,1,0:T(8,128)(2,1)S(1)} collective-permute-done((bf16[64,128,128]{2,1,0:T(8,128)(2,1)}, bf16[64,128,128]{2,1,0:T(8,128)(2,1)S(1)}, u32[]{:S(2)}, u32[]{:S(2)}) %collective-permute-start.9) | collective-permute-done | bytes 2097184 | tf_op jit(solution)/shard_map/ppermute | solution.py:109
  48.6 6.8 %collective-permute-start.10 = (bf16[64,128,128]{2,1,0:T(8,128)(2,1)S(1)}, bf16[64,128,128]{2,1,0:T(8,128)(2,1)S(1)}, u32[]{:S(2)}, u32[]{:S(2)}) collective-permute-start(bf16[64,128,128]{2,1,0:T(8,128)(2,1)S(1)} %collective-permute-done.9.refs_4_), channel_id=1, source_target_pairs={{16,0},{17,1},{18,2},{19,3},{20,4},{21,5},{22,6},{23,7},{24,8},{25... | collective-permute-start | bytes 6291464 | tf_op jit(solution)/shard_map/ppermute | solution.py:109
  55.4 1.3 copy-done.1
  56.7 3.7 %collective-permute-start.6 = (bf16[16,2,128,128]{3,2,1,0:T(8,128)(2,1)}, bf16[16,2,128,128]{3,2,1,0:T(8,128)(2,1)S(1)}, u32[]{:S(2)}, u32[]{:S(2)}) collective-permute-start(bf16[16,2,128,128]{3,2,1,0:T(8,128)(2,1)} %bitcast.10), channel_id=1, source_target_pairs={{1,0},{2,1},{3,2},{4,3},{5,4},{6,5},{7,6},{8,7},{9,8},{10,9},{11,1... | collective-permute-start | bytes 3145736 | tf_op jit(solution)/shard_map/ppermute | solution.py:110
  60.4 14.1 %collective-permute-done.6.refs_3_ = bf16[16,2,128,128]{3,2,1,0:T(8,128)(2,1)S(1)} collective-permute-done((bf16[16,2,128,128]{3,2,1,0:T(8,128)(2,1)}, bf16[16,2,128,128]{3,2,1,0:T(8,128)(2,1)S(1)}, u32[]{:S(2)}, u32[]{:S(2)}) %collective-permute-start.6) | collective-permute-done | bytes 1048608 | tf_op jit(solution)/shard_map/ppermute | solution.py:110
  74.5 5.4 %collective-permute-start.7 = (bf16[16,2,128,128]{3,2,1,0:T(8,128)(2,1)S(1)}, bf16[16,2,128,128]{3,2,1,0:T(8,128)(2,1)S(1)}, u32[]{:S(2)}, u32[]{:S(2)}) collective-permute-start(bf16[16,2,128,128]{3,2,1,0:T(8,128)(2,1)S(1)} %collective-permute-done.6.refs_3_), channel_id=1, source_target_pairs={{1,0},{2,1},{3,2},{4,3},{5,4},{6,5},{7,6},{8,7},{9,8},{10,9},{11,1... | collective-permute-start | bytes 3145736 | tf_op jit(solution)/shard_map/ppermute | solution.py:110
  80.0 1.0 copy-done.3
  80.9 17.8 %collective-permute-done.10.refs_4_ = bf16[64,128,128]{2,1,0:T(8,128)(2,1)S(1)} collective-permute-done((bf16[64,128,128]{2,1,0:T(8,128)(2,1)S(1)}, bf16[64,128,128]{2,1,0:T(8,128)(2,1)S(1)}, u32[]{:S(2)}, u32[]{:S(2)}) %collective-permute-start.10) | collective-permute-done | bytes 2097184 | tf_op jit(solution)/shard_map/ppermute | solution.py:109
  98.7 7.0 %collective-permute-start.11 = (bf16[64,128,128]{2,1,0:T(8,128)(2,1)S(1)}, bf16[64,128,128]{2,1,0:T(8,128)(2,1)}, u32[]{:S(2)}, u32[]{:S(2)}) collective-permute-start(bf16[64,128,128]{2,1,0:T(8,128)(2,1)S(1)} %collective-permute-done.10.refs_4_), channel_id=1, source_target_pairs={{16,0},{17,1},{18,2},{19,3},{20,4},{21,5},{22,6},{23,7},{24,8},{25... | collective-permute-start | bytes 6291464 | tf_op jit(solution)/shard_map/ppermute | solution.py:109
  105.8 4.7 %collective-permute-start.8 = (bf16[16,2,128,128]{3,2,1,0:T(8,128)(2,1)S(1)}, bf16[16,2,128,128]{3,2,1,0:T(8,128)(2,1)}, u32[]{:S(2)}, u32[]{:S(2)}) collective-permute-start(bf16[16,2,128,128]{3,2,1,0:T(8,128)(2,1)S(1)} %collective-permute-done.7.refs_3_), channel_id=1, source_target_pairs={{1,0},{2,1},{3,2},{4,3},{5,4},{6,5},{7,6},{8,7},{9,8},{10,9},{11,1... | collective-permute-start | bytes 3145736 | tf_op jit(solution)/shard_map/ppermute | solution.py:110
  111.2 25.2 %collective-permute-start.3 = (s32[32,2]{1,0:T(8,128)S(1)}, s32[32,2]{1,0:T(8,128)S(1)}, u32[]{:S(2)}, u32[]{:S(2)}) collective-permute-start(s32[32,2]{1,0:T(8,128)S(1)} %copy.7.refs_2_), channel_id=1, source_target_pairs={{16,0},{17,1},{18,2},{19,3},{20,4},{21,5},{22,6},{23,7},{24,8},{25... | collective-permute-start | bytes 776 | tf_op jit(solution)/shard_map/ppermute | solution.py:112
  137.2 6.8 %collective-permute-start = (s32[16,2]{1,0:T(8,128)S(1)}, s32[16,2]{1,0:T(8,128)S(1)}, u32[]{:S(2)}, u32[]{:S(2)}) collective-permute-start(s32[16,2]{1,0:T(8,128)S(1)} %copy.6.refs_1_), channel_id=1, source_target_pairs={{1,0},{2,1},{3,2},{4,3},{5,4},{6,5},{7,6},{8,7},{9,8},{10,9},{11,1... | collective-permute-start | bytes 392 | tf_op jit(solution)/shard_map/ppermute | solution.py:111
  144.7 2.4 %collective-permute-start.1 = (s32[16,2]{1,0:T(8,128)S(1)}, s32[16,2]{1,0:T(8,128)S(1)}, u32[]{:S(2)}, u32[]{:S(2)}) collective-permute-start(s32[16,2]{1,0:T(8,128)S(1)} %collective-permute-done.refs_1_), channel_id=1, source_target_pairs={{1,0},{2,1},{3,2},{4,3},{5,4},{6,5},{7,6},{8,7},{9,8},{10,9},{11,1... | collective-permute-start | bytes 392 | tf_op jit(solution)/shard_map/ppermute | solution.py:111
  147.2 1.3 collective-permute-done.3.refs_2_
  148.5 58.9 %collective-permute-start.4 = (s32[32,2]{1,0:T(8,128)S(1)}, s32[32,2]{1,0:T(8,128)S(1)}, u32[]{:S(2)}, u32[]{:S(2)}) collective-permute-start(s32[32,2]{1,0:T(8,128)S(1)} %collective-permute-done.3.refs_2_), channel_id=1, source_target_pairs={{16,0},{17,1},{18,2},{19,3},{20,4},{21,5},{22,6},{23,7},{24,8},{25... | collective-permute-start | bytes 776 | tf_op jit(solution)/shard_map/ppermute | solution.py:112
  207.5 1.6 copy-done
  209.1 1.2 copy-done.5
  210.3 2.4 %shard_map.55.refs_5_ = f32[16,3,128,128]{3,2,1,0:T(8,128)S(1)} custom-call(s32[16,3]{1,0:T(8,128)S(1)} %bitcast.12, s32[16,2]{1,0:T(8,128)S(1)} %copy.6.refs_1_, s32[32,2]{1,0:T(8,128)S(1)} %copy.7.refs_2_, bf16[16,2,128,128]{3,2,1,0:T(8,128)(2,1)S(1)} %bitcast.11, bf16[64,128,128]{2,1,0:T(8,128)(2,1)S(1)} %bitcast.9), custom_call_target="tpu_custom_call" | custom-call | flops 402653184 | bytes 10485760 | tf_op jit(solution)/shard_map/pallas_call | solution.py:78
  212.7 6.0 %collective-permute-start.2 = (s32[16,2]{1,0:T(8,128)S(1)}, s32[16,2]{1,0:T(8,128)S(1)}, u32[]{:S(2)}, u32[]{:S(2)}) collective-permute-start(s32[16,2]{1,0:T(8,128)S(1)} %collective-permute-done.1.refs_1_), channel_id=1, source_target_pairs={{1,0},{2,1},{3,2},{4,3},{5,4},{6,5},{7,6},{8,7},{9,8},{10,9},{11,1... | collective-permute-start | bytes 392 | tf_op jit(solution)/shard_map/ppermute | solution.py:111
  218.8 8.3 %collective-permute-start.5 = (s32[32,2]{1,0:T(8,128)S(1)}, s32[32,2]{1,0:T(8,128)S(1)}, u32[]{:S(2)}, u32[]{:S(2)}) collective-permute-start(s32[32,2]{1,0:T(8,128)S(1)} %collective-permute-done.4.refs_2_), channel_id=1, source_target_pairs={{16,0},{17,1},{18,2},{19,3},{20,4},{21,5},{22,6},{23,7},{24,8},{25... | collective-permute-start | bytes 776 | tf_op jit(solution)/shard_map/ppermute | solution.py:112
  227.1 2.4 %shard_map.56.refs_5_ = f32[16,3,128,128]{3,2,1,0:T(8,128)S(1)} custom-call(s32[16,3]{1,0:T(8,128)S(1)} %bitcast.13, s32[16,2]{1,0:T(8,128)S(1)} %collective-permute-done.refs_1_, s32[32,2]{1,0:T(8,128)S(1)} %collective-permute-done.3.refs_2_, bf16[16,2,128,128]{3,2,1,0:T(8,128)(2,1)S(1)} %copy-done.4, bf16[64,128,128]{2,1,0:T(8,128)(2,1)S(1)} %copy-done.2, ...), custom_call_target="tpu_custom_call" | custom-call | flops 402653184 | bytes 10485760 | tf_op jit(solution)/shard_map/pallas_call | solution.py:78
  229.6 2.4 %shard_map.57.refs_5_ = f32[16,3,128,128]{3,2,1,0:T(8,128)S(1)} custom-call(s32[16,3]{1,0:T(8,128)S(1)} %bitcast.14, s32[16,2]{1,0:T(8,128)S(1)} %collective-permute-done.1.refs_1_, s32[32,2]{1,0:T(8,128)S(1)} %collective-permute-done.4.refs_2_, bf16[16,2,128,128]{3,2,1,0:T(8,128)(2,1)S(1)} %collective-permute-done.7.refs_3_, ...), custom_call_target="tpu_custom_call" | custom-call | flops 402653184 | bytes 10485760 | tf_op jit(solution)/shard_map/pallas_call | solution.py:78
  232.0 5.2 %shard_map.58 = bf16[16,3,128,128]{3,2,1,0:T(8,128)(2,1)} custom-call(s32[16,3]{1,0:T(8,128)S(1)} %bitcast.15, s32[16,2]{1,0:T(8,128)S(1)} %collective-permute-done.2.refs_1_, s32[32,2]{1,0:T(8,128)S(1)} %collective-permute-done.5.refs_2_, bf16[16,2,128,128]{3,2,1,0:T(8,128)(2,1)} %collective-permute-done.8.refs_3_, ...), custom_call_target="tpu_custom_call" | custom-call | flops 402653184 | bytes 10485760 | tf_op jit(solution)/shard_map/pallas_call | solution.py:78
  (19 shorter events, 2.4 us)
Async XLA Ops:
  0.0 48.6 %collective-permute-start.9 = (bf16[64,128,128]{2,1,0:T(8,128)(2,1)}, bf16[64,128,128]{2,1,0:T(8,128)(2,1)S(1)}, u32[]{:S(2)}, u32[]{:S(2)}) collective-permute-start(bf16[64,128,128]{2,1,0:T(8,128)(2,1)} %bitcast.8), channel_id=1, source_target_pairs={{16,0},{17,1},{18,2},{19,3},{20,4},{21,5},{22,6},{23,7},{24,8},{25... | collective-permute-start | bytes 6291464 | tf_op jit(solution)/shard_map/ppermute | solution.py:109
  48.6 50.1 %collective-permute-start.10 = (bf16[64,128,128]{2,1,0:T(8,128)(2,1)S(1)}, bf16[64,128,128]{2,1,0:T(8,128)(2,1)S(1)}, u32[]{:S(2)}, u32[]{:S(2)}) collective-permute-start(bf16[64,128,128]{2,1,0:T(8,128)(2,1)S(1)} %collective-permute-done.9.refs_4_), channel_id=1, source_target_pairs={{16,0},{17,1},{18,2},{19,3},{20,4},{21,5},{22,6},{23,7},{24,8},{25... | collective-permute-start | bytes 6291464 | tf_op jit(solution)/shard_map/ppermute | solution.py:109
  55.4 1.3 copy-start.1
  56.7 17.8 %collective-permute-start.6 = (bf16[16,2,128,128]{3,2,1,0:T(8,128)(2,1)}, bf16[16,2,128,128]{3,2,1,0:T(8,128)(2,1)S(1)}, u32[]{:S(2)}, u32[]{:S(2)}) collective-permute-start(bf16[16,2,128,128]{3,2,1,0:T(8,128)(2,1)} %bitcast.10), channel_id=1, source_target_pairs={{1,0},{2,1},{3,2},{4,3},{5,4},{6,5},{7,6},{8,7},{9,8},{10,9},{11,1... | collective-permute-start | bytes 3145736 | tf_op jit(solution)/shard_map/ppermute | solution.py:110
  74.5 31.2 %collective-permute-start.7 = (bf16[16,2,128,128]{3,2,1,0:T(8,128)(2,1)S(1)}, bf16[16,2,128,128]{3,2,1,0:T(8,128)(2,1)S(1)}, u32[]{:S(2)}, u32[]{:S(2)}) collective-permute-start(bf16[16,2,128,128]{3,2,1,0:T(8,128)(2,1)S(1)} %collective-permute-done.6.refs_3_), channel_id=1, source_target_pairs={{1,0},{2,1},{3,2},{4,3},{5,4},{6,5},{7,6},{8,7},{9,8},{10,9},{11,1... | collective-permute-start | bytes 3145736 | tf_op jit(solution)/shard_map/ppermute | solution.py:110
  79.9 1.0 copy-start.3
  98.7 133.3 %collective-permute-start.11 = (bf16[64,128,128]{2,1,0:T(8,128)(2,1)S(1)}, bf16[64,128,128]{2,1,0:T(8,128)(2,1)}, u32[]{:S(2)}, u32[]{:S(2)}) collective-permute-start(bf16[64,128,128]{2,1,0:T(8,128)(2,1)S(1)} %collective-permute-done.10.refs_4_), channel_id=1, source_target_pairs={{16,0},{17,1},{18,2},{19,3},{20,4},{21,5},{22,6},{23,7},{24,8},{25... | collective-permute-start | bytes 6291464 | tf_op jit(solution)/shard_map/ppermute | solution.py:109
  105.8 126.3 %collective-permute-start.8 = (bf16[16,2,128,128]{3,2,1,0:T(8,128)(2,1)S(1)}, bf16[16,2,128,128]{3,2,1,0:T(8,128)(2,1)}, u32[]{:S(2)}, u32[]{:S(2)}) collective-permute-start(bf16[16,2,128,128]{3,2,1,0:T(8,128)(2,1)S(1)} %collective-permute-done.7.refs_3_), channel_id=1, source_target_pairs={{1,0},{2,1},{3,2},{4,3},{5,4},{6,5},{7,6},{8,7},{9,8},{10,9},{11,1... | collective-permute-start | bytes 3145736 | tf_op jit(solution)/shard_map/ppermute | solution.py:110
  111.2 37.3 %collective-permute-start.3 = (s32[32,2]{1,0:T(8,128)S(1)}, s32[32,2]{1,0:T(8,128)S(1)}, u32[]{:S(2)}, u32[]{:S(2)}) collective-permute-start(s32[32,2]{1,0:T(8,128)S(1)} %copy.7.refs_2_), channel_id=1, source_target_pairs={{16,0},{17,1},{18,2},{19,3},{20,4},{21,5},{22,6},{23,7},{24,8},{25... | collective-permute-start | bytes 776 | tf_op jit(solution)/shard_map/ppermute | solution.py:112
  137.2 7.6 %collective-permute-start = (s32[16,2]{1,0:T(8,128)S(1)}, s32[16,2]{1,0:T(8,128)S(1)}, u32[]{:S(2)}, u32[]{:S(2)}) collective-permute-start(s32[16,2]{1,0:T(8,128)S(1)} %copy.6.refs_1_), channel_id=1, source_target_pairs={{1,0},{2,1},{3,2},{4,3},{5,4},{6,5},{7,6},{8,7},{9,8},{10,9},{11,1... | collective-permute-start | bytes 392 | tf_op jit(solution)/shard_map/ppermute | solution.py:111
  144.7 68.0 %collective-permute-start.1 = (s32[16,2]{1,0:T(8,128)S(1)}, s32[16,2]{1,0:T(8,128)S(1)}, u32[]{:S(2)}, u32[]{:S(2)}) collective-permute-start(s32[16,2]{1,0:T(8,128)S(1)} %collective-permute-done.refs_1_), channel_id=1, source_target_pairs={{1,0},{2,1},{3,2},{4,3},{5,4},{6,5},{7,6},{8,7},{9,8},{10,9},{11,1... | collective-permute-start | bytes 392 | tf_op jit(solution)/shard_map/ppermute | solution.py:111
  148.5 70.2 %collective-permute-start.4 = (s32[32,2]{1,0:T(8,128)S(1)}, s32[32,2]{1,0:T(8,128)S(1)}, u32[]{:S(2)}, u32[]{:S(2)}) collective-permute-start(s32[32,2]{1,0:T(8,128)S(1)} %collective-permute-done.3.refs_2_), channel_id=1, source_target_pairs={{16,0},{17,1},{18,2},{19,3},{20,4},{21,5},{22,6},{23,7},{24,8},{25... | collective-permute-start | bytes 776 | tf_op jit(solution)/shard_map/ppermute | solution.py:112
  207.5 1.6 copy-start
  209.1 1.2 copy-start.5
  210.3 16.8 %copy-start.2 = (bf16[64,128,128]{2,1,0:T(8,128)(2,1)S(1)}, bf16[64,128,128]{2,1,0:T(8,128)(2,1)}, u32[]{:S(2)}) copy-start(bf16[64,128,128]{2,1,0:T(8,128)(2,1)} %copy-done.1) | copy-start | bytes 6291460
  210.3 16.8 %copy-start.4 = (bf16[16,2,128,128]{3,2,1,0:T(8,128)(2,1)S(1)}, bf16[16,2,128,128]{3,2,1,0:T(8,128)(2,1)}, u32[]{:S(2)}) copy-start(bf16[16,2,128,128]{3,2,1,0:T(8,128)(2,1)} %copy-done.3) | copy-start | bytes 3145732
  212.7 19.3 %collective-permute-start.2 = (s32[16,2]{1,0:T(8,128)S(1)}, s32[16,2]{1,0:T(8,128)S(1)}, u32[]{:S(2)}, u32[]{:S(2)}) collective-permute-start(s32[16,2]{1,0:T(8,128)S(1)} %collective-permute-done.1.refs_1_), channel_id=1, source_target_pairs={{1,0},{2,1},{3,2},{4,3},{5,4},{6,5},{7,6},{8,7},{9,8},{10,9},{11,1... | collective-permute-start | bytes 392 | tf_op jit(solution)/shard_map/ppermute | solution.py:111
  218.8 13.3 %collective-permute-start.5 = (s32[32,2]{1,0:T(8,128)S(1)}, s32[32,2]{1,0:T(8,128)S(1)}, u32[]{:S(2)}, u32[]{:S(2)}) collective-permute-start(s32[32,2]{1,0:T(8,128)S(1)} %collective-permute-done.4.refs_2_), channel_id=1, source_target_pairs={{16,0},{17,1},{18,2},{19,3},{20,4},{21,5},{22,6},{23,7},{24,8},{25... | collective-permute-start | bytes 776 | tf_op jit(solution)/shard_map/ppermute | solution.py:112

commit v2 on v1

v2 whole, which is shorter than its diff:
```python
import functools

import jax
import jax.numpy as jnp
from jax import lax
from jax.experimental import pallas as pl
from jax.experimental.pallas import tpu as pltpu
from jax.sharding import PartitionSpec as P

STEPS = 4
HALF = 16
RING = 8
AXES = ("row", "col")
CUT = 44


def block_kernel(first, sizes, *refs):
    cols, ka, kb, a = refs[:4]
    parts = refs[4 : 4 + len(sizes)]
    rest = refs[4 + len(sizes) :]
    total = None if first else rest[0]
    out, held, sems = rest[-3:]
    copies = []
    at = 0
    for n, (part, size) in enumerate(zip(parts, sizes)):
        copies.append(pltpu.make_async_copy(part.at[pl.ds(0, size)], held.at[pl.ds(at, size)], sems.at[n]))
        at += size
    for copy in copies:
        copy.start()
    held[at] = jnp.zeros(held.shape[1:], held.dtype)
    for copy in copies:
        copy.wait()
    rows, kept = cols.shape

    @pl.loop(0, rows, unroll=4)
    def _(i):
        left = jnp.concatenate([a[2 * i], a[2 * i + 1]], axis=1)
        right = []
        for o in range(kept):
            j = cols[i, o]
            low, high = kb[2 * j], kb[2 * j + 1]
            column = []
            for k in range(2):
                want = ka[2 * i + k]
                place = jnp.where(low == want, 2 * j, jnp.where(high == want, 2 * j + 1, at))
                column.append(held[place])
            right.append(jnp.concatenate(column, axis=0))
        made = jnp.dot(left, jnp.concatenate(right, axis=1), preferred_element_type=jnp.float32)
        for o in range(kept):
            value = made[:, o * 128 : (o + 1) * 128]
            if not first:
                value = value + total[i, o]
            out[i, o] = value.astype(out.dtype)


def contribute(total, cols, ka, kb, a, parts, sizes, last):
    rows, kept = cols.shape
    size = a.shape[2]
    first = total is None
    smem = pl.BlockSpec(memory_space=pltpu.SMEM)
    vmem = pl.BlockSpec(memory_space=pltpu.VMEM)
    whole = pl.BlockSpec(memory_space=pl.ANY)
    return pl.pallas_call(
        functools.partial(block_kernel, first, sizes),
        out_shape=jax.ShapeDtypeStruct((rows, kept, size, size), jnp.bfloat16 if last else jnp.float32),
        in_specs=[smem] * 3 + [vmem] + [whole] * len(parts) + ([] if first else [vmem]),
        out_specs=vmem,
        scratch_shapes=[
            pltpu.VMEM((sum(sizes) + 1, size, size), jnp.bfloat16),
            pltpu.SemaphoreType.DMA((len(parts),)),
        ],
        compiler_params=pltpu.CompilerParams(vmem_limit_bytes=24 * 2**20),
        cost_estimate=pl.CostEstimate(
            flops=rows * kept * 4 * size**3, bytes_accessed=10 * 2**20, transcendentals=0
        ),
    )(cols, ka, kb, a, *parts, *(() if first else (total,)))


def with_indices(blocks, indices):
    flat = indices.reshape(-1).astype(blocks.dtype)
    extra = jnp.zeros((1,) + blocks.shape[1:], blocks.dtype).at[0, 0, : flat.shape[0]].set(flat)
    return jnp.concatenate([blocks, extra], axis=0)


def indices_of(blocks, count):
    return blocks[-1, 0, :count].astype(jnp.int32)


class Paths:
    def __init__(self, n_row, n_col):
        self.n_row, self.n_col = n_row, n_col
        self.down = self.pairs(lambda z, y, t: (z + t * (y == RING - 1), y + 1))
        self.up_two = self.pairs(lambda z, y, t: (z, y - 2))
        self.up_turn = self.pairs(lambda z, y, t: (z + t * (4 <= y < RING - 1), y - 2))
        self.up_in = self.pairs(lambda z, y, t: (z, y - 1))
        self.up = self.pairs(lambda z, y, t: (z - t * (y == 0), y - 1))
        self.side = [
            (row * n_col + (col + 1) % n_col, row * n_col + col) for row in range(n_row) for col in range(n_col)
        ]

    def pairs(self, source):
        made = []
        for row in range(self.n_row):
            for col in range(self.n_col):
                z, y = source(*divmod(row, RING), 1 if col < self.n_col // 2 else -1)
                from_row = z % (self.n_row // RING) * RING + y % RING
                made.append((from_row * self.n_col + col, row * self.n_col + col))
        return made


def local(paths, a_blocks, a_cols, b_blocks, b_rows, out_cols):
    cols = out_cols[:, 0]
    ka, kb = a_cols[:, 0].reshape(-1), b_rows[0].reshape(-1)
    block = b_blocks.shape[3:]
    own = b_blocks[0].reshape((-1,) + block)
    count = own.shape[0]
    send = lambda value, pairs: lax.ppermute(value, AXES, pairs)
    sizes = (CUT, count - CUT)

    most = [with_indices(own[:CUT], kb)]
    rest = own[CUT:]
    left = [with_indices(a_blocks[:, 0].reshape((-1,) + block), ka)]
    for step in range(1, STEPS):
        most.append(send(most[-1], paths.down))
        left.append(send(left[-1], paths.side))
    far = send(send(rest, paths.up_two), paths.up_turn)
    third = send(far, paths.up_in)
    second = send(third, paths.up)
    first = send(second, paths.up)
    around = [rest, first, second, third]

    total = None
    for step in range(STEPS):
        total = contribute(
            total,
            cols,
            indices_of(left[step], ka.shape[0]) if step else ka,
            indices_of(most[step], kb.shape[0]) if step else kb,
            left[step],
            [most[step], around[step]],
            sizes,
            step + 1 == STEPS,
        )
    return total[:, None]


def solution(mesh):
    paths = Paths(mesh.shape["row"], mesh.shape["col"])
    return jax.shard_map(
        functools.partial(local, paths),
        mesh=mesh,
        in_specs=(
            P("row", "col", None, None, None),
            P("row", "col", None),
            P("row", "col", None, None, None),
            P("row", "col", None),
            P("row", "col", None),
        ),
        out_specs=P("row", "col", None, None, None),
        check_vma=False,
    )
```

time: 238 us -> 179 us (0.75)
  the two profiles are of different devices: /device:TPU:73 before, /device:TPU:1 now
where the time goes in v2:
time: 179 us
  waiting for transfers between devices  90.5 us (51%)
  starting transfers between devices  65 us (36%)
  Pallas kernels  14.8 us (8%)
  other arithmetic  5.03 us (3%)
  local copies, waits for them, and re-layouts  3.04 us (2%)
    ppermute x11, waiting for transfers between devices, local(): send = lambda value, pairs: lax.ppermute(value, AXES, pairs)  90.5 us
    ppermute x11, starting transfers between devices, local(): send = lambda value, pairs: lax.ppermute(value, AXES, pairs)  65 us
    pallas_call x4, Pallas kernels, contribute(): pl.pallas_call(functools.partial(block_kernel, first, sizes), out_shape=j...  14.8 us
  transfers between devices with their start and end apart: 11, of which 6 were waited for; matrix products, arithmetic and copies ran while one was open for 3% of the time, Pallas kernels for 5%

profile of v2, /device:TPU:1, one launch (start us, length us, event | category | flops | bytes accessed | tf_op | source)
XLA Modules:
  0.0 178.6 jit_solution(12707434769671672349)
XLA Ops:
  0.0 0.8 copy-done.4
  1.6 14.4 %collective-permute-start.3 = (bf16[45,128,128]{2,1,0:T(8,128)(2,1)S(1)}, bf16[45,128,128]{2,1,0:T(8,128)(2,1)}, u32[]{:S(2)}, u32[]{:S(2)}) collective-permute-start(bf16[45,128,128]{2,1,0:T(8,128)(2,1)S(1)} %fusion.2.refs_4_), channel_id=1, source_target_pairs={{16,0},{17,1},{18,2},{19,3},{20,4},{21,5},{22,6},{23,7},{24,8},{25... | collective-permute-start | bytes 4423688 | tf_op jit(solution)/shard_map/ppermute | solution.py:117
  16.2 1.5 fusion.3.refs_3_
  17.7 2.9 %collective-permute-start = (bf16[33,128,128]{2,1,0:T(8,128)(2,1)S(1)}, bf16[33,128,128]{2,1,0:T(8,128)(2,1)S(1)}, u32[]{:S(2)}, u32[]{:S(2)}) collective-permute-start(bf16[33,128,128]{2,1,0:T(8,128)(2,1)S(1)} %fusion.3.refs_3_), channel_id=1, source_target_pairs={{1,0},{2,1},{3,2},{4,3},{5,4},{6,5},{7,6},{8,7},{9,8},{10,9},{11,1... | collective-permute-start | bytes 3244040 | tf_op jit(solution)/shard_map/ppermute | solution.py:117
  20.6 1.9 %collective-permute-start.6 = (bf16[20,128,128]{2,1,0:T(8,128)(2,1)S(1)}, bf16[20,128,128]{2,1,0:T(8,128)(2,1)S(1)}, u32[]{:S(2)}, u32[]{:S(2)}) collective-permute-start(bf16[20,128,128]{2,1,0:T(8,128)(2,1)S(1)} %bitcast.41), channel_id=1, source_target_pairs={{96,0},{97,1},{98,2},{99,3},{100,4},{101,5},{102,6},{103,7},{104,8... | collective-permute-start | bytes 1966088 | tf_op jit(solution)/shard_map/ppermute | solution.py:117
  22.5 24.4 %collective-permute-done.3.refs_4_ = bf16[45,128,128]{2,1,0:T(8,128)(2,1)} collective-permute-done((bf16[45,128,128]{2,1,0:T(8,128)(2,1)S(1)}, bf16[45,128,128]{2,1,0:T(8,128)(2,1)}, u32[]{:S(2)}, u32[]{:S(2)}) %collective-permute-start.3) | collective-permute-done | bytes 1474592 | tf_op jit(solution)/shard_map/ppermute | solution.py:117
  46.9 8.4 %collective-permute-start.4 = (bf16[45,128,128]{2,1,0:T(8,128)(2,1)}, bf16[45,128,128]{2,1,0:T(8,128)(2,1)}, u32[]{:S(2)}, u32[]{:S(2)}) collective-permute-start(bf16[45,128,128]{2,1,0:T(8,128)(2,1)} %collective-permute-done.3.refs_4_), channel_id=1, source_target_pairs={{16,0},{17,1},{18,2},{19,3},{20,4},{21,5},{22,6},{23,7},{24,8},{25... | collective-permute-start | bytes 4423688 | tf_op jit(solution)/shard_map/ppermute | solution.py:117
  55.3 1.9 %collective-permute-start.7 = (bf16[20,128,128]{2,1,0:T(8,128)(2,1)S(1)}, bf16[20,128,128]{2,1,0:T(8,128)(2,1)S(1)}, u32[]{:S(2)}, u32[]{:S(2)}) collective-permute-start(bf16[20,128,128]{2,1,0:T(8,128)(2,1)S(1)} %collective-permute-done.6), channel_id=1, source_target_pairs={{96,0},{97,1},{98,2},{99,3},{100,4},{101,5},{102,6},{103,7},{104,8... | collective-permute-start | bytes 1966088 | tf_op jit(solution)/shard_map/ppermute | solution.py:117
  57.3 1.0 copy-done
  58.3 3.8 %collective-permute-start.1 = (bf16[33,128,128]{2,1,0:T(8,128)(2,1)S(1)}, bf16[33,128,128]{2,1,0:T(8,128)(2,1)}, u32[]{:S(2)}, u32[]{:S(2)}) collective-permute-start(bf16[33,128,128]{2,1,0:T(8,128)(2,1)S(1)} %collective-permute-done.refs_3_), channel_id=1, source_target_pairs={{1,0},{2,1},{3,2},{4,3},{5,4},{6,5},{7,6},{8,7},{9,8},{10,9},{11,1... | collective-permute-start | bytes 3244040 | tf_op jit(solution)/shard_map/ppermute | solution.py:117
  62.1 18.3 %collective-permute-done.7 = bf16[20,128,128]{2,1,0:T(8,128)(2,1)S(1)} collective-permute-done((bf16[20,128,128]{2,1,0:T(8,128)(2,1)S(1)}, bf16[20,128,128]{2,1,0:T(8,128)(2,1)S(1)}, u32[]{:S(2)}, u32[]{:S(2)}) %collective-permute-start.7) | collective-permute-done | bytes 655392 | tf_op jit(solution)/shard_map/ppermute | solution.py:117
  80.4 4.2 %collective-permute-start.8 = (bf16[20,128,128]{2,1,0:T(8,128)(2,1)S(1)}, bf16[20,128,128]{2,1,0:T(8,128)(2,1)}, u32[]{:S(2)}, u32[]{:S(2)}) collective-permute-start(bf16[20,128,128]{2,1,0:T(8,128)(2,1)S(1)} %collective-permute-done.7), channel_id=1, source_target_pairs={{112,0},{113,1},{114,2},{115,3},{116,4},{117,5},{118,6},{119,7},{1... | collective-permute-start | bytes 1966088 | tf_op jit(solution)/shard_map/ppermute | solution.py:117
  84.7 0.9 collective-permute-done.4.refs_4_
  85.5 17.0 %collective-permute-start.5 = (bf16[45,128,128]{2,1,0:T(8,128)(2,1)}, bf16[45,128,128]{2,1,0:T(8,128)(2,1)}, u32[]{:S(2)}, u32[]{:S(2)}) collective-permute-start(bf16[45,128,128]{2,1,0:T(8,128)(2,1)} %collective-permute-done.4.refs_4_), channel_id=1, source_target_pairs={{16,0},{17,1},{18,2},{19,3},{20,4},{21,5},{22,6},{23,7},{24,8},{25... | collective-permute-start | bytes 4423688 | tf_op jit(solution)/shard_map/ppermute | solution.py:117
  102.6 4.2 %collective-permute-done.8.refs_5_ = bf16[20,128,128]{2,1,0:T(8,128)(2,1)} collective-permute-done((bf16[20,128,128]{2,1,0:T(8,128)(2,1)S(1)}, bf16[20,128,128]{2,1,0:T(8,128)(2,1)}, u32[]{:S(2)}, u32[]{:S(2)}) %collective-permute-start.8) | collective-permute-done | bytes 655392 | tf_op jit(solution)/shard_map/ppermute | solution.py:117
  106.8 1.9 %collective-permute-start.9 = (bf16[20,128,128]{2,1,0:T(8,128)(2,1)}, bf16[20,128,128]{2,1,0:T(8,128)(2,1)}, u32[]{:S(2)}, u32[]{:S(2)}) collective-permute-start(bf16[20,128,128]{2,1,0:T(8,128)(2,1)} %collective-permute-done.8.refs_5_), channel_id=1, source_target_pairs={{496,0},{497,1},{498,2},{499,3},{500,4},{501,5},{502,6},{503,7},{2... | collective-permute-start | bytes 1966088 | tf_op jit(solution)/shard_map/ppermute | solution.py:117
  108.7 6.6 %collective-permute-start.2 = (bf16[33,128,128]{2,1,0:T(8,128)(2,1)}, bf16[33,128,128]{2,1,0:T(8,128)(2,1)}, u32[]{:S(2)}, u32[]{:S(2)}) collective-permute-start(bf16[33,128,128]{2,1,0:T(8,128)(2,1)} %collective-permute-done.1.refs_3_), channel_id=1, source_target_pairs={{1,0},{2,1},{3,2},{4,3},{5,4},{6,5},{7,6},{8,7},{9,8},{10,9},{11,1... | collective-permute-start | bytes 3244040 | tf_op jit(solution)/shard_map/ppermute | solution.py:117
  115.7 2.4 %shard_map.55.refs_6_ = f32[16,3,128,128]{3,2,1,0:T(8,128)S(1)} custom-call(s32[16,3]{1,0:T(8,128)S(1)} %bitcast.43, s32[32]{0:T(128)S(1)} %reshape_squeeze.11.refs_1_, s32[64]{0:T(128)S(1)} %reshape_squeeze.12.refs_2_, bf16[33,128,128]{2,1,0:T(8,128)(2,1)S(1)} %fusion.3.refs_3_, bf16[45,128,128]{2,1,0:T(8,128)(2,1)S(1)} %fusion.2.refs_4_, ...), custom_call_target="tpu_custom_call" | custom-call | flops 402653184 | bytes 10485760 | tf_op jit(solution)/shard_map/pallas_call | solution.py:63
  118.8 6.4 %collective-permute-done.9.refs_5_ = bf16[20,128,128]{2,1,0:T(8,128)(2,1)} collective-permute-done((bf16[20,128,128]{2,1,0:T(8,128)(2,1)}, bf16[20,128,128]{2,1,0:T(8,128)(2,1)}, u32[]{:S(2)}, u32[]{:S(2)}) %collective-permute-start.9) | collective-permute-done | bytes 655392 | tf_op jit(solution)/shard_map/ppermute | solution.py:117
  125.3 1.9 %collective-permute-start.10 = (bf16[20,128,128]{2,1,0:T(8,128)(2,1)}, bf16[20,128,128]{2,1,0:T(8,128)(2,1)S(1)}, u32[]{:S(2)}, u32[]{:S(2)}) collective-permute-start(bf16[20,128,128]{2,1,0:T(8,128)(2,1)} %collective-permute-done.9.refs_5_), channel_id=1, source_target_pairs={{496,0},{497,1},{498,2},{499,3},{500,4},{501,5},{502,6},{503,7},{2... | collective-permute-start | bytes 1966088 | tf_op jit(solution)/shard_map/ppermute | solution.py:117
  129.2 36.2 %collective-permute-done.10.refs_5_ = bf16[20,128,128]{2,1,0:T(8,128)(2,1)S(1)} collective-permute-done((bf16[20,128,128]{2,1,0:T(8,128)(2,1)}, bf16[20,128,128]{2,1,0:T(8,128)(2,1)S(1)}, u32[]{:S(2)}, u32[]{:S(2)}) %collective-permute-start.10) | collective-permute-done | bytes 655392 | tf_op jit(solution)/shard_map/ppermute | solution.py:117
  165.5 3.3 %shard_map.56.refs_6_ = f32[16,3,128,128]{3,2,1,0:T(8,128)S(1)} custom-call(s32[16,3]{1,0:T(8,128)S(1)} %bitcast.44, s32[32]{0:T(128)S(1)} %fusion.5.refs_1_, s32[64]{0:T(128)S(1)} %fusion.4.refs_2_, bf16[33,128,128]{2,1,0:T(8,128)(2,1)S(1)} %copy-done.1, bf16[45,128,128]{2,1,0:T(8,128)(2,1)} %collective-permute-done.3.refs_4_, ...), custom_call_target="tpu_custom_call" | custom-call | flops 402653184 | bytes 10485760 | tf_op jit(solution)/shard_map/pallas_call | solution.py:63
  168.7 4.0 %shard_map.57.refs_6_ = f32[16,3,128,128]{3,2,1,0:T(8,128)S(1)} custom-call(s32[16,3]{1,0:T(8,128)S(1)} %bitcast.45, s32[32]{0:T(128)S(1)} %fusion.7.refs_1_, s32[64]{0:T(128)S(1)} %fusion.6.refs_2_, bf16[33,128,128]{2,1,0:T(8,128)(2,1)} %collective-permute-done.1.refs_3_, bf16[45,128,128]{2,1,0:T(8,128)(2,1)} %collective-permute-done.4.refs_4_, ...), custom_call_target="tpu_custom_call" | custom-call | flops 402653184 | bytes 10485760 | tf_op jit(solution)/shard_map/pallas_call | solution.py:63
  173.4 5.1 %shard_map.58 = bf16[16,3,128,128]{3,2,1,0:T(8,128)(2,1)} custom-call(s32[16,3]{1,0:T(8,128)S(1)} %bitcast.46, s32[32]{0:T(128)S(1)} %fusion.9.refs_1_, s32[64]{0:T(128)S(1)} %fusion.8.refs_2_, bf16[33,128,128]{2,1,0:T(8,128)(2,1)} %collective-permute-done.2.refs_3_, bf16[45,128,128]{2,1,0:T(8,128)(2,1)} %collective-permute-done.5.refs_4_, ...), custom_call_target="tpu_custom_call" | custom-call | flops 402653184 | bytes 10485760 | tf_op jit(solution)/shard_map/pallas_call | solution.py:63
  (36 shorter events, 4.9 us)
Async XLA Ops:
  0.0 1.4 slice-start
  0.0 0.8 copy-start.4
  0.8 15.2 %copy-start.5 = (s32[16,1,2]{0,2,1:T(2,128)S(1)}, s32[16,1,2]{0,2,1:T(2,128)}, u32[]{:S(2)}) copy-start(s32[16,1,2]{0,2,1:T(2,128)} %param.10) | copy-start | bytes 388
  1.6 45.3 %collective-permute-start.3 = (bf16[45,128,128]{2,1,0:T(8,128)(2,1)S(1)}, bf16[45,128,128]{2,1,0:T(8,128)(2,1)}, u32[]{:S(2)}, u32[]{:S(2)}) collective-permute-start(bf16[45,128,128]{2,1,0:T(8,128)(2,1)S(1)} %fusion.2.refs_4_), channel_id=1, source_target_pairs={{16,0},{17,1},{18,2},{19,3},{20,4},{21,5},{22,6},{23,7},{24,8},{25... | collective-permute-start | bytes 4423688 | tf_op jit(solution)/shard_map/ppermute | solution.py:117
  16.2 4.4 %copy-start.2 = (bf16[1,32,2,128,128]{4,3,2,1,0:T(8,128)(2,1)S(1)}, bf16[1,32,2,128,128]{4,3,2,1,0:T(8,128)(2,1)}, u32[]{:S(2)}) copy-start(bf16[1,32,2,128,128]{4,3,2,1,0:T(8,128)(2,1)} %param.11) | copy-start | bytes 6291460
  16.2 99.3 %copy-start.3 = (s32[16,1,3]{0,1,2:T(1,128)S(1)}, s32[16,1,3]{0,1,2:T(1,128)}, u32[]{:S(2)}) copy-start(s32[16,1,3]{0,1,2:T(1,128)} %param.13) | copy-start | bytes 580
  17.7 39.6 %collective-permute-start = (bf16[33,128,128]{2,1,0:T(8,128)(2,1)S(1)}, bf16[33,128,128]{2,1,0:T(8,128)(2,1)S(1)}, u32[]{:S(2)}, u32[]{:S(2)}) collective-permute-start(bf16[33,128,128]{2,1,0:T(8,128)(2,1)S(1)} %fusion.3.refs_3_), channel_id=1, source_target_pairs={{1,0},{2,1},{3,2},{4,3},{5,4},{6,5},{7,6},{8,7},{9,8},{10,9},{11,1... | collective-permute-start | bytes 3244040 | tf_op jit(solution)/shard_map/ppermute | solution.py:117
  20.6 34.7 %collective-permute-start.6 = (bf16[20,128,128]{2,1,0:T(8,128)(2,1)S(1)}, bf16[20,128,128]{2,1,0:T(8,128)(2,1)S(1)}, u32[]{:S(2)}, u32[]{:S(2)}) collective-permute-start(bf16[20,128,128]{2,1,0:T(8,128)(2,1)S(1)} %bitcast.41), channel_id=1, source_target_pairs={{96,0},{97,1},{98,2},{99,3},{100,4},{101,5},{102,6},{103,7},{104,8... | collective-permute-start | bytes 1966088 | tf_op jit(solution)/shard_map/ppermute | solution.py:117
  46.9 38.7 %collective-permute-start.4 = (bf16[45,128,128]{2,1,0:T(8,128)(2,1)}, bf16[45,128,128]{2,1,0:T(8,128)(2,1)}, u32[]{:S(2)}, u32[]{:S(2)}) collective-permute-start(bf16[45,128,128]{2,1,0:T(8,128)(2,1)} %collective-permute-done.3.refs_4_), channel_id=1, source_target_pairs={{16,0},{17,1},{18,2},{19,3},{20,4},{21,5},{22,6},{23,7},{24,8},{25... | collective-permute-start | bytes 4423688 | tf_op jit(solution)/shard_map/ppermute | solution.py:117
  55.3 25.1 %collective-permute-start.7 = (bf16[20,128,128]{2,1,0:T(8,128)(2,1)S(1)}, bf16[20,128,128]{2,1,0:T(8,128)(2,1)S(1)}, u32[]{:S(2)}, u32[]{:S(2)}) collective-permute-start(bf16[20,128,128]{2,1,0:T(8,128)(2,1)S(1)} %collective-permute-done.6), channel_id=1, source_target_pairs={{96,0},{97,1},{98,2},{99,3},{100,4},{101,5},{102,6},{103,7},{104,8... | collective-permute-start | bytes 1966088 | tf_op jit(solution)/shard_map/ppermute | solution.py:117
  57.3 1.0 copy-start
  58.3 50.4 %collective-permute-start.1 = (bf16[33,128,128]{2,1,0:T(8,128)(2,1)S(1)}, bf16[33,128,128]{2,1,0:T(8,128)(2,1)}, u32[]{:S(2)}, u32[]{:S(2)}) collective-permute-start(bf16[33,128,128]{2,1,0:T(8,128)(2,1)S(1)} %collective-permute-done.refs_3_), channel_id=1, source_target_pairs={{1,0},{2,1},{3,2},{4,3},{5,4},{6,5},{7,6},{8,7},{9,8},{10,9},{11,1... | collective-permute-start | bytes 3244040 | tf_op jit(solution)/shard_map/ppermute | solution.py:117
  80.4 26.4 %collective-permute-start.8 = (bf16[20,128,128]{2,1,0:T(8,128)(2,1)S(1)}, bf16[20,128,128]{2,1,0:T(8,128)(2,1)}, u32[]{:S(2)}, u32[]{:S(2)}) collective-permute-start(bf16[20,128,128]{2,1,0:T(8,128)(2,1)S(1)} %collective-permute-done.7), channel_id=1, source_target_pairs={{112,0},{113,1},{114,2},{115,3},{116,4},{117,5},{118,6},{119,7},{1... | collective-permute-start | bytes 1966088 | tf_op jit(solution)/shard_map/ppermute | solution.py:117
  85.5 87.2 %collective-permute-start.5 = (bf16[45,128,128]{2,1,0:T(8,128)(2,1)}, bf16[45,128,128]{2,1,0:T(8,128)(2,1)}, u32[]{:S(2)}, u32[]{:S(2)}) collective-permute-start(bf16[45,128,128]{2,1,0:T(8,128)(2,1)} %collective-permute-done.4.refs_4_), channel_id=1, source_target_pairs={{16,0},{17,1},{18,2},{19,3},{20,4},{21,5},{22,6},{23,7},{24,8},{25... | collective-permute-start | bytes 4423688 | tf_op jit(solution)/shard_map/ppermute | solution.py:117
  106.8 18.5 %collective-permute-start.9 = (bf16[20,128,128]{2,1,0:T(8,128)(2,1)}, bf16[20,128,128]{2,1,0:T(8,128)(2,1)}, u32[]{:S(2)}, u32[]{:S(2)}) collective-permute-start(bf16[20,128,128]{2,1,0:T(8,128)(2,1)} %collective-permute-done.8.refs_5_), channel_id=1, source_target_pairs={{496,0},{497,1},{498,2},{499,3},{500,4},{501,5},{502,6},{503,7},{2... | collective-permute-start | bytes 1966088 | tf_op jit(solution)/shard_map/ppermute | solution.py:117
  108.7 19.8 %collective-permute-start.2 = (bf16[33,128,128]{2,1,0:T(8,128)(2,1)}, bf16[33,128,128]{2,1,0:T(8,128)(2,1)}, u32[]{:S(2)}, u32[]{:S(2)}) collective-permute-start(bf16[33,128,128]{2,1,0:T(8,128)(2,1)} %collective-permute-done.1.refs_3_), channel_id=1, source_target_pairs={{1,0},{2,1},{3,2},{4,3},{5,4},{6,5},{7,6},{8,7},{9,8},{10,9},{11,1... | collective-permute-start | bytes 3244040 | tf_op jit(solution)/shard_map/ppermute | solution.py:117
  115.7 2.4 %copy-start.1 = (bf16[33,128,128]{2,1,0:T(8,128)(2,1)S(1)}, bf16[33,128,128]{2,1,0:T(8,128)(2,1)}, u32[]{:S(2)}) copy-start(bf16[33,128,128]{2,1,0:T(8,128)(2,1)} %copy-done) | copy-start | bytes 3244036
  125.3 40.2 %collective-permute-start.10 = (bf16[20,128,128]{2,1,0:T(8,128)(2,1)}, bf16[20,128,128]{2,1,0:T(8,128)(2,1)S(1)}, u32[]{:S(2)}, u32[]{:S(2)}) collective-permute-start(bf16[20,128,128]{2,1,0:T(8,128)(2,1)} %collective-permute-done.9.refs_5_), channel_id=1, source_target_pairs={{496,0},{497,1},{498,2},{499,3},{500,4},{501,5},{502,6},{503,7},{2... | collective-permute-start | bytes 1966088 | tf_op jit(solution)/shard_map/ppermute | solution.py:117

commit v3 on v2

v3 whole, which is shorter than its diff:
```python
import functools

import jax
import jax.numpy as jnp
from jax import lax
from jax.experimental import pallas as pl
from jax.experimental.pallas import tpu as pltpu
from jax.sharding import PartitionSpec as P

STEPS = 4
HALF = 16
RING = 8
AXES = ("row", "col")
CUT = 46


def block_kernel(first, flip, count, sizes, *refs):
    flip_ref, cols, ka, kb, *rest = refs
    lefts, rest = rest[:2], rest[2:]
    parts, rest = rest[: 2 * len(sizes)], rest[2 * len(sizes) :]
    total = None if first else rest[0]
    out, made_so_far, a, held, a_sems, sems = rest[-6:]
    rows, kept = cols.shape
    span = count + 1

    def left_copy(n, slot):
        return pltpu.make_async_copy(lefts[n].at[pl.ds(0, a.shape[1])], a.at[slot], a_sems.at[slot])

    copies = [[], []]
    for slot in range(2):
        at = slot * span
        for n, size in enumerate(sizes):
            part = parts[slot * len(sizes) + n]
            copies[slot].append(
                pltpu.make_async_copy(part.at[pl.ds(0, size)], held.at[pl.ds(at, size)], sems.at[slot, n])
            )
            at += size
    if flip:

        @pl.when(flip_ref[0] == 0)
        def _():
            left_copy(0, 0).start()
            left_copy(1, 1).start()

        @pl.when(flip_ref[0] != 0)
        def _():
            left_copy(1, 0).start()
            left_copy(0, 1).start()
    else:
        left_copy(0, 0).start()
        left_copy(1, 1).start()
    for copy in copies[0] + copies[1]:
        copy.start()
    for slot in range(2):
        held[slot * span + count] = jnp.zeros(held.shape[1:], held.dtype)

    for slot in range(2):
        left_copy(slot, slot).wait()
        for copy in copies[slot]:
            copy.wait()

        @pl.loop(0, rows, unroll=4)
        def _(i):
            left = jnp.concatenate([a[slot, 2 * i], a[slot, 2 * i + 1]], axis=1)
            right = []
            for o in range(kept):
                j = cols[i, o]
                low, high = kb[slot, 2 * j], kb[slot, 2 * j + 1]
                column = []
                for k in range(2):
                    want = ka[slot, 2 * i + k]
                    place = jnp.where(low == want, 2 * j, jnp.where(high == want, 2 * j + 1, count))
                    column.append(held[slot * span + place])
                right.append(jnp.concatenate(column, axis=0))
            made = jnp.dot(left, jnp.concatenate(right, axis=1), preferred_element_type=jnp.float32)
            for o in range(kept):
                value = made[:, o * 128 : (o + 1) * 128]
                if slot:
                    value = value + made_so_far[i, o]
                    out[i, o] = value.astype(out.dtype)
                else:
                    made_so_far[i, o] = value if first else value + total[i, o]


def contribute(total, flip, cols, ka, kb, lefts, parts, sizes, last):
    rows, kept = cols.shape
    block = lefts[0].shape[1:]
    count = sum(sizes)
    first = total is None
    smem = pl.BlockSpec(memory_space=pltpu.SMEM)
    vmem = pl.BlockSpec(memory_space=pltpu.VMEM)
    whole = pl.BlockSpec(memory_space=pl.ANY)
    tall = (rows, kept) + block
    flat = [part for step in parts for part in step]
    return pl.pallas_call(
        functools.partial(block_kernel, first, flip is not None, count, sizes),
        out_shape=jax.ShapeDtypeStruct(tall, jnp.bfloat16 if last else jnp.float32),
        in_specs=[smem] * 4 + [whole] * (2 + len(flat)) + ([] if first else [vmem]),
        out_specs=vmem,
        scratch_shapes=[
            pltpu.VMEM(tall, jnp.float32),
            pltpu.VMEM((2, 2 * rows) + block, jnp.bfloat16),
            pltpu.VMEM((2 * (count + 1),) + block, jnp.bfloat16),
            pltpu.SemaphoreType.DMA((2,)),
            pltpu.SemaphoreType.DMA((2, len(sizes))),
        ],
        compiler_params=pltpu.CompilerParams(vmem_limit_bytes=28 * 2**20),
        cost_estimate=pl.CostEstimate(
            flops=rows * kept * 8 * block[0] ** 3, bytes_accessed=12 * 2**20, transcendentals=0
        ),
    )(
        jnp.zeros((1,), jnp.int32) if flip is None else flip,
        cols,
        jnp.stack(ka),
        jnp.stack(kb),
        *lefts,
        *flat,
        *(() if first else (total,)),
    )


def with_indices(blocks, indices):
    flat = indices.reshape(-1).astype(blocks.dtype)
    extra = jnp.zeros((1,) + blocks.shape[1:], blocks.dtype).at[0, 0, : flat.shape[0]].set(flat)
    return jnp.concatenate([blocks, extra], axis=0)


def indices_of(blocks, count):
    return blocks[-1, 0, :count].astype(jnp.int32)


def after(value, *others):
    return lax.optimization_barrier((value, *others))


class Paths:
    def __init__(self, n_row, n_col):
        self.n_row, self.n_col = n_row, n_col
        self.down = self.pairs(lambda z, y, t: (z + t * (y == RING - 1), y + 1))
        self.up_three = self.pairs(lambda z, y, t: (z + t * (3 <= y <= 5), y - 3))
        self.up_two = self.pairs(lambda z, y, t: (z, y - 2))
        self.up = self.pairs(lambda z, y, t: (z - t * (y == 0), y - 1))
        self.side_two = self.over_columns(lambda col: col + 2)
        self.side_odd = self.over_columns(lambda col: col + (3 if col % 2 else 1))
        self.swap = self.over_columns(lambda col: col ^ 1)

    def over_columns(self, source):
        return [
            (row * self.n_col + source(col) % self.n_col, row * self.n_col + col)
            for row in range(self.n_row)
            for col in range(self.n_col)
        ]

    def pairs(self, source):
        made = []
        for row in range(self.n_row):
            for col in range(self.n_col):
                z, y = source(*divmod(row, RING), 1 if col < self.n_col // 2 else -1)
                from_row = z % (self.n_row // RING) * RING + y % RING
                made.append((from_row * self.n_col + col, row * self.n_col + col))
        return made


def local(paths, a_blocks, a_cols, b_blocks, b_rows, out_cols):
    cols = out_cols[:, 0]
    ka, kb = a_cols[:, 0].reshape(-1), b_rows[0].reshape(-1)
    block = b_blocks.shape[3:]
    own = b_blocks[0].reshape((-1,) + block)
    count = own.shape[0]
    send = lambda value, pairs: lax.ppermute(value, AXES, pairs)
    sizes = (CUT, count - CUT)

    left = with_indices(a_blocks[:, 0].reshape((-1,) + block), ka)
    left_two = send(left, paths.side_two)
    left_odd = send(left, paths.side_odd)
    left_other = send(left_two, paths.swap)
    odd = lax.axis_index("col") % 2

    rest = own[CUT:]
    most = [with_indices(own[:CUT], kb)]
    up_one = send(rest, paths.up_three)
    most.append(send(most[0], paths.down))
    ready, left_two, up_one = after(most[1], left_two, up_one)
    most[1] = ready
    most.append(send(most[1], paths.down))
    third = send(up_one, paths.up_two)
    ready, left_odd, third = after(most[2], left_odd, third)
    most[2] = ready
    most.append(send(most[2], paths.down))
    second = send(third, paths.up)
    first = send(second, paths.up)
    parts = [[most[0], rest], [most[1], first], [most[2], second], [most[3], third]]

    rows_of = lambda value: indices_of(value, kb.shape[0])
    ka_odd, ka_other = indices_of(left_odd, ka.shape[0]), indices_of(left_other, ka.shape[0])
    ka_one, ka_three = jnp.where(odd == 0, ka_odd, ka_other), jnp.where(odd == 0, ka_other, ka_odd)
    total = contribute(
        None,
        None,
        cols,
        [ka, indices_of(left_two, ka.shape[0])],
        [kb, rows_of(most[2])],
        [left, left_two],
        [parts[0], parts[2]],
        sizes,
        False,
    )
    total = contribute(
        total,
        odd.reshape(1),
        cols,
        [ka_one, ka_three],
        [rows_of(most[1]), rows_of(most[3])],
        [left_odd, left_other],
        [parts[1], parts[3]],
        sizes,
        True,
    )
    return total[:, None]


def solution(mesh):
    paths = Paths(mesh.shape["row"], mesh.shape["col"])
    return jax.shard_map(
        functools.partial(local, paths),
        mesh=mesh,
        in_specs=(
            P("row", "col", None, None, None),
            P("row", "col", None),
            P("row", "col", None, None, None),
            P("row", "col", None),
            P("row", "col", None),
        ),
        out_specs=P("row", "col", None, None, None),
        check_vma=False,
    )
```

time: 179 us -> 192 us (1.073)
  the two profiles are of different devices: /device:TPU:1 before, /device:TPU:128 now
where the time goes in v3:
time: 192 us; the launch traced here: 191 us
  starting transfers between devices  91.4 us (48%)
  waiting for transfers between devices  80.4 us (42%)
  Pallas kernels  10.1 us (5%)
  local copies, waits for them, and re-layouts  5.22 us (3%)
  other arithmetic  3.78 us (2%)
    ppermute x10, starting transfers between devices, local(): send = lambda value, pairs: lax.ppermute(value, AXES, pairs)  91.4 us
    ppermute x10, waiting for transfers between devices, local(): send = lambda value, pairs: lax.ppermute(value, AXES, pairs)  80.4 us
    pallas_call x2, Pallas kernels, contribute(): pl.pallas_call(functools.partial(block_kernel, first, flip is not None, c...  10.1 us
  transfers between devices with their start and end apart: 10, of which 6 were waited for; matrix products, arithmetic and copies ran while one was open for 3% of the time, Pallas kernels for 2%

profile of v3, /device:TPU:128, one launch (start us, length us, event | category | flops | bytes accessed | tf_op | source)
XLA Modules:
  0.0 191.1 jit_solution(12767654324960140624)
XLA Ops:
  0.0 0.8 copy-done.6
  1.6 3.6 %collective-permute-start = (bf16[47,128,128]{2,1,0:T(8,128)(2,1)S(1)}, bf16[47,128,128]{2,1,0:T(8,128)(2,1)}, u32[]{:S(2)}, u32[]{:S(2)}) collective-permute-start(bf16[47,128,128]{2,1,0:T(8,128)(2,1)S(1)} %fusion.2.refs_6_), channel_id=1, source_target_pairs={{16,0},{17,1},{18,2},{19,3},{20,4},{21,5},{22,6},{23,7},{24,8},{25... | collective-permute-start | bytes 4620296 | tf_op jit(solution)/shard_map/ppermute | solution.py:170
  5.4 1.5 fusion.3.refs_4_
  6.9 12.2 %collective-permute-start.1 = (bf16[33,128,128]{2,1,0:T(8,128)(2,1)S(1)}, bf16[33,128,128]{2,1,0:T(8,128)(2,1)}, u32[]{:S(2)}, u32[]{:S(2)}) collective-permute-start(bf16[33,128,128]{2,1,0:T(8,128)(2,1)S(1)} %fusion.3.refs_4_), channel_id=1, source_target_pairs={{2,0},{3,1},{4,2},{5,3},{6,4},{7,5},{8,6},{9,7},{10,8},{11,9},{12,... | collective-permute-start | bytes 3244040 | tf_op jit(solution)/shard_map/ppermute | solution.py:170
  19.2 1.9 %collective-permute-start.2 = (bf16[18,128,128]{2,1,0:T(8,128)(2,1)S(1)}, bf16[18,128,128]{2,1,0:T(8,128)(2,1)S(1)}, u32[]{:S(2)}, u32[]{:S(2)}) collective-permute-start(bf16[18,128,128]{2,1,0:T(8,128)(2,1)S(1)} %bitcast.26), channel_id=1, source_target_pairs={{80,0},{81,1},{82,2},{83,3},{84,4},{85,5},{86,6},{87,7},{88,8},{89... | collective-permute-start | bytes 1769480 | tf_op jit(solution)/shard_map/ppermute | solution.py:170
  21.1 35.9 %collective-permute-done.2 = bf16[18,128,128]{2,1,0:T(8,128)(2,1)S(1)} collective-permute-done((bf16[18,128,128]{2,1,0:T(8,128)(2,1)S(1)}, bf16[18,128,128]{2,1,0:T(8,128)(2,1)S(1)}, u32[]{:S(2)}, u32[]{:S(2)}) %collective-permute-start.2) | collective-permute-done | bytes 589856 | tf_op jit(solution)/shard_map/ppermute | solution.py:170
  57.0 14.1 %collective-permute-start.3 = (bf16[47,128,128]{2,1,0:T(8,128)(2,1)}, bf16[47,128,128]{2,1,0:T(8,128)(2,1)}, u32[]{:S(2)}, u32[]{:S(2)}) collective-permute-start(bf16[47,128,128]{2,1,0:T(8,128)(2,1)} %collective-permute-done.refs_6_), channel_id=1, source_target_pairs={{16,0},{17,1},{18,2},{19,3},{20,4},{21,5},{22,6},{23,7},{24,8},{25... | collective-permute-start | bytes 4620296 | tf_op jit(solution)/shard_map/ppermute | solution.py:170
  71.1 1.9 %collective-permute-start.4 = (bf16[33,128,128]{2,1,0:T(8,128)(2,1)S(1)}, bf16[33,128,128]{2,1,0:T(8,128)(2,1)S(1)}, u32[]{:S(2)}, u32[]{:S(2)}) collective-permute-start(bf16[33,128,128]{2,1,0:T(8,128)(2,1)S(1)} %fusion.3.refs_4_), channel_id=1, source_target_pairs={{1,0},{4,1},{3,2},{6,3},{5,4},{8,5},{7,6},{10,7},{9,8},{12,9},{11,... | collective-permute-start | bytes 3244040 | tf_op jit(solution)/shard_map/ppermute | solution.py:170
  73.1 1.9 %collective-permute-start.5 = (bf16[18,128,128]{2,1,0:T(8,128)(2,1)S(1)}, bf16[18,128,128]{2,1,0:T(8,128)(2,1)S(1)}, u32[]{:S(2)}, u32[]{:S(2)}) collective-permute-start(bf16[18,128,128]{2,1,0:T(8,128)(2,1)S(1)} %collective-permute-done.2), channel_id=1, source_target_pairs={{96,0},{97,1},{98,2},{99,3},{100,4},{101,5},{102,6},{103,7},{104,8... | collective-permute-start | bytes 1769480 | tf_op jit(solution)/shard_map/ppermute | solution.py:170
  75.0 2.4 %collective-permute-start.6 = (bf16[33,128,128]{2,1,0:T(8,128)(2,1)}, bf16[33,128,128]{2,1,0:T(8,128)(2,1)}, u32[]{:S(2)}, u32[]{:S(2)}) collective-permute-start(bf16[33,128,128]{2,1,0:T(8,128)(2,1)} %collective-permute-done.1.refs_5_), channel_id=1, source_target_pairs={{1,0},{0,1},{3,2},{2,3},{5,4},{4,5},{7,6},{6,7},{9,8},{8,9},{11,10... | collective-permute-start | bytes 3244040 | tf_op jit(solution)/shard_map/ppermute | solution.py:170
  77.4 8.3 %collective-permute-done.4.refs_4_ = bf16[33,128,128]{2,1,0:T(8,128)(2,1)S(1)} collective-permute-done((bf16[33,128,128]{2,1,0:T(8,128)(2,1)S(1)}, bf16[33,128,128]{2,1,0:T(8,128)(2,1)S(1)}, u32[]{:S(2)}, u32[]{:S(2)}) %collective-permute-start.4) | collective-permute-done | bytes 1081376 | tf_op jit(solution)/shard_map/ppermute | solution.py:170
  85.7 1.0 copy-done
  86.7 12.1 %collective-permute-done.5.refs_9_ = bf16[18,128,128]{2,1,0:T(8,128)(2,1)S(1)} collective-permute-done((bf16[18,128,128]{2,1,0:T(8,128)(2,1)S(1)}, bf16[18,128,128]{2,1,0:T(8,128)(2,1)S(1)}, u32[]{:S(2)}, u32[]{:S(2)}) %collective-permute-start.5) | collective-permute-done | bytes 589856 | tf_op jit(solution)/shard_map/ppermute | solution.py:170
  98.8 0.8 copy-done.2
  99.6 5.0 %collective-permute-done.3.refs_8_ = bf16[47,128,128]{2,1,0:T(8,128)(2,1)} collective-permute-done((bf16[47,128,128]{2,1,0:T(8,128)(2,1)}, bf16[47,128,128]{2,1,0:T(8,128)(2,1)}, u32[]{:S(2)}, u32[]{:S(2)}) %collective-permute-start.3) | collective-permute-done | bytes 1540128 | tf_op jit(solution)/shard_map/ppermute | solution.py:170
  104.6 49.5 %collective-permute-start.7 = (bf16[47,128,128]{2,1,0:T(8,128)(2,1)}, bf16[47,128,128]{2,1,0:T(8,128)(2,1)}, u32[]{:S(2)}, u32[]{:S(2)}) collective-permute-start(bf16[47,128,128]{2,1,0:T(8,128)(2,1)} %collective-permute-done.3.refs_8_), channel_id=1, source_target_pairs={{16,0},{17,1},{18,2},{19,3},{20,4},{21,5},{22,6},{23,7},{24,8},{25... | collective-permute-start | bytes 4620296 | tf_op jit(solution)/shard_map/ppermute | solution.py:170
  155.2 1.9 collective-permute-start.8
  157.8 0.7 bitcast_convert_fusion
  158.5 0.7 fusion.4
  159.2 11.0 %collective-permute-done.8.refs_9_ = bf16[18,128,128]{2,1,0:T(8,128)(2,1)S(1)} collective-permute-done((bf16[18,128,128]{2,1,0:T(8,128)(2,1)}, bf16[18,128,128]{2,1,0:T(8,128)(2,1)S(1)}, u32[]{:S(2)}, u32[]{:S(2)}) %collective-permute-start.8) | collective-permute-done | bytes 589856 | tf_op jit(solution)/shard_map/ppermute | solution.py:170
  170.2 1.9 collective-permute-start.9
  172.1 4.0 %shard_map.55.refs_10_ = f32[16,3,128,128]{3,2,1,0:T(8,128)S(1)} custom-call(s32[1]{0:T(128)} %constant.72.clone.1.refs_0_, s32[16,3]{1,0:T(8,128)S(1)} %bitcast.28, s32[2,32]{1,0:T(2,128)S(1)} %pad_add_fusion.1.refs_2_, s32[2,64]{1,0:T(2,128)S(1)} %pad_add_fusion.2.refs_3_, bf16[33,128,128]{2,1,0:T(8,128)(2,1)S(1)} %fusion.3.refs_4_, ...), custom_call_target="tpu_custom_call" | custom-call | flops 805306368 | bytes 12582912 | tf_op jit(solution)/shard_map/pallas_call | solution.py:95
  176.8 8.1 %collective-permute-done.9.refs_7_ = bf16[18,128,128]{2,1,0:T(8,128)(2,1)S(1)} collective-permute-done((bf16[18,128,128]{2,1,0:T(8,128)(2,1)S(1)}, bf16[18,128,128]{2,1,0:T(8,128)(2,1)S(1)}, u32[]{:S(2)}, u32[]{:S(2)}) %collective-permute-start.9) | collective-permute-done | bytes 589856 | tf_op jit(solution)/shard_map/ppermute | solution.py:170
  184.9 6.1 %shard_map.56 = bf16[16,3,128,128]{3,2,1,0:T(8,128)(2,1)} custom-call(s32[1]{0:T(128)} %bitcast.refs_0_, s32[16,3]{1,0:T(8,128)S(1)} %bitcast.29, s32[2,32]{1,0:T(2,128)S(1)} %pad_add_fusion.refs_2_, s32[2,64]{1,0:T(2,128)S(1)} %maximum_convert_fusion.refs_3_, bf16[33,128,128]{2,1,0:T(8,128)(2,1)S(1)} %copy-done.1, ...), custom_call_target="tpu_custom_call" | custom-call | flops 805306368 | bytes 12582912 | tf_op jit(solution)/shard_map/pallas_call | solution.py:95
  (39 shorter events, 3.6 us)
Async XLA Ops:
  0.0 1.4 slice-start
  0.0 0.8 copy-start.6
  0.8 4.4 %copy-start.7 = (s32[16,1,2]{0,2,1:T(2,128)S(1)}, s32[16,1,2]{0,2,1:T(2,128)}, u32[]{:S(2)}) copy-start(s32[16,1,2]{0,2,1:T(2,128)} %param.10) | copy-start | bytes 388
  1.6 55.4 %collective-permute-start = (bf16[47,128,128]{2,1,0:T(8,128)(2,1)S(1)}, bf16[47,128,128]{2,1,0:T(8,128)(2,1)}, u32[]{:S(2)}, u32[]{:S(2)}) collective-permute-start(bf16[47,128,128]{2,1,0:T(8,128)(2,1)S(1)} %fusion.2.refs_6_), channel_id=1, source_target_pairs={{16,0},{17,1},{18,2},{19,3},{20,4},{21,5},{22,6},{23,7},{24,8},{25... | collective-permute-start | bytes 4620296 | tf_op jit(solution)/shard_map/ppermute | solution.py:170
  5.4 13.8 %copy-start.4 = (bf16[1,32,2,128,128]{4,3,2,1,0:T(8,128)(2,1)S(1)}, bf16[1,32,2,128,128]{4,3,2,1,0:T(8,128)(2,1)}, u32[]{:S(2)}) copy-start(bf16[1,32,2,128,128]{4,3,2,1,0:T(8,128)(2,1)} %param.11) | copy-start | bytes 6291460
  5.4 149.0 %copy-start.5 = (s32[16,1,3]{0,1,2:T(1,128)S(1)}, s32[16,1,3]{0,1,2:T(1,128)}, u32[]{:S(2)}) copy-start(s32[16,1,3]{0,1,2:T(1,128)} %param.13) | copy-start | bytes 580
  6.9 50.1 %collective-permute-start.1 = (bf16[33,128,128]{2,1,0:T(8,128)(2,1)S(1)}, bf16[33,128,128]{2,1,0:T(8,128)(2,1)}, u32[]{:S(2)}, u32[]{:S(2)}) collective-permute-start(bf16[33,128,128]{2,1,0:T(8,128)(2,1)S(1)} %fusion.3.refs_4_), channel_id=1, source_target_pairs={{2,0},{3,1},{4,2},{5,3},{6,4},{7,5},{8,6},{9,7},{10,8},{11,9},{12,... | collective-permute-start | bytes 3244040 | tf_op jit(solution)/shard_map/ppermute | solution.py:170
  19.2 37.8 %collective-permute-start.2 = (bf16[18,128,128]{2,1,0:T(8,128)(2,1)S(1)}, bf16[18,128,128]{2,1,0:T(8,128)(2,1)S(1)}, u32[]{:S(2)}, u32[]{:S(2)}) collective-permute-start(bf16[18,128,128]{2,1,0:T(8,128)(2,1)S(1)} %bitcast.26), channel_id=1, source_target_pairs={{80,0},{81,1},{82,2},{83,3},{84,4},{85,5},{86,6},{87,7},{88,8},{89... | collective-permute-start | bytes 1769480 | tf_op jit(solution)/shard_map/ppermute | solution.py:170
  57.0 47.6 %collective-permute-start.3 = (bf16[47,128,128]{2,1,0:T(8,128)(2,1)}, bf16[47,128,128]{2,1,0:T(8,128)(2,1)}, u32[]{:S(2)}, u32[]{:S(2)}) collective-permute-start(bf16[47,128,128]{2,1,0:T(8,128)(2,1)} %collective-permute-done.refs_6_), channel_id=1, source_target_pairs={{16,0},{17,1},{18,2},{19,3},{20,4},{21,5},{22,6},{23,7},{24,8},{25... | collective-permute-start | bytes 4620296 | tf_op jit(solution)/shard_map/ppermute | solution.py:170
  71.1 14.6 %collective-permute-start.4 = (bf16[33,128,128]{2,1,0:T(8,128)(2,1)S(1)}, bf16[33,128,128]{2,1,0:T(8,128)(2,1)S(1)}, u32[]{:S(2)}, u32[]{:S(2)}) collective-permute-start(bf16[33,128,128]{2,1,0:T(8,128)(2,1)S(1)} %fusion.3.refs_4_), channel_id=1, source_target_pairs={{1,0},{4,1},{3,2},{6,3},{5,4},{8,5},{7,6},{10,7},{9,8},{12,9},{11,... | collective-permute-start | bytes 3244040 | tf_op jit(solution)/shard_map/ppermute | solution.py:170
  73.1 25.7 %collective-permute-start.5 = (bf16[18,128,128]{2,1,0:T(8,128)(2,1)S(1)}, bf16[18,128,128]{2,1,0:T(8,128)(2,1)S(1)}, u32[]{:S(2)}, u32[]{:S(2)}) collective-permute-start(bf16[18,128,128]{2,1,0:T(8,128)(2,1)S(1)} %collective-permute-done.2), channel_id=1, source_target_pairs={{96,0},{97,1},{98,2},{99,3},{100,4},{101,5},{102,6},{103,7},{104,8... | collective-permute-start | bytes 1769480 | tf_op jit(solution)/shard_map/ppermute | solution.py:170
  75.0 83.5 %collective-permute-start.6 = (bf16[33,128,128]{2,1,0:T(8,128)(2,1)}, bf16[33,128,128]{2,1,0:T(8,128)(2,1)}, u32[]{:S(2)}, u32[]{:S(2)}) collective-permute-start(bf16[33,128,128]{2,1,0:T(8,128)(2,1)} %collective-permute-done.1.refs_5_), channel_id=1, source_target_pairs={{1,0},{0,1},{3,2},{2,3},{5,4},{4,5},{7,6},{6,7},{9,8},{8,9},{11,10... | collective-permute-start | bytes 3244040 | tf_op jit(solution)/shard_map/ppermute | solution.py:170
  85.7 1.0 copy-start
  98.8 0.8 copy-start.2
  104.6 71.6 %collective-permute-start.7 = (bf16[47,128,128]{2,1,0:T(8,128)(2,1)}, bf16[47,128,128]{2,1,0:T(8,128)(2,1)}, u32[]{:S(2)}, u32[]{:S(2)}) collective-permute-start(bf16[47,128,128]{2,1,0:T(8,128)(2,1)} %collective-permute-done.3.refs_8_), channel_id=1, source_target_pairs={{16,0},{17,1},{18,2},{19,3},{20,4},{21,5},{22,6},{23,7},{24,8},{25... | collective-permute-start | bytes 4620296 | tf_op jit(solution)/shard_map/ppermute | solution.py:170
  155.2 15.0 %collective-permute-start.8 = (bf16[18,128,128]{2,1,0:T(8,128)(2,1)}, bf16[18,128,128]{2,1,0:T(8,128)(2,1)S(1)}, u32[]{:S(2)}, u32[]{:S(2)}) collective-permute-start(bf16[18,128,128]{2,1,0:T(8,128)(2,1)} %copy-done.2), channel_id=1, source_target_pairs={{496,0},{497,1},{498,2},{499,3},{500,4},{501,5},{502,6},{503,7},{2... | collective-permute-start | bytes 1769480 | tf_op jit(solution)/shard_map/ppermute | solution.py:170
  170.2 14.8 %collective-permute-start.9 = (bf16[18,128,128]{2,1,0:T(8,128)(2,1)S(1)}, bf16[18,128,128]{2,1,0:T(8,128)(2,1)S(1)}, u32[]{:S(2)}, u32[]{:S(2)}) collective-permute-start(bf16[18,128,128]{2,1,0:T(8,128)(2,1)S(1)} %collective-permute-done.8.refs_9_), channel_id=1, source_target_pairs={{496,0},{497,1},{498,2},{499,3},{500,4},{501,5},{502,6},{503,7},{2... | collective-permute-start | bytes 1769480 | tf_op jit(solution)/shard_map/ppermute | solution.py:170
  172.1 12.8 %copy-start.1 = (bf16[33,128,128]{2,1,0:T(8,128)(2,1)S(1)}, bf16[33,128,128]{2,1,0:T(8,128)(2,1)}, u32[]{:S(2)}) copy-start(bf16[33,128,128]{2,1,0:T(8,128)(2,1)} %copy-done) | copy-start | bytes 3244036
  172.1 12.8 %copy-start.3 = (bf16[18,128,128]{2,1,0:T(8,128)(2,1)S(1)}, bf16[18,128,128]{2,1,0:T(8,128)(2,1)}, u32[]{:S(2)}) copy-start(bf16[18,128,128]{2,1,0:T(8,128)(2,1)} %copy-done.2) | copy-start | bytes 1769476

commit v4 on v3

--- a/solution.py
+++ b/solution.py
@@ -11,7 +11,7 @@
 HALF = 16
 RING = 8
 AXES = ("row", "col")
-CUT = 46
+CUTS = (30, 44)
 
 
 def block_kernel(first, flip, count, sizes, *refs):
@@ -129,14 +129,12 @@
     return blocks[-1, 0, :count].astype(jnp.int32)
 
 
-def after(value, *others):
-    return lax.optimization_barrier((value, *others))
-
-
 class Paths:
     def __init__(self, n_row, n_col):
         self.n_row, self.n_col = n_row, n_col
         self.down = self.pairs(lambda z, y, t: (z + t * (y == RING - 1), y + 1))
+        self.ring = self.pairs(lambda z, y, t: (z, y + 1))
+        self.enter = self.pairs(lambda z, y, t: (z + t, y), only=0)
         self.up_three = self.pairs(lambda z, y, t: (z + t * (3 <= y <= 5), y - 3))
         self.up_two = self.pairs(lambda z, y, t: (z, y - 2))
         self.up = self.pairs(lambda z, y, t: (z - t * (y == 0), y - 1))
@@ -151,9 +149,11 @@
             for col in range(self.n_col)
         ]
 
-    def pairs(self, source):
+    def pairs(self, source, only=None):
         made = []
         for row in range(self.n_row):
+            if only is not None and row % RING != only:
+                continue
             for col in range(self.n_col):
                 z, y = source(*divmod(row, RING), 1 if col < self.n_col // 2 else -1)
                 from_row = z % (self.n_row // RING) * RING + y % RING
@@ -168,7 +168,8 @@
     own = b_blocks[0].reshape((-1,) + block)
     count = own.shape[0]
     send = lambda value, pairs: lax.ppermute(value, AXES, pairs)
-    sizes = (CUT, count - CUT)
+    cut, end = CUTS
+    sizes = (cut, end - cut, count - end)
 
     left = with_indices(a_blocks[:, 0].reshape((-1,) + block), ka)
     left_two = send(left, paths.side_two)
@@ -176,20 +177,29 @@
     left_other = send(left_two, paths.swap)
     odd = lax.axis_index("col") % 2
 
-    rest = own[CUT:]
-    most = [with_indices(own[:CUT], kb)]
+    rest = own[end:]
+    most = [with_indices(own[:cut], kb)]
+    some = [own[cut:end]]
+    at_edge = lax.axis_index("row") % RING == 0
+
+    def inside(value):
+        return send(jnp.where(at_edge, send(value, paths.enter), value), paths.ring)
+
     up_one = send(rest, paths.up_three)
     most.append(send(most[0], paths.down))
-    ready, left_two, up_one = after(most[1], left_two, up_one)
-    most[1] = ready
+    some.append(inside(some[0]))
+    most[1], some[1], left_two, left_odd, up_one = lax.optimization_barrier(
+        (most[1], some[1], left_two, left_odd, up_one)
+    )
+    third = send(up_one, paths.up_two)
     most.append(send(most[1], paths.down))
-    third = send(up_one, paths.up_two)
-    ready, left_odd, third = after(most[2], left_odd, third)
-    most[2] = ready
+    some.append(inside(some[1]))
+    most[2], some[2], third = lax.optimization_barrier((most[2], some[2], third))
     most.append(send(most[2], paths.down))
+    some.append(inside(some[2]))
     second = send(third, paths.up)
     first = send(second, paths.up)
-    parts = [[most[0], rest], [most[1], first], [most[2], second], [most[3], third]]
+    parts = list(zip(most, some, [rest, first, second, third]))
 
     rows_of = lambda value: indices_of(value, kb.shape[0])
     ka_odd, ka_other = indices_of(left_odd, ka.shape[0]), indices_of(left_other, ka.shape[0])

time: 192 us -> 198 us (1.031)
  the two profiles are of different devices: /device:TPU:128 before, /device:TPU:4 now
where the time goes in v4:
time: 198 us; the launch traced here: 197 us
  waiting for transfers between devices  92.2 us (47%)
  starting transfers between devices  83.8 us (42%)
  Pallas kernels  10.2 us (5%)
  other arithmetic  6.19 us (3%)
  local copies, waits for them, and re-layouts  4.51 us (2%)
    ppermute x16, waiting for transfers between devices, local(): send = lambda value, pairs: lax.ppermute(value, AXES, pairs)  92.2 us
    ppermute x16, starting transfers between devices, local(): send = lambda value, pairs: lax.ppermute(value, AXES, pairs)  83.8 us
    pallas_call x2, Pallas kernels, contribute(): pl.pallas_call(functools.partial(block_kernel, first, flip is not None, c...  10.2 us
  transfers between devices with their start and end apart: 16, of which 5 were waited for; matrix products, arithmetic and copies ran while one was open for 4% of the time, Pallas kernels for 2%

profile of v4, /device:TPU:4, one launch (start us, length us, event | category | flops | bytes accessed | tf_op | source)
XLA Modules:
  0.0 197.2 jit_solution(13427859250422435743)
XLA Ops:
  1.1 10.9 %collective-permute-start.1 = (bf16[14,128,128]{2,1,0:T(8,128)(2,1)S(1)}, bf16[14,128,128]{2,1,0:T(8,128)(2,1)}, u32[]{:S(2)}, u32[]{:S(2)}) collective-permute-start(bf16[14,128,128]{2,1,0:T(8,128)(2,1)S(1)} %bitcast.28), channel_id=1, source_target_pairs={{128,0},{129,1},{130,2},{131,3},{132,4},{133,5},{134,6},{135,7},{3... | collective-permute-start | bytes 1376264 | tf_op jit(solution)/shard_map/ppermute | solution.py:170
  12.9 1.4 fusion.2.refs_4_
  14.3 2.4 %collective-permute-start.3 = (bf16[33,128,128]{2,1,0:T(8,128)(2,1)S(1)}, bf16[33,128,128]{2,1,0:T(8,128)(2,1)}, u32[]{:S(2)}, u32[]{:S(2)}) collective-permute-start(bf16[33,128,128]{2,1,0:T(8,128)(2,1)S(1)} %fusion.2.refs_4_), channel_id=1, source_target_pairs={{2,0},{3,1},{4,2},{5,3},{6,4},{7,5},{8,6},{9,7},{10,8},{11,9},{12,... | collective-permute-start | bytes 3244040 | tf_op jit(solution)/shard_map/ppermute | solution.py:170
  16.8 1.9 collective-permute-start.4
  19.1 7.1 %collective-permute-start = (bf16[31,128,128]{2,1,0:T(8,128)(2,1)S(1)}, bf16[31,128,128]{2,1,0:T(8,128)(2,1)}, u32[]{:S(2)}, u32[]{:S(2)}) collective-permute-start(bf16[31,128,128]{2,1,0:T(8,128)(2,1)S(1)} %fusion.3.refs_6_), channel_id=1, source_target_pairs={{16,0},{17,1},{18,2},{19,3},{20,4},{21,5},{22,6},{23,7},{24,8},{25... | collective-permute-start | bytes 3047432 | tf_op jit(solution)/shard_map/ppermute | solution.py:170
  27.3 2.5 %collective-permute-start.5 = (bf16[20,128,128]{2,1,0:T(8,128)(2,1)S(1)}, bf16[20,128,128]{2,1,0:T(8,128)(2,1)}, u32[]{:S(2)}, u32[]{:S(2)}) collective-permute-start(bf16[20,128,128]{2,1,0:T(8,128)(2,1)S(1)} %bitcast.30), channel_id=1, source_target_pairs={{80,0},{81,1},{82,2},{83,3},{84,4},{85,5},{86,6},{87,7},{88,8},{89... | collective-permute-start | bytes 1966088 | tf_op jit(solution)/shard_map/ppermute | solution.py:170
  30.9 1.9 collective-permute-start.2
  32.9 33.0 %collective-permute-done.5 = bf16[20,128,128]{2,1,0:T(8,128)(2,1)} collective-permute-done((bf16[20,128,128]{2,1,0:T(8,128)(2,1)S(1)}, bf16[20,128,128]{2,1,0:T(8,128)(2,1)}, u32[]{:S(2)}, u32[]{:S(2)}) %collective-permute-start.5) | collective-permute-done | bytes 655392 | tf_op jit(solution)/shard_map/ppermute | solution.py:170
  65.9 8.2 %collective-permute-start.8 = (bf16[14,128,128]{2,1,0:T(8,128)(2,1)S(1)}, bf16[14,128,128]{2,1,0:T(8,128)(2,1)S(1)}, u32[]{:S(2)}, u32[]{:S(2)}) collective-permute-start(bf16[14,128,128]{2,1,0:T(8,128)(2,1)S(1)} %collective-permute-done.2.refs_7_), channel_id=1, source_target_pairs={{128,0},{129,1},{130,2},{131,3},{132,4},{133,5},{134,6},{135,7},{3... | collective-permute-start | bytes 1376264 | tf_op jit(solution)/shard_map/ppermute | solution.py:170
  74.1 1.9 collective-permute-start.7
  76.0 2.2 %collective-permute-start.10 = (bf16[20,128,128]{2,1,0:T(8,128)(2,1)}, bf16[20,128,128]{2,1,0:T(8,128)(2,1)}, u32[]{:S(2)}, u32[]{:S(2)}) collective-permute-start(bf16[20,128,128]{2,1,0:T(8,128)(2,1)} %collective-permute-done.5), channel_id=1, source_target_pairs={{96,0},{97,1},{98,2},{99,3},{100,4},{101,5},{102,6},{103,7},{104,8... | collective-permute-start | bytes 1966088 | tf_op jit(solution)/shard_map/ppermute | solution.py:170
  78.2 27.0 %collective-permute-start.6 = (bf16[33,128,128]{2,1,0:T(8,128)(2,1)}, bf16[33,128,128]{2,1,0:T(8,128)(2,1)}, u32[]{:S(2)}, u32[]{:S(2)}) collective-permute-start(bf16[33,128,128]{2,1,0:T(8,128)(2,1)} %collective-permute-done.3.refs_5_), channel_id=1, source_target_pairs={{1,0},{0,1},{3,2},{2,3},{5,4},{4,5},{7,6},{6,7},{9,8},{8,9},{11,10... | collective-permute-start | bytes 3244040 | tf_op jit(solution)/shard_map/ppermute | solution.py:170
  106.8 1.9 collective-permute-start.9
  110.5 10.9 %collective-permute-done.9.refs_10_ = bf16[14,128,128]{2,1,0:T(8,128)(2,1)} collective-permute-done((bf16[14,128,128]{2,1,0:T(8,128)(2,1)}, bf16[14,128,128]{2,1,0:T(8,128)(2,1)}, u32[]{:S(2)}, u32[]{:S(2)}) %collective-permute-start.9) | collective-permute-done | bytes 458784 | tf_op jit(solution)/shard_map/ppermute | solution.py:170
  121.4 1.9 collective-permute-start.12
  123.3 8.1 %collective-permute-start.11 = (bf16[31,128,128]{2,1,0:T(8,128)(2,1)}, bf16[31,128,128]{2,1,0:T(8,128)(2,1)S(1)}, u32[]{:S(2)}, u32[]{:S(2)}) collective-permute-start(bf16[31,128,128]{2,1,0:T(8,128)(2,1)} %collective-permute-done.7.refs_9_), channel_id=1, source_target_pairs={{16,0},{17,1},{18,2},{19,3},{20,4},{21,5},{22,6},{23,7},{24,8},{25... | collective-permute-start | bytes 3047432 | tf_op jit(solution)/shard_map/ppermute | solution.py:170
  131.5 1.9 collective-permute-start.14
  134.8 10.2 %collective-permute-done.12.refs_11_ = bf16[20,128,128]{2,1,0:T(8,128)(2,1)S(1)} collective-permute-done((bf16[20,128,128]{2,1,0:T(8,128)(2,1)}, bf16[20,128,128]{2,1,0:T(8,128)(2,1)S(1)}, u32[]{:S(2)}, u32[]{:S(2)}) %collective-permute-start.12) | collective-permute-done | bytes 655392 | tf_op jit(solution)/shard_map/ppermute | solution.py:170
  145.0 1.9 collective-permute-start.13
  146.9 30.2 %collective-permute-done.14 = bf16[14,128,128]{2,1,0:T(8,128)(2,1)S(1)} collective-permute-done((bf16[14,128,128]{2,1,0:T(8,128)(2,1)}, bf16[14,128,128]{2,1,0:T(8,128)(2,1)S(1)}, u32[]{:S(2)}, u32[]{:S(2)}) %collective-permute-start.14) | collective-permute-done | bytes 458784 | tf_op jit(solution)/shard_map/ppermute | solution.py:170
  177.2 1.9 collective-permute-start.15
  179.1 4.3 %shard_map.55.refs_12_ = f32[16,3,128,128]{3,2,1,0:T(8,128)S(1)} custom-call(s32[1]{0:T(128)} %constant.87.clone.1.refs_0_, s32[16,3]{1,0:T(8,128)S(1)} %bitcast.32, s32[2,32]{1,0:T(2,128)S(1)} %pad_add_fusion.1.refs_2_, s32[2,64]{1,0:T(2,128)S(1)} %pad_add_fusion.2.refs_3_, bf16[33,128,128]{2,1,0:T(8,128)(2,1)S(1)} %fusion.2.refs_4_, ...), custom_call_target="tpu_custom_call" | custom-call | flops 805306368 | bytes 12582912 | tf_op jit(solution)/shard_map/pallas_call | solution.py:95
  183.5 7.8 %collective-permute-done.15.refs_10_ = bf16[14,128,128]{2,1,0:T(8,128)(2,1)S(1)} collective-permute-done((bf16[14,128,128]{2,1,0:T(8,128)(2,1)S(1)}, bf16[14,128,128]{2,1,0:T(8,128)(2,1)S(1)}, u32[]{:S(2)}, u32[]{:S(2)}) %collective-permute-start.15) | collective-permute-done | bytes 458784 | tf_op jit(solution)/shard_map/ppermute | solution.py:170
  191.3 5.9 %shard_map.56 = bf16[16,3,128,128]{3,2,1,0:T(8,128)(2,1)} custom-call(s32[1]{0:T(128)} %bitcast.refs_0_, s32[16,3]{1,0:T(8,128)S(1)} %bitcast.33, s32[2,32]{1,0:T(2,128)S(1)} %pad_add_fusion.refs_2_, s32[2,64]{1,0:T(2,128)S(1)} %maximum_convert_fusion.refs_3_, bf16[33,128,128]{2,1,0:T(8,128)(2,1)} %collective-permute-done.4.refs_4_, ...), custom_call_target="tpu_custom_call" | custom-call | flops 805306368 | bytes 12582912 | tf_op jit(solution)/shard_map/pallas_call | solution.py:95
  (49 shorter events, 9.3 us)
Async XLA Ops:
  1.1 28.8 %collective-permute-start.1 = (bf16[14,128,128]{2,1,0:T(8,128)(2,1)S(1)}, bf16[14,128,128]{2,1,0:T(8,128)(2,1)}, u32[]{:S(2)}, u32[]{:S(2)}) collective-permute-start(bf16[14,128,128]{2,1,0:T(8,128)(2,1)S(1)} %bitcast.28), channel_id=1, source_target_pairs={{128,0},{129,1},{130,2},{131,3},{132,4},{133,5},{134,6},{135,7},{3... | collective-permute-start | bytes 1376264 | tf_op jit(solution)/shard_map/ppermute | solution.py:170
  12.9 5.8 %copy-start.3 = (s32[1,32,2]{1,2,0:T(2,128)S(1)}, s32[1,32,2]{1,2,0:T(2,128)}, u32[]{:S(2)}) copy-start(s32[1,32,2]{1,2,0:T(2,128)} %param.12) | copy-start | bytes 772
  12.9 6.0 %slice-start = ((bf16[1,32,2,128,128]{4,3,2,1,0:T(8,128)(2,1)}), bf16[1,15,2,128,128]{4,3,2,1,0:T(8,128)(2,1)S(1)}, s32[]{:S(2)}) async-start(bf16[1,32,2,128,128]{4,3,2,1,0:T(8,128)(2,1)} %param.11), calls=%async_computation | async-start | bytes 1966080 | tf_op jit(solution)/shard_map/slice | solution.py:181
  14.3 51.6 %collective-permute-start.3 = (bf16[33,128,128]{2,1,0:T(8,128)(2,1)S(1)}, bf16[33,128,128]{2,1,0:T(8,128)(2,1)}, u32[]{:S(2)}, u32[]{:S(2)}) collective-permute-start(bf16[33,128,128]{2,1,0:T(8,128)(2,1)S(1)} %fusion.2.refs_4_), channel_id=1, source_target_pairs={{2,0},{3,1},{4,2},{5,3},{6,4},{7,5},{8,6},{9,7},{10,8},{11,9},{12,... | collective-permute-start | bytes 3244040 | tf_op jit(solution)/shard_map/ppermute | solution.py:170
  16.8 49.1 %collective-permute-start.4 = (bf16[33,128,128]{2,1,0:T(8,128)(2,1)S(1)}, bf16[33,128,128]{2,1,0:T(8,128)(2,1)}, u32[]{:S(2)}, u32[]{:S(2)}) collective-permute-start(bf16[33,128,128]{2,1,0:T(8,128)(2,1)S(1)} %fusion.2.refs_4_), channel_id=1, source_target_pairs={{1,0},{4,1},{3,2},{6,3},{5,4},{8,5},{7,6},{10,7},{9,8},{12,9},{11,... | collective-permute-start | bytes 3244040 | tf_op jit(solution)/shard_map/ppermute | solution.py:170
  19.1 46.8 %collective-permute-start = (bf16[31,128,128]{2,1,0:T(8,128)(2,1)S(1)}, bf16[31,128,128]{2,1,0:T(8,128)(2,1)}, u32[]{:S(2)}, u32[]{:S(2)}) collective-permute-start(bf16[31,128,128]{2,1,0:T(8,128)(2,1)S(1)} %fusion.3.refs_6_), channel_id=1, source_target_pairs={{16,0},{17,1},{18,2},{19,3},{20,4},{21,5},{22,6},{23,7},{24,8},{25... | collective-permute-start | bytes 3047432 | tf_op jit(solution)/shard_map/ppermute | solution.py:170
  27.3 81.4 %copy-start.4 = (s32[16,1,2]{0,2,1:T(2,128)S(1)}, s32[16,1,2]{0,2,1:T(2,128)}, u32[]{:S(2)}) copy-start(s32[16,1,2]{0,2,1:T(2,128)} %param.10) | copy-start | bytes 388
  27.3 81.7 %copy-start.2 = (s32[16,1,3]{0,1,2:T(1,128)S(1)}, s32[16,1,3]{0,1,2:T(1,128)}, u32[]{:S(2)}) copy-start(s32[16,1,3]{0,1,2:T(1,128)} %param.13) | copy-start | bytes 580
  27.3 38.5 %collective-permute-start.5 = (bf16[20,128,128]{2,1,0:T(8,128)(2,1)S(1)}, bf16[20,128,128]{2,1,0:T(8,128)(2,1)}, u32[]{:S(2)}, u32[]{:S(2)}) collective-permute-start(bf16[20,128,128]{2,1,0:T(8,128)(2,1)S(1)} %bitcast.30), channel_id=1, source_target_pairs={{80,0},{81,1},{82,2},{83,3},{84,4},{85,5},{86,6},{87,7},{88,8},{89... | collective-permute-start | bytes 1966088 | tf_op jit(solution)/shard_map/ppermute | solution.py:170
  30.9 34.9 %collective-permute-start.2 = (bf16[14,128,128]{2,1,0:T(8,128)(2,1)S(1)}, bf16[14,128,128]{2,1,0:T(8,128)(2,1)S(1)}, u32[]{:S(2)}, u32[]{:S(2)}) collective-permute-start(bf16[14,128,128]{2,1,0:T(8,128)(2,1)S(1)} %broadcast_select_fusion.2), channel_id=1, source_target_pairs={{16,0},{17,1},{18,2},{19,3},{20,4},{21,5},{22,6},{23,7},{24,8},{25... | collective-permute-start | bytes 1376264 | tf_op jit(solution)/shard_map/ppermute | solution.py:170
  65.9 39.3 %collective-permute-start.8 = (bf16[14,128,128]{2,1,0:T(8,128)(2,1)S(1)}, bf16[14,128,128]{2,1,0:T(8,128)(2,1)S(1)}, u32[]{:S(2)}, u32[]{:S(2)}) collective-permute-start(bf16[14,128,128]{2,1,0:T(8,128)(2,1)S(1)} %collective-permute-done.2.refs_7_), channel_id=1, source_target_pairs={{128,0},{129,1},{130,2},{131,3},{132,4},{133,5},{134,6},{135,7},{3... | collective-permute-start | bytes 1376264 | tf_op jit(solution)/shard_map/ppermute | solution.py:170
  74.1 47.3 %collective-permute-start.7 = (bf16[31,128,128]{2,1,0:T(8,128)(2,1)}, bf16[31,128,128]{2,1,0:T(8,128)(2,1)}, u32[]{:S(2)}, u32[]{:S(2)}) collective-permute-start(bf16[31,128,128]{2,1,0:T(8,128)(2,1)} %collective-permute-done.refs_6_), channel_id=1, source_target_pairs={{16,0},{17,1},{18,2},{19,3},{20,4},{21,5},{22,6},{23,7},{24,8},{25... | collective-permute-start | bytes 3047432 | tf_op jit(solution)/shard_map/ppermute | solution.py:170
  76.0 34.5 %collective-permute-start.10 = (bf16[20,128,128]{2,1,0:T(8,128)(2,1)}, bf16[20,128,128]{2,1,0:T(8,128)(2,1)}, u32[]{:S(2)}, u32[]{:S(2)}) collective-permute-start(bf16[20,128,128]{2,1,0:T(8,128)(2,1)} %collective-permute-done.5), channel_id=1, source_target_pairs={{96,0},{97,1},{98,2},{99,3},{100,4},{101,5},{102,6},{103,7},{104,8... | collective-permute-start | bytes 1966088 | tf_op jit(solution)/shard_map/ppermute | solution.py:170
  78.2 55.9 %collective-permute-start.6 = (bf16[33,128,128]{2,1,0:T(8,128)(2,1)}, bf16[33,128,128]{2,1,0:T(8,128)(2,1)}, u32[]{:S(2)}, u32[]{:S(2)}) collective-permute-start(bf16[33,128,128]{2,1,0:T(8,128)(2,1)} %collective-permute-done.3.refs_5_), channel_id=1, source_target_pairs={{1,0},{0,1},{3,2},{2,3},{5,4},{4,5},{7,6},{6,7},{9,8},{8,9},{11,10... | collective-permute-start | bytes 3244040 | tf_op jit(solution)/shard_map/ppermute | solution.py:170
  106.0 0.8 copy-start
  106.8 14.6 %collective-permute-start.9 = (bf16[14,128,128]{2,1,0:T(8,128)(2,1)}, bf16[14,128,128]{2,1,0:T(8,128)(2,1)}, u32[]{:S(2)}, u32[]{:S(2)}) collective-permute-start(bf16[14,128,128]{2,1,0:T(8,128)(2,1)} %broadcast_select_fusion.1), channel_id=1, source_target_pairs={{16,0},{17,1},{18,2},{19,3},{20,4},{21,5},{22,6},{23,7},{24,8},{25... | collective-permute-start | bytes 1376264 | tf_op jit(solution)/shard_map/ppermute | solution.py:170
  121.4 23.6 %collective-permute-start.12 = (bf16[20,128,128]{2,1,0:T(8,128)(2,1)}, bf16[20,128,128]{2,1,0:T(8,128)(2,1)S(1)}, u32[]{:S(2)}, u32[]{:S(2)}) collective-permute-start(bf16[20,128,128]{2,1,0:T(8,128)(2,1)} %collective-permute-done.10.refs_11_), channel_id=1, source_target_pairs={{496,0},{497,1},{498,2},{499,3},{500,4},{501,5},{502,6},{503,7},{2... | collective-permute-start | bytes 1966088 | tf_op jit(solution)/shard_map/ppermute | solution.py:170
  123.3 60.2 %collective-permute-start.11 = (bf16[31,128,128]{2,1,0:T(8,128)(2,1)}, bf16[31,128,128]{2,1,0:T(8,128)(2,1)S(1)}, u32[]{:S(2)}, u32[]{:S(2)}) collective-permute-start(bf16[31,128,128]{2,1,0:T(8,128)(2,1)} %collective-permute-done.7.refs_9_), channel_id=1, source_target_pairs={{16,0},{17,1},{18,2},{19,3},{20,4},{21,5},{22,6},{23,7},{24,8},{25... | collective-permute-start | bytes 3047432 | tf_op jit(solution)/shard_map/ppermute | solution.py:170
  131.5 45.7 %collective-permute-start.14 = (bf16[14,128,128]{2,1,0:T(8,128)(2,1)}, bf16[14,128,128]{2,1,0:T(8,128)(2,1)S(1)}, u32[]{:S(2)}, u32[]{:S(2)}) collective-permute-start(bf16[14,128,128]{2,1,0:T(8,128)(2,1)} %collective-permute-done.9.refs_10_), channel_id=1, source_target_pairs={{128,0},{129,1},{130,2},{131,3},{132,4},{133,5},{134,6},{135,7},{3... | collective-permute-start | bytes 1376264 | tf_op jit(solution)/shard_map/ppermute | solution.py:170
  145.0 46.3 %collective-permute-start.13 = (bf16[20,128,128]{2,1,0:T(8,128)(2,1)S(1)}, bf16[20,128,128]{2,1,0:T(8,128)(2,1)S(1)}, u32[]{:S(2)}, u32[]{:S(2)}) collective-permute-start(bf16[20,128,128]{2,1,0:T(8,128)(2,1)S(1)} %collective-permute-done.12.refs_11_), channel_id=1, source_target_pairs={{496,0},{497,1},{498,2},{499,3},{500,4},{501,5},{502,6},{503,7},{2... | collective-permute-start | bytes 1966088 | tf_op jit(solution)/shard_map/ppermute | solution.py:170
  177.2 14.1 %collective-permute-start.15 = (bf16[14,128,128]{2,1,0:T(8,128)(2,1)S(1)}, bf16[14,128,128]{2,1,0:T(8,128)(2,1)S(1)}, u32[]{:S(2)}, u32[]{:S(2)}) collective-permute-start(bf16[14,128,128]{2,1,0:T(8,128)(2,1)S(1)} %broadcast_select_fusion), channel_id=1, source_target_pairs={{16,0},{17,1},{18,2},{19,3},{20,4},{21,5},{22,6},{23,7},{24,8},{25... | collective-permute-start | bytes 1376264 | tf_op jit(solution)/shard_map/ppermute | solution.py:170
  179.1 12.2 %copy-start.1 = (bf16[14,128,128]{2,1,0:T(8,128)(2,1)S(1)}, bf16[14,128,128]{2,1,0:T(8,128)(2,1)}, u32[]{:S(2)}) copy-start(bf16[14,128,128]{2,1,0:T(8,128)(2,1)} %copy-done) | copy-start | bytes 1376260

commit v5 on v4

--- a/solution.py
+++ b/solution.py
@@ -11,7 +11,7 @@
 HALF = 16
 RING = 8
 AXES = ("row", "col")
-CUTS = (30, 44)
+CUTS = (32, 46)
 
 
 def block_kernel(first, flip, count, sizes, *refs):
@@ -188,9 +188,7 @@
     up_one = send(rest, paths.up_three)
     most.append(send(most[0], paths.down))
     some.append(inside(some[0]))
-    most[1], some[1], left_two, left_odd, up_one = lax.optimization_barrier(
-        (most[1], some[1], left_two, left_odd, up_one)
-    )
+    most[1], some[1], left_two, up_one = lax.optimization_barrier((most[1], some[1], left_two, up_one))
     third = send(up_one, paths.up_two)
     most.append(send(most[1], paths.down))
     some.append(inside(some[1]))
@@ -199,6 +197,9 @@
     some.append(inside(some[2]))
     second = send(third, paths.up)
     first = send(second, paths.up)
+    most[3], some[3], first, left_odd, left_other = lax.optimization_barrier(
+        (most[3], some[3], first, left_odd, left_other)
+    )
     parts = list(zip(most, some, [rest, first, second, third]))
 
     rows_of = lambda value: indices_of(value, kb.shape[0])

time: 198 us -> 173 us (0.87)
  the two profiles are of different devices: /device:TPU:4 before, /device:TPU:6 now
where the time goes in v5:
time: 173 us; the launch traced here: 172 us
  waiting for transfers between devices  91 us (53%)
  starting transfers between devices  57.4 us (33%)
  Pallas kernels  9.82 us (6%)
  other arithmetic  6.96 us (4%)
  local copies, waits for them, and re-layouts  6.02 us (3%)
    ppermute x16, waiting for transfers between devices, local(): send = lambda value, pairs: lax.ppermute(value, AXES, pairs)  91 us
    ppermute x16, starting transfers between devices, local(): send = lambda value, pairs: lax.ppermute(value, AXES, pairs)  57.4 us
    pallas_call x2, Pallas kernels, contribute(): pl.pallas_call(functools.partial(block_kernel, first, flip is not None, c...  9.82 us
  transfers between devices with their start and end apart: 16, of which 7 were waited for; matrix products, arithmetic and copies ran while one was open for 7% of the time, Pallas kernels for 2%

profile of v5, /device:TPU:6, one launch (start us, length us, event | category | flops | bytes accessed | tf_op | source)
XLA Modules:
  0.0 171.5 jit_solution(6140369453503819688)
XLA Ops:
  1.1 10.9 %collective-permute-start.1 = (bf16[14,128,128]{2,1,0:T(8,128)(2,1)S(1)}, bf16[14,128,128]{2,1,0:T(8,128)(2,1)}, u32[]{:S(2)}, u32[]{:S(2)}) collective-permute-start(bf16[14,128,128]{2,1,0:T(8,128)(2,1)S(1)} %bitcast.28), channel_id=1, source_target_pairs={{128,0},{129,1},{130,2},{131,3},{132,4},{133,5},{134,6},{135,7},{3... | collective-permute-start | bytes 1376264 | tf_op jit(solution)/shard_map/ppermute | solution.py:170
  14.3 2.7 %collective-permute-start.3 = (bf16[33,128,128]{2,1,0:T(8,128)(2,1)S(1)}, bf16[33,128,128]{2,1,0:T(8,128)(2,1)}, u32[]{:S(2)}, u32[]{:S(2)}) collective-permute-start(bf16[33,128,128]{2,1,0:T(8,128)(2,1)S(1)} %fusion.3.refs_4_), channel_id=1, source_target_pairs={{2,0},{3,1},{4,2},{5,3},{6,4},{7,5},{8,6},{9,7},{10,8},{11,9},{12,... | collective-permute-start | bytes 3244040 | tf_op jit(solution)/shard_map/ppermute | solution.py:170
  17.0 2.3 %slice.78 = bf16[1,16,2,128,128]{4,3,2,1,0:T(8,128)(2,1)} slice(bf16[1,32,2,128,128]{4,3,2,1,0:T(8,128)(2,1)} %param.11), slice={[0:1], [0:16], [0:2], [0:128], [0:128]} | slice | bytes 2097152 | tf_op jit(solution)/shard_map/slice | solution.py:181
  20.9 4.3 %collective-permute-start = (bf16[33,128,128]{2,1,0:T(8,128)(2,1)S(1)}, bf16[33,128,128]{2,1,0:T(8,128)(2,1)}, u32[]{:S(2)}, u32[]{:S(2)}) collective-permute-start(bf16[33,128,128]{2,1,0:T(8,128)(2,1)S(1)} %fusion.2.refs_6_), channel_id=1, source_target_pairs={{16,0},{17,1},{18,2},{19,3},{20,4},{21,5},{22,6},{23,7},{24,8},{25... | collective-permute-start | bytes 3244040 | tf_op jit(solution)/shard_map/ppermute | solution.py:170
  26.4 2.5 %collective-permute-start.4 = (bf16[18,128,128]{2,1,0:T(8,128)(2,1)S(1)}, bf16[18,128,128]{2,1,0:T(8,128)(2,1)}, u32[]{:S(2)}, u32[]{:S(2)}) collective-permute-start(bf16[18,128,128]{2,1,0:T(8,128)(2,1)S(1)} %bitcast.30), channel_id=1, source_target_pairs={{80,0},{81,1},{82,2},{83,3},{84,4},{85,5},{86,6},{87,7},{88,8},{89... | collective-permute-start | bytes 1769480 | tf_op jit(solution)/shard_map/ppermute | solution.py:170
  30.0 1.9 %collective-permute-start.2 = (bf16[14,128,128]{2,1,0:T(8,128)(2,1)S(1)}, bf16[14,128,128]{2,1,0:T(8,128)(2,1)S(1)}, u32[]{:S(2)}, u32[]{:S(2)}) collective-permute-start(bf16[14,128,128]{2,1,0:T(8,128)(2,1)S(1)} %broadcast_select_fusion.2), channel_id=1, source_target_pairs={{16,0},{17,1},{18,2},{19,3},{20,4},{21,5},{22,6},{23,7},{24,8},{25... | collective-permute-start | bytes 1376264 | tf_op jit(solution)/shard_map/ppermute | solution.py:170
  31.9 30.5 %collective-permute-done.4 = bf16[18,128,128]{2,1,0:T(8,128)(2,1)} collective-permute-done((bf16[18,128,128]{2,1,0:T(8,128)(2,1)S(1)}, bf16[18,128,128]{2,1,0:T(8,128)(2,1)}, u32[]{:S(2)}, u32[]{:S(2)}) %collective-permute-start.4) | collective-permute-done | bytes 589856 | tf_op jit(solution)/shard_map/ppermute | solution.py:170
  62.5 9.5 %collective-permute-start.6 = (bf16[14,128,128]{2,1,0:T(8,128)(2,1)S(1)}, bf16[14,128,128]{2,1,0:T(8,128)(2,1)S(1)}, u32[]{:S(2)}, u32[]{:S(2)}) collective-permute-start(bf16[14,128,128]{2,1,0:T(8,128)(2,1)S(1)} %collective-permute-done.2.refs_7_), channel_id=1, source_target_pairs={{128,0},{129,1},{130,2},{131,3},{132,4},{133,5},{134,6},{135,7},{3... | collective-permute-start | bytes 1376264 | tf_op jit(solution)/shard_map/ppermute | solution.py:170
  72.0 1.9 %collective-permute-start.5 = (bf16[33,128,128]{2,1,0:T(8,128)(2,1)}, bf16[33,128,128]{2,1,0:T(8,128)(2,1)S(1)}, u32[]{:S(2)}, u32[]{:S(2)}) collective-permute-start(bf16[33,128,128]{2,1,0:T(8,128)(2,1)} %collective-permute-done.refs_6_), channel_id=1, source_target_pairs={{16,0},{17,1},{18,2},{19,3},{20,4},{21,5},{22,6},{23,7},{24,8},{25... | collective-permute-start | bytes 3244040 | tf_op jit(solution)/shard_map/ppermute | solution.py:170
  73.9 1.9 %collective-permute-start.8 = (bf16[18,128,128]{2,1,0:T(8,128)(2,1)}, bf16[18,128,128]{2,1,0:T(8,128)(2,1)}, u32[]{:S(2)}, u32[]{:S(2)}) collective-permute-start(bf16[18,128,128]{2,1,0:T(8,128)(2,1)} %collective-permute-done.4), channel_id=1, source_target_pairs={{96,0},{97,1},{98,2},{99,3},{100,4},{101,5},{102,6},{103,7},{104,8... | collective-permute-start | bytes 1769480 | tf_op jit(solution)/shard_map/ppermute | solution.py:170
  75.8 6.1 %collective-permute-done.6 = bf16[14,128,128]{2,1,0:T(8,128)(2,1)S(1)} collective-permute-done((bf16[14,128,128]{2,1,0:T(8,128)(2,1)S(1)}, bf16[14,128,128]{2,1,0:T(8,128)(2,1)S(1)}, u32[]{:S(2)}, u32[]{:S(2)}) %collective-permute-start.6) | collective-permute-done | bytes 458784 | tf_op jit(solution)/shard_map/ppermute | solution.py:170
  82.0 1.9 %collective-permute-start.7 = (bf16[14,128,128]{2,1,0:T(8,128)(2,1)S(1)}, bf16[14,128,128]{2,1,0:T(8,128)(2,1)}, u32[]{:S(2)}, u32[]{:S(2)}) collective-permute-start(bf16[14,128,128]{2,1,0:T(8,128)(2,1)S(1)} %broadcast_select_fusion.1), channel_id=1, source_target_pairs={{16,0},{17,1},{18,2},{19,3},{20,4},{21,5},{22,6},{23,7},{24,8},{25... | collective-permute-start | bytes 1376264 | tf_op jit(solution)/shard_map/ppermute | solution.py:170
  83.9 20.5 %collective-permute-done.8.refs_11_ = bf16[18,128,128]{2,1,0:T(8,128)(2,1)} collective-permute-done((bf16[18,128,128]{2,1,0:T(8,128)(2,1)}, bf16[18,128,128]{2,1,0:T(8,128)(2,1)}, u32[]{:S(2)}, u32[]{:S(2)}) %collective-permute-start.8) | collective-permute-done | bytes 589856 | tf_op jit(solution)/shard_map/ppermute | solution.py:170
  104.4 5.1 %collective-permute-done.7.refs_10_ = bf16[14,128,128]{2,1,0:T(8,128)(2,1)} collective-permute-done((bf16[14,128,128]{2,1,0:T(8,128)(2,1)S(1)}, bf16[14,128,128]{2,1,0:T(8,128)(2,1)}, u32[]{:S(2)}, u32[]{:S(2)}) %collective-permute-start.7) | collective-permute-done | bytes 458784 | tf_op jit(solution)/shard_map/ppermute | solution.py:170
  111.4 2.2 %collective-permute-start.10 = (bf16[14,128,128]{2,1,0:T(8,128)(2,1)}, bf16[14,128,128]{2,1,0:T(8,128)(2,1)}, u32[]{:S(2)}, u32[]{:S(2)}) collective-permute-start(bf16[14,128,128]{2,1,0:T(8,128)(2,1)} %collective-permute-done.7.refs_10_), channel_id=1, source_target_pairs={{128,0},{129,1},{130,2},{131,3},{132,4},{133,5},{134,6},{135,7},{3... | collective-permute-start | bytes 1376264 | tf_op jit(solution)/shard_map/ppermute | solution.py:170
  113.7 1.9 %collective-permute-start.14 = (bf16[33,128,128]{2,1,0:T(8,128)(2,1)S(1)}, bf16[33,128,128]{2,1,0:T(8,128)(2,1)}, u32[]{:S(2)}, u32[]{:S(2)}) collective-permute-start(bf16[33,128,128]{2,1,0:T(8,128)(2,1)S(1)} %fusion.3.refs_4_), channel_id=1, source_target_pairs={{1,0},{4,1},{3,2},{6,3},{5,4},{8,5},{7,6},{10,7},{9,8},{12,9},{11,... | collective-permute-start | bytes 3244040 | tf_op jit(solution)/shard_map/ppermute | solution.py:170
  116.1 2.5 %collective-permute-start.15 = (bf16[33,128,128]{2,1,0:T(8,128)(2,1)}, bf16[33,128,128]{2,1,0:T(8,128)(2,1)S(1)}, u32[]{:S(2)}, u32[]{:S(2)}) collective-permute-start(bf16[33,128,128]{2,1,0:T(8,128)(2,1)} %collective-permute-done.3.refs_5_), channel_id=1, source_target_pairs={{1,0},{0,1},{3,2},{2,3},{5,4},{4,5},{7,6},{6,7},{9,8},{8,9},{11,10... | collective-permute-start | bytes 3244040 | tf_op jit(solution)/shard_map/ppermute | solution.py:170
  118.6 7.4 %collective-permute-start.9 = (bf16[33,128,128]{2,1,0:T(8,128)(2,1)}, bf16[33,128,128]{2,1,0:T(8,128)(2,1)S(1)}, u32[]{:S(2)}, u32[]{:S(2)}) collective-permute-start(bf16[33,128,128]{2,1,0:T(8,128)(2,1)} %copy-done.2), channel_id=1, source_target_pairs={{16,0},{17,1},{18,2},{19,3},{20,4},{21,5},{22,6},{23,7},{24,8},{25... | collective-permute-start | bytes 3244040 | tf_op jit(solution)/shard_map/ppermute | solution.py:170
  127.3 6.7 %collective-permute-done.12.refs_11_ = bf16[18,128,128]{2,1,0:T(8,128)(2,1)} collective-permute-done((bf16[18,128,128]{2,1,0:T(8,128)(2,1)}, bf16[18,128,128]{2,1,0:T(8,128)(2,1)}, u32[]{:S(2)}, u32[]{:S(2)}) %collective-permute-start.12) | collective-permute-done | bytes 589856 | tf_op jit(solution)/shard_map/ppermute | solution.py:170
  135.9 17.5 %collective-permute-done.10 = bf16[14,128,128]{2,1,0:T(8,128)(2,1)} collective-permute-done((bf16[14,128,128]{2,1,0:T(8,128)(2,1)}, bf16[14,128,128]{2,1,0:T(8,128)(2,1)}, u32[]{:S(2)}, u32[]{:S(2)}) %collective-permute-start.10) | collective-permute-done | bytes 458784 | tf_op jit(solution)/shard_map/ppermute | solution.py:170
  154.5 1.9 %collective-permute-start.11 = (bf16[14,128,128]{2,1,0:T(8,128)(2,1)S(1)}, bf16[14,128,128]{2,1,0:T(8,128)(2,1)S(1)}, u32[]{:S(2)}, u32[]{:S(2)}) collective-permute-start(bf16[14,128,128]{2,1,0:T(8,128)(2,1)S(1)} %broadcast_select_fusion), channel_id=1, source_target_pairs={{16,0},{17,1},{18,2},{19,3},{20,4},{21,5},{22,6},{23,7},{24,8},{25... | collective-permute-start | bytes 1376264 | tf_op jit(solution)/shard_map/ppermute | solution.py:170
  156.5 3.9 %shard_map.55.refs_12_ = f32[16,3,128,128]{3,2,1,0:T(8,128)S(1)} custom-call(s32[1]{0:T(128)} %constant.87.clone.1.refs_0_, s32[16,3]{1,0:T(8,128)S(1)} %bitcast.32, s32[2,32]{1,0:T(2,128)S(1)} %pad_add_fusion.1.refs_2_, s32[2,64]{1,0:T(2,128)S(1)} %pad_add_fusion.2.refs_3_, bf16[33,128,128]{2,1,0:T(8,128)(2,1)S(1)} %fusion.3.refs_4_, ...), custom_call_target="tpu_custom_call" | custom-call | flops 805306368 | bytes 12582912 | tf_op jit(solution)/shard_map/pallas_call | solution.py:95
  160.4 4.5 %collective-permute-done.11.refs_10_ = bf16[14,128,128]{2,1,0:T(8,128)(2,1)S(1)} collective-permute-done((bf16[14,128,128]{2,1,0:T(8,128)(2,1)S(1)}, bf16[14,128,128]{2,1,0:T(8,128)(2,1)S(1)}, u32[]{:S(2)}, u32[]{:S(2)}) %collective-permute-start.11) | collective-permute-done | bytes 458784 | tf_op jit(solution)/shard_map/ppermute | solution.py:170
  165.6 5.9 %shard_map.56 = bf16[16,3,128,128]{3,2,1,0:T(8,128)(2,1)} custom-call(s32[1]{0:T(128)} %bitcast.refs_0_, s32[16,3]{1,0:T(8,128)S(1)} %bitcast.33, s32[2,32]{1,0:T(2,128)S(1)} %pad_add_fusion.refs_2_, s32[2,64]{1,0:T(2,128)S(1)} %maximum_convert_fusion.refs_3_, bf16[33,128,128]{2,1,0:T(8,128)(2,1)} %collective-permute-done.14.refs_4_, ...), custom_call_target="tpu_custom_call" | custom-call | flops 805306368 | bytes 12582912 | tf_op jit(solution)/shard_map/pallas_call | solution.py:95
  (52 shorter events, 14.5 us)
Async XLA Ops:
  1.1 27.8 %collective-permute-start.1 = (bf16[14,128,128]{2,1,0:T(8,128)(2,1)S(1)}, bf16[14,128,128]{2,1,0:T(8,128)(2,1)}, u32[]{:S(2)}, u32[]{:S(2)}) collective-permute-start(bf16[14,128,128]{2,1,0:T(8,128)(2,1)S(1)} %bitcast.28), channel_id=1, source_target_pairs={{128,0},{129,1},{130,2},{131,3},{132,4},{133,5},{134,6},{135,7},{3... | collective-permute-start | bytes 1376264 | tf_op jit(solution)/shard_map/ppermute | solution.py:170
  14.2 5.1 %copy-start.5 = (s32[1,32,2]{1,2,0:T(2,128)S(1)}, s32[1,32,2]{1,2,0:T(2,128)}, u32[]{:S(2)}) copy-start(s32[1,32,2]{1,2,0:T(2,128)} %param.12) | copy-start | bytes 772
  14.3 48.2 %collective-permute-start.3 = (bf16[33,128,128]{2,1,0:T(8,128)(2,1)S(1)}, bf16[33,128,128]{2,1,0:T(8,128)(2,1)}, u32[]{:S(2)}, u32[]{:S(2)}) collective-permute-start(bf16[33,128,128]{2,1,0:T(8,128)(2,1)S(1)} %fusion.3.refs_4_), channel_id=1, source_target_pairs={{2,0},{3,1},{4,2},{5,3},{6,4},{7,5},{8,6},{9,7},{10,8},{11,9},{12,... | collective-permute-start | bytes 3244040 | tf_op jit(solution)/shard_map/ppermute | solution.py:170
  20.9 41.6 %collective-permute-start = (bf16[33,128,128]{2,1,0:T(8,128)(2,1)S(1)}, bf16[33,128,128]{2,1,0:T(8,128)(2,1)}, u32[]{:S(2)}, u32[]{:S(2)}) collective-permute-start(bf16[33,128,128]{2,1,0:T(8,128)(2,1)S(1)} %fusion.2.refs_6_), channel_id=1, source_target_pairs={{16,0},{17,1},{18,2},{19,3},{20,4},{21,5},{22,6},{23,7},{24,8},{25... | collective-permute-start | bytes 3244040 | tf_op jit(solution)/shard_map/ppermute | solution.py:170
  26.4 36.1 %collective-permute-start.4 = (bf16[18,128,128]{2,1,0:T(8,128)(2,1)S(1)}, bf16[18,128,128]{2,1,0:T(8,128)(2,1)}, u32[]{:S(2)}, u32[]{:S(2)}) collective-permute-start(bf16[18,128,128]{2,1,0:T(8,128)(2,1)S(1)} %bitcast.30), channel_id=1, source_target_pairs={{80,0},{81,1},{82,2},{83,3},{84,4},{85,5},{86,6},{87,7},{88,8},{89... | collective-permute-start | bytes 1769480 | tf_op jit(solution)/shard_map/ppermute | solution.py:170
  28.9 86.8 %copy-start.6 = (s32[16,1,2]{0,2,1:T(2,128)S(1)}, s32[16,1,2]{0,2,1:T(2,128)}, u32[]{:S(2)}) copy-start(s32[16,1,2]{0,2,1:T(2,128)} %param.10) | copy-start | bytes 388
  28.9 87.1 %copy-start.4 = (s32[16,1,3]{0,1,2:T(1,128)S(1)}, s32[16,1,3]{0,1,2:T(1,128)}, u32[]{:S(2)}) copy-start(s32[16,1,3]{0,1,2:T(1,128)} %param.13) | copy-start | bytes 580
  30.0 32.5 %collective-permute-start.2 = (bf16[14,128,128]{2,1,0:T(8,128)(2,1)S(1)}, bf16[14,128,128]{2,1,0:T(8,128)(2,1)S(1)}, u32[]{:S(2)}, u32[]{:S(2)}) collective-permute-start(bf16[14,128,128]{2,1,0:T(8,128)(2,1)S(1)} %broadcast_select_fusion.2), channel_id=1, source_target_pairs={{16,0},{17,1},{18,2},{19,3},{20,4},{21,5},{22,6},{23,7},{24,8},{25... | collective-permute-start | bytes 1376264 | tf_op jit(solution)/shard_map/ppermute | solution.py:170
  62.5 49.0 %copy-start = (bf16[14,128,128]{2,1,0:T(8,128)(2,1)}, bf16[14,128,128]{2,1,0:T(8,128)(2,1)S(1)}, u32[]{:S(2)}) copy-start(bf16[14,128,128]{2,1,0:T(8,128)(2,1)S(1)} %collective-permute-done.2.refs_7_) | copy-start | bytes 1376260
  62.5 19.4 %collective-permute-start.6 = (bf16[14,128,128]{2,1,0:T(8,128)(2,1)S(1)}, bf16[14,128,128]{2,1,0:T(8,128)(2,1)S(1)}, u32[]{:S(2)}, u32[]{:S(2)}) collective-permute-start(bf16[14,128,128]{2,1,0:T(8,128)(2,1)S(1)} %collective-permute-done.2.refs_7_), channel_id=1, source_target_pairs={{128,0},{129,1},{130,2},{131,3},{132,4},{133,5},{134,6},{135,7},{3... | collective-permute-start | bytes 1376264 | tf_op jit(solution)/shard_map/ppermute | solution.py:170
  72.0 37.5 %collective-permute-start.5 = (bf16[33,128,128]{2,1,0:T(8,128)(2,1)}, bf16[33,128,128]{2,1,0:T(8,128)(2,1)S(1)}, u32[]{:S(2)}, u32[]{:S(2)}) collective-permute-start(bf16[33,128,128]{2,1,0:T(8,128)(2,1)} %collective-permute-done.refs_6_), channel_id=1, source_target_pairs={{16,0},{17,1},{18,2},{19,3},{20,4},{21,5},{22,6},{23,7},{24,8},{25... | collective-permute-start | bytes 3244040 | tf_op jit(solution)/shard_map/ppermute | solution.py:170
  73.9 30.5 %collective-permute-start.8 = (bf16[18,128,128]{2,1,0:T(8,128)(2,1)}, bf16[18,128,128]{2,1,0:T(8,128)(2,1)}, u32[]{:S(2)}, u32[]{:S(2)}) collective-permute-start(bf16[18,128,128]{2,1,0:T(8,128)(2,1)} %collective-permute-done.4), channel_id=1, source_target_pairs={{96,0},{97,1},{98,2},{99,3},{100,4},{101,5},{102,6},{103,7},{104,8... | collective-permute-start | bytes 1769480 | tf_op jit(solution)/shard_map/ppermute | solution.py:170
  82.0 27.6 %collective-permute-start.7 = (bf16[14,128,128]{2,1,0:T(8,128)(2,1)S(1)}, bf16[14,128,128]{2,1,0:T(8,128)(2,1)}, u32[]{:S(2)}, u32[]{:S(2)}) collective-permute-start(bf16[14,128,128]{2,1,0:T(8,128)(2,1)S(1)} %broadcast_select_fusion.1), channel_id=1, source_target_pairs={{16,0},{17,1},{18,2},{19,3},{20,4},{21,5},{22,6},{23,7},{24,8},{25... | collective-permute-start | bytes 1376264 | tf_op jit(solution)/shard_map/ppermute | solution.py:170
  109.5 4.1 %copy-start.2 = (bf16[33,128,128]{2,1,0:T(8,128)(2,1)}, bf16[33,128,128]{2,1,0:T(8,128)(2,1)S(1)}, u32[]{:S(2)}) copy-start(bf16[33,128,128]{2,1,0:T(8,128)(2,1)S(1)} %collective-permute-done.5.refs_9_) | copy-start | bytes 3244036
  109.5 24.5 %collective-permute-start.12 = (bf16[18,128,128]{2,1,0:T(8,128)(2,1)}, bf16[18,128,128]{2,1,0:T(8,128)(2,1)}, u32[]{:S(2)}, u32[]{:S(2)}) collective-permute-start(bf16[18,128,128]{2,1,0:T(8,128)(2,1)} %collective-permute-done.8.refs_11_), channel_id=1, source_target_pairs={{496,0},{497,1},{498,2},{499,3},{500,4},{501,5},{502,6},{503,7},{2... | collective-permute-start | bytes 1769480 | tf_op jit(solution)/shard_map/ppermute | solution.py:170
  111.4 42.0 %collective-permute-start.10 = (bf16[14,128,128]{2,1,0:T(8,128)(2,1)}, bf16[14,128,128]{2,1,0:T(8,128)(2,1)}, u32[]{:S(2)}, u32[]{:S(2)}) collective-permute-start(bf16[14,128,128]{2,1,0:T(8,128)(2,1)} %collective-permute-done.7.refs_10_), channel_id=1, source_target_pairs={{128,0},{129,1},{130,2},{131,3},{132,4},{133,5},{134,6},{135,7},{3... | collective-permute-start | bytes 1376264 | tf_op jit(solution)/shard_map/ppermute | solution.py:170
  113.7 46.7 %collective-permute-start.14 = (bf16[33,128,128]{2,1,0:T(8,128)(2,1)S(1)}, bf16[33,128,128]{2,1,0:T(8,128)(2,1)}, u32[]{:S(2)}, u32[]{:S(2)}) collective-permute-start(bf16[33,128,128]{2,1,0:T(8,128)(2,1)S(1)} %fusion.3.refs_4_), channel_id=1, source_target_pairs={{1,0},{4,1},{3,2},{6,3},{5,4},{8,5},{7,6},{10,7},{9,8},{12,9},{11,... | collective-permute-start | bytes 3244040 | tf_op jit(solution)/shard_map/ppermute | solution.py:170
  116.1 40.4 %copy-start.3 = (bf16[33,128,128]{2,1,0:T(8,128)(2,1)S(1)}, bf16[33,128,128]{2,1,0:T(8,128)(2,1)}, u32[]{:S(2)}) copy-start(bf16[33,128,128]{2,1,0:T(8,128)(2,1)} %copy-done.2) | copy-start | bytes 3244036
  116.1 44.3 %collective-permute-start.15 = (bf16[33,128,128]{2,1,0:T(8,128)(2,1)}, bf16[33,128,128]{2,1,0:T(8,128)(2,1)S(1)}, u32[]{:S(2)}, u32[]{:S(2)}) collective-permute-start(bf16[33,128,128]{2,1,0:T(8,128)(2,1)} %collective-permute-done.3.refs_5_), channel_id=1, source_target_pairs={{1,0},{0,1},{3,2},{2,3},{5,4},{4,5},{7,6},{6,7},{9,8},{8,9},{11,10... | collective-permute-start | bytes 3244040 | tf_op jit(solution)/shard_map/ppermute | solution.py:170
  118.6 46.3 %collective-permute-start.9 = (bf16[33,128,128]{2,1,0:T(8,128)(2,1)}, bf16[33,128,128]{2,1,0:T(8,128)(2,1)S(1)}, u32[]{:S(2)}, u32[]{:S(2)}) collective-permute-start(bf16[33,128,128]{2,1,0:T(8,128)(2,1)} %copy-done.2), channel_id=1, source_target_pairs={{16,0},{17,1},{18,2},{19,3},{20,4},{21,5},{22,6},{23,7},{24,8},{25... | collective-permute-start | bytes 3244040 | tf_op jit(solution)/shard_map/ppermute | solution.py:170
  134.0 30.9 %collective-permute-start.13 = (bf16[18,128,128]{2,1,0:T(8,128)(2,1)}, bf16[18,128,128]{2,1,0:T(8,128)(2,1)S(1)}, u32[]{:S(2)}, u32[]{:S(2)}) collective-permute-start(bf16[18,128,128]{2,1,0:T(8,128)(2,1)} %collective-permute-done.12.refs_11_), channel_id=1, source_target_pairs={{496,0},{497,1},{498,2},{499,3},{500,4},{501,5},{502,6},{503,7},{2... | collective-permute-start | bytes 1769480 | tf_op jit(solution)/shard_map/ppermute | solution.py:170
  154.5 10.4 %collective-permute-start.11 = (bf16[14,128,128]{2,1,0:T(8,128)(2,1)S(1)}, bf16[14,128,128]{2,1,0:T(8,128)(2,1)S(1)}, u32[]{:S(2)}, u32[]{:S(2)}) collective-permute-start(bf16[14,128,128]{2,1,0:T(8,128)(2,1)S(1)} %broadcast_select_fusion), channel_id=1, source_target_pairs={{16,0},{17,1},{18,2},{19,3},{20,4},{21,5},{22,6},{23,7},{24,8},{25... | collective-permute-start | bytes 1376264 | tf_op jit(solution)/shard_map/ppermute | solution.py:170
  156.5 9.1 %copy-start.1 = (bf16[14,128,128]{2,1,0:T(8,128)(2,1)S(1)}, bf16[14,128,128]{2,1,0:T(8,128)(2,1)}, u32[]{:S(2)}) copy-start(bf16[14,128,128]{2,1,0:T(8,128)(2,1)} %copy-done) | copy-start | bytes 1376260

commit v6 on v5

--- a/solution.py
+++ b/solution.py
@@ -15,12 +15,13 @@
 
 
 def block_kernel(first, flip, count, sizes, *refs):
-    flip_ref, cols, ka, kb, *rest = refs
+    flip_ref, cols, *rest = refs
+    kas, kbs, rest = rest[:2], rest[2:4], rest[4:]
     lefts, rest = rest[:2], rest[2:]
     parts, rest = rest[: 2 * len(sizes)], rest[2 * len(sizes) :]
     total = None if first else rest[0]
     out, made_so_far, a, held, a_sems, sems = rest[-6:]
-    rows, kept = cols.shape
+    kept, rows = cols.shape
     span = count + 1
 
     def left_copy(n, slot):
@@ -59,16 +60,16 @@
         for copy in copies[slot]:
             copy.wait()
 
-        @pl.loop(0, rows, unroll=4)
+        @pl.loop(0, rows, unroll=8)
         def _(i):
             left = jnp.concatenate([a[slot, 2 * i], a[slot, 2 * i + 1]], axis=1)
             right = []
             for o in range(kept):
-                j = cols[i, o]
-                low, high = kb[slot, 2 * j], kb[slot, 2 * j + 1]
+                j = cols[o, i]
+                low, high = kbs[slot][0, j], kbs[slot][1, j]
                 column = []
                 for k in range(2):
-                    want = ka[slot, 2 * i + k]
+                    want = kas[slot][k, i]
                     place = jnp.where(low == want, 2 * j, jnp.where(high == want, 2 * j + 1, count))
                     column.append(held[slot * span + place])
                 right.append(jnp.concatenate(column, axis=0))
@@ -83,7 +84,7 @@
 
 
 def contribute(total, flip, cols, ka, kb, lefts, parts, sizes, last):
-    rows, kept = cols.shape
+    kept, rows = cols.shape
     block = lefts[0].shape[1:]
     count = sum(sizes)
     first = total is None
@@ -95,7 +96,7 @@
     return pl.pallas_call(
         functools.partial(block_kernel, first, flip is not None, count, sizes),
         out_shape=jax.ShapeDtypeStruct(tall, jnp.bfloat16 if last else jnp.float32),
-        in_specs=[smem] * 4 + [whole] * (2 + len(flat)) + ([] if first else [vmem]),
+        in_specs=[smem] * 6 + [whole] * (2 + len(flat)) + ([] if first else [vmem]),
         out_specs=vmem,
         scratch_shapes=[
             pltpu.VMEM(tall, jnp.float32),
@@ -111,8 +112,8 @@
     )(
         jnp.zeros((1,), jnp.int32) if flip is None else flip,
         cols,
-        jnp.stack(ka),
-        jnp.stack(kb),
+        *ka,
+        *kb,
         *lefts,
         *flat,
         *(() if first else (total,)),
@@ -120,13 +121,13 @@
 
 
 def with_indices(blocks, indices):
-    flat = indices.reshape(-1).astype(blocks.dtype)
-    extra = jnp.zeros((1,) + blocks.shape[1:], blocks.dtype).at[0, 0, : flat.shape[0]].set(flat)
-    return jnp.concatenate([blocks, extra], axis=0)
-
-
-def indices_of(blocks, count):
-    return blocks[-1, 0, :count].astype(jnp.int32)
+    low, high = (blocks.shape[n] - indices.shape[n - 1] for n in (1, 2))
+    extra = jnp.pad(indices.astype(blocks.dtype), ((0, low), (0, high)))
+    return jnp.concatenate([blocks, extra[None]], axis=0)
+
+
+def indices_of(blocks, shape):
+    return blocks[-1, : shape[0], : shape[1]].astype(jnp.int32)
 
 
 class Paths:
@@ -135,8 +136,9 @@
         self.down = self.pairs(lambda z, y, t: (z + t * (y == RING - 1), y + 1))
         self.ring = self.pairs(lambda z, y, t: (z, y + 1))
         self.enter = self.pairs(lambda z, y, t: (z + t, y), only=0)
-        self.up_three = self.pairs(lambda z, y, t: (z + t * (3 <= y <= 5), y - 3))
         self.up_two = self.pairs(lambda z, y, t: (z, y - 2))
+        self.up_turn = self.pairs(lambda z, y, t: (z + t * (4 <= y < RING - 1), y - 2))
+        self.up_in = self.pairs(lambda z, y, t: (z, y - 1))
         self.up = self.pairs(lambda z, y, t: (z - t * (y == 0), y - 1))
         self.side_two = self.over_columns(lambda col: col + 2)
         self.side_odd = self.over_columns(lambda col: col + (3 if col % 2 else 1))
@@ -162,8 +164,8 @@
 
 
 def local(paths, a_blocks, a_cols, b_blocks, b_rows, out_cols):
-    cols = out_cols[:, 0]
-    ka, kb = a_cols[:, 0].reshape(-1), b_rows[0].reshape(-1)
+    cols = out_cols[:, 0].T
+    ka, kb = a_cols[:, 0].T, b_rows[0].T
     block = b_blocks.shape[3:]
     own = b_blocks[0].reshape((-1,) + block)
     count = own.shape[0]
@@ -185,31 +187,29 @@
     def inside(value):
         return send(jnp.where(at_edge, send(value, paths.enter), value), paths.ring)
 
-    up_one = send(rest, paths.up_three)
+    up_one = send(rest, paths.up_two)
     most.append(send(most[0], paths.down))
     some.append(inside(some[0]))
     most[1], some[1], left_two, up_one = lax.optimization_barrier((most[1], some[1], left_two, up_one))
-    third = send(up_one, paths.up_two)
+    up_two = send(up_one, paths.up_turn)
+    third = send(up_two, paths.up_in)
     most.append(send(most[1], paths.down))
     some.append(inside(some[1]))
-    most[2], some[2], third = lax.optimization_barrier((most[2], some[2], third))
+    most[2], some[2], _ = lax.optimization_barrier((most[2], some[2], up_two))
     most.append(send(most[2], paths.down))
     some.append(inside(some[2]))
     second = send(third, paths.up)
     first = send(second, paths.up)
-    most[3], some[3], first, left_odd, left_other = lax.optimization_barrier(
-        (most[3], some[3], first, left_odd, left_other)
-    )
     parts = list(zip(most, some, [rest, first, second, third]))
 
-    rows_of = lambda value: indices_of(value, kb.shape[0])
-    ka_odd, ka_other = indices_of(left_odd, ka.shape[0]), indices_of(left_other, ka.shape[0])
+    rows_of = lambda value: indices_of(value, kb.shape)
+    ka_odd, ka_other = indices_of(left_odd, ka.shape), indices_of(left_other, ka.shape)
     ka_one, ka_three = jnp.where(odd == 0, ka_odd, ka_other), jnp.where(odd == 0, ka_other, ka_odd)
     total = contribute(
         None,
         None,
         cols,
-        [ka, indices_of(left_two, ka.shape[0])],
+        [ka, indices_of(left_two, ka.shape)],
         [kb, rows_of(most[2])],
         [left, left_two],
         [parts[0], parts[2]],

time: 173 us -> 159 us (0.919)
  waiting for transfers between devices: 91 us -> 64 us
  starting transfers between devices: 57.4 us -> 75.9 us
  local copies, waits for them, and re-layouts: 6.02 us -> 1.91 us
    ppermute x16 -> x17, waiting for transfers between devices: 91 us -> 64 us  [local(): send = lambda value, pairs: lax.ppermute(value, AXES, pairs)]
    ppermute x16 -> x17, starting transfers between devices: 57.4 us -> 75.9 us  [local(): send = lambda value, pairs: lax.ppermute(value, AXES, pairs)]
    slice x1 -> x2, local copies, waits for them, and re-layouts: 2.31 us -> 0.01 us  [local(): most = [with_indices(own[:cut], kb)]]
  transfers between devices with their start and end apart: 16 -> 17, of which waited for: 7 -> 6; matrix products, arithmetic and copies ran while one was open for 7% -> 4% of each run, Pallas kernels for 2% -> 2%
where the time goes in v6:
time: 159 us; the launch traced here: 158 us
  starting transfers between devices  75.9 us (48%)
  waiting for transfers between devices  64 us (40%)
  Pallas kernels  8.74 us (5%)
  other arithmetic  6.81 us (4%)
  local copies, waits for them, and re-layouts  1.91 us (1%)
    ppermute x17, starting transfers between devices, local(): send = lambda value, pairs: lax.ppermute(value, AXES, pairs)  75.9 us
    ppermute x17, waiting for transfers between devices, local(): send = lambda value, pairs: lax.ppermute(value, AXES, pairs)  64 us
    pallas_call x2, Pallas kernels, contribute(): pl.pallas_call(functools.partial(block_kernel, first, flip is not None, c...  8.74 us
  transfers between devices with their start and end apart: 17, of which 6 were waited for; matrix products, arithmetic and copies ran while one was open for 4% of the time, Pallas kernels for 2%

profile of v6, /device:TPU:6, one launch (start us, length us, event | category | flops | bytes accessed | tf_op | source)
XLA Modules:
  0.0 157.7 jit_solution(15141652151961453220)
XLA Ops:
  1.1 10.9 %collective-permute-start.4 = (bf16[14,128,128]{2,1,0:T(8,128)(2,1)S(1)}, bf16[14,128,128]{2,1,0:T(8,128)(2,1)}, u32[]{:S(2)}, u32[]{:S(2)}) collective-permute-start(bf16[14,128,128]{2,1,0:T(8,128)(2,1)S(1)} %bitcast.44), channel_id=1, source_target_pairs={{128,0},{129,1},{130,2},{131,3},{132,4},{133,5},{134,6},{135,7},{3... | collective-permute-start | bytes 1376264 | tf_op jit(solution)/shard_map/ppermute | solution.py:172
  14.0 2.9 %collective-permute-start.1 = (bf16[33,128,128]{2,1,0:T(8,128)(2,1)S(1)}, bf16[33,128,128]{2,1,0:T(8,128)(2,1)}, u32[]{:S(2)}, u32[]{:S(2)}) collective-permute-start(bf16[33,128,128]{2,1,0:T(8,128)(2,1)S(1)} %pad_maximum_fusion.refs_6_), channel_id=1, source_target_pairs={{2,0},{3,1},{4,2},{5,3},{6,4},{7,5},{8,6},{9,7},{10,8},{11,9},{12,... | collective-permute-start | bytes 3244040 | tf_op jit(solution)/shard_map/ppermute | solution.py:172
  17.1 4.5 %collective-permute-start.3 = (bf16[33,128,128]{2,1,0:T(8,128)(2,1)S(1)}, bf16[33,128,128]{2,1,0:T(8,128)(2,1)}, u32[]{:S(2)}, u32[]{:S(2)}) collective-permute-start(bf16[33,128,128]{2,1,0:T(8,128)(2,1)S(1)} %pad_maximum_fusion.1.refs_8_), channel_id=1, source_target_pairs={{16,0},{17,1},{18,2},{19,3},{20,4},{21,5},{22,6},{23,7},{24,8},{25... | collective-permute-start | bytes 3244040 | tf_op jit(solution)/shard_map/ppermute | solution.py:172
  21.6 1.9 %collective-permute-start.6 = (bf16[18,128,128]{2,1,0:T(8,128)(2,1)S(1)}, bf16[18,128,128]{2,1,0:T(8,128)(2,1)}, u32[]{:S(2)}, u32[]{:S(2)}) collective-permute-start(bf16[18,128,128]{2,1,0:T(8,128)(2,1)S(1)} %bitcast.46), channel_id=1, source_target_pairs={{96,0},{97,1},{98,2},{99,3},{100,4},{101,5},{102,6},{103,7},{104,8... | collective-permute-start | bytes 1769480 | tf_op jit(solution)/shard_map/ppermute | solution.py:172
  24.7 3.2 %collective-permute-start.5 = (bf16[14,128,128]{2,1,0:T(8,128)(2,1)S(1)}, bf16[14,128,128]{2,1,0:T(8,128)(2,1)S(1)}, u32[]{:S(2)}, u32[]{:S(2)}) collective-permute-start(bf16[14,128,128]{2,1,0:T(8,128)(2,1)S(1)} %broadcast_select_fusion.2), channel_id=1, source_target_pairs={{16,0},{17,1},{18,2},{19,3},{20,4},{21,5},{22,6},{23,7},{24,8},{25... | collective-permute-start | bytes 1376264 | tf_op jit(solution)/shard_map/ppermute | solution.py:172
  27.9 23.8 %collective-permute-done.6 = bf16[18,128,128]{2,1,0:T(8,128)(2,1)} collective-permute-done((bf16[18,128,128]{2,1,0:T(8,128)(2,1)S(1)}, bf16[18,128,128]{2,1,0:T(8,128)(2,1)}, u32[]{:S(2)}, u32[]{:S(2)}) %collective-permute-start.6) | collective-permute-done | bytes 589856 | tf_op jit(solution)/shard_map/ppermute | solution.py:172
  51.7 2.5 %collective-permute-done.5.refs_9_ = bf16[14,128,128]{2,1,0:T(8,128)(2,1)S(1)} collective-permute-done((bf16[14,128,128]{2,1,0:T(8,128)(2,1)S(1)}, bf16[14,128,128]{2,1,0:T(8,128)(2,1)S(1)}, u32[]{:S(2)}, u32[]{:S(2)}) %collective-permute-start.5) | collective-permute-done | bytes 458784 | tf_op jit(solution)/shard_map/ppermute | solution.py:172
  54.2 1.9 %collective-permute-start.10 = (bf16[18,128,128]{2,1,0:T(8,128)(2,1)}, bf16[18,128,128]{2,1,0:T(8,128)(2,1)}, u32[]{:S(2)}, u32[]{:S(2)}) collective-permute-start(bf16[18,128,128]{2,1,0:T(8,128)(2,1)} %collective-permute-done.6), channel_id=1, source_target_pairs={{96,0},{97,1},{98,2},{99,3},{100,4},{101,5},{102,6},{103,7},{104,8... | collective-permute-start | bytes 1769480 | tf_op jit(solution)/shard_map/ppermute | solution.py:172
  56.1 4.1 %collective-permute-start.8 = (bf16[14,128,128]{2,1,0:T(8,128)(2,1)S(1)}, bf16[14,128,128]{2,1,0:T(8,128)(2,1)S(1)}, u32[]{:S(2)}, u32[]{:S(2)}) collective-permute-start(bf16[14,128,128]{2,1,0:T(8,128)(2,1)S(1)} %collective-permute-done.5.refs_9_), channel_id=1, source_target_pairs={{128,0},{129,1},{130,2},{131,3},{132,4},{133,5},{134,6},{135,7},{3... | collective-permute-start | bytes 1376264 | tf_op jit(solution)/shard_map/ppermute | solution.py:172
  60.2 13.8 %collective-permute-start.7 = (bf16[33,128,128]{2,1,0:T(8,128)(2,1)}, bf16[33,128,128]{2,1,0:T(8,128)(2,1)}, u32[]{:S(2)}, u32[]{:S(2)}) collective-permute-start(bf16[33,128,128]{2,1,0:T(8,128)(2,1)} %collective-permute-done.3.refs_8_), channel_id=1, source_target_pairs={{16,0},{17,1},{18,2},{19,3},{20,4},{21,5},{22,6},{23,7},{24,8},{25... | collective-permute-start | bytes 3244040 | tf_op jit(solution)/shard_map/ppermute | solution.py:172
  74.0 1.9 %collective-permute-start = (bf16[33,128,128]{2,1,0:T(8,128)(2,1)S(1)}, bf16[33,128,128]{2,1,0:T(8,128)(2,1)}, u32[]{:S(2)}, u32[]{:S(2)}) collective-permute-start(bf16[33,128,128]{2,1,0:T(8,128)(2,1)S(1)} %pad_maximum_fusion.refs_6_), channel_id=1, source_target_pairs={{1,0},{4,1},{3,2},{6,3},{5,4},{8,5},{7,6},{10,7},{9,8},{12,9},{11,... | collective-permute-start | bytes 3244040 | tf_op jit(solution)/shard_map/ppermute | solution.py:172
  76.0 2.4 %collective-permute-start.2 = (bf16[33,128,128]{2,1,0:T(8,128)(2,1)}, bf16[33,128,128]{2,1,0:T(8,128)(2,1)}, u32[]{:S(2)}, u32[]{:S(2)}) collective-permute-start(bf16[33,128,128]{2,1,0:T(8,128)(2,1)} %collective-permute-done.1.refs_7_), channel_id=1, source_target_pairs={{1,0},{0,1},{3,2},{2,3},{5,4},{4,5},{7,6},{6,7},{9,8},{8,9},{11,10... | collective-permute-start | bytes 3244040 | tf_op jit(solution)/shard_map/ppermute | solution.py:172
  78.4 10.0 %collective-permute-start.12 = (bf16[18,128,128]{2,1,0:T(8,128)(2,1)}, bf16[18,128,128]{2,1,0:T(8,128)(2,1)}, u32[]{:S(2)}, u32[]{:S(2)}) collective-permute-start(bf16[18,128,128]{2,1,0:T(8,128)(2,1)} %collective-permute-done.10), channel_id=1, source_target_pairs={{112,0},{113,1},{114,2},{115,3},{116,4},{117,5},{118,6},{119,7},{1... | collective-permute-start | bytes 1769480 | tf_op jit(solution)/shard_map/ppermute | solution.py:172
  90.0 3.4 %collective-permute-start.9 = (bf16[14,128,128]{2,1,0:T(8,128)(2,1)}, bf16[14,128,128]{2,1,0:T(8,128)(2,1)}, u32[]{:S(2)}, u32[]{:S(2)}) collective-permute-start(bf16[14,128,128]{2,1,0:T(8,128)(2,1)} %broadcast_select_fusion.1), channel_id=1, source_target_pairs={{16,0},{17,1},{18,2},{19,3},{20,4},{21,5},{22,6},{23,7},{24,8},{25... | collective-permute-start | bytes 1376264 | tf_op jit(solution)/shard_map/ppermute | solution.py:172
  93.4 13.0 %collective-permute-done.9.refs_12_ = bf16[14,128,128]{2,1,0:T(8,128)(2,1)} collective-permute-done((bf16[14,128,128]{2,1,0:T(8,128)(2,1)}, bf16[14,128,128]{2,1,0:T(8,128)(2,1)}, u32[]{:S(2)}, u32[]{:S(2)}) %collective-permute-start.9) | collective-permute-done | bytes 458784 | tf_op jit(solution)/shard_map/ppermute | solution.py:172
  106.4 2.4 %collective-permute-start.15 = (bf16[14,128,128]{2,1,0:T(8,128)(2,1)}, bf16[14,128,128]{2,1,0:T(8,128)(2,1)S(1)}, u32[]{:S(2)}, u32[]{:S(2)}) collective-permute-start(bf16[14,128,128]{2,1,0:T(8,128)(2,1)} %collective-permute-done.9.refs_12_), channel_id=1, source_target_pairs={{128,0},{129,1},{130,2},{131,3},{132,4},{133,5},{134,6},{135,7},{3... | collective-permute-start | bytes 1376264 | tf_op jit(solution)/shard_map/ppermute | solution.py:172
  108.8 3.8 %collective-permute-start.11 = (bf16[33,128,128]{2,1,0:T(8,128)(2,1)}, bf16[33,128,128]{2,1,0:T(8,128)(2,1)S(1)}, u32[]{:S(2)}, u32[]{:S(2)}) collective-permute-start(bf16[33,128,128]{2,1,0:T(8,128)(2,1)} %collective-permute-done.7.refs_11_), channel_id=1, source_target_pairs={{16,0},{17,1},{18,2},{19,3},{20,4},{21,5},{22,6},{23,7},{24,8},{25... | collective-permute-start | bytes 3244040 | tf_op jit(solution)/shard_map/ppermute | solution.py:172
  112.7 2.0 %collective-permute-start.13 = (bf16[18,128,128]{2,1,0:T(8,128)(2,1)}, bf16[18,128,128]{2,1,0:T(8,128)(2,1)S(1)}, u32[]{:S(2)}, u32[]{:S(2)}) collective-permute-start(bf16[18,128,128]{2,1,0:T(8,128)(2,1)} %collective-permute-done.12.refs_13_), channel_id=1, source_target_pairs={{496,0},{497,1},{498,2},{499,3},{500,4},{501,5},{502,6},{503,7},{2... | collective-permute-start | bytes 1769480 | tf_op jit(solution)/shard_map/ppermute | solution.py:172
  116.8 17.3 %collective-permute-done.13.refs_13_ = bf16[18,128,128]{2,1,0:T(8,128)(2,1)S(1)} collective-permute-done((bf16[18,128,128]{2,1,0:T(8,128)(2,1)}, bf16[18,128,128]{2,1,0:T(8,128)(2,1)S(1)}, u32[]{:S(2)}, u32[]{:S(2)}) %collective-permute-start.13) | collective-permute-done | bytes 589856 | tf_op jit(solution)/shard_map/ppermute | solution.py:172
  136.1 4.8 %collective-permute-start.16 = (bf16[14,128,128]{2,1,0:T(8,128)(2,1)S(1)}, bf16[14,128,128]{2,1,0:T(8,128)(2,1)S(1)}, u32[]{:S(2)}, u32[]{:S(2)}) collective-permute-start(bf16[14,128,128]{2,1,0:T(8,128)(2,1)S(1)} %broadcast_select_fusion), channel_id=1, source_target_pairs={{16,0},{17,1},{18,2},{19,3},{20,4},{21,5},{22,6},{23,7},{24,8},{25... | collective-permute-start | bytes 1376264 | tf_op jit(solution)/shard_map/ppermute | solution.py:172
  141.6 3.5 %shard_map.55.refs_14_ = f32[16,3,128,128]{3,2,1,0:T(8,128)S(1)} custom-call(s32[1]{0:T(128)} %constant.36.clone.1.refs_0_, s32[3,16]{1,0:T(4,128)S(1)} %bitcast.48, s32[2,16]{1,0:T(2,128)S(1)} %bitcast.50, s32[2,16]{1,0:T(2,128)S(1)} %bitcast_convert_fusion.1.refs_3_, s32[2,32]{1,0:T(2,128)S(1)} %bitcast.51, s32[2,32]{1,0:T(2,128)S(1)} %bitcast_convert_fusion.refs_5_, ...), custom_call_target="tpu_custom_call" | custom-call | flops 805306368 | bytes 12582912 | tf_op jit(solution)/shard_map/pallas_call | solution.py:96
  145.1 2.3 %collective-permute-done.16.refs_12_ = bf16[14,128,128]{2,1,0:T(8,128)(2,1)S(1)} collective-permute-done((bf16[14,128,128]{2,1,0:T(8,128)(2,1)S(1)}, bf16[14,128,128]{2,1,0:T(8,128)(2,1)S(1)}, u32[]{:S(2)}, u32[]{:S(2)}) %collective-permute-start.16) | collective-permute-done | bytes 458784 | tf_op jit(solution)/shard_map/ppermute | solution.py:172
  147.5 5.0 %collective-permute-done.14.refs_10_ = bf16[18,128,128]{2,1,0:T(8,128)(2,1)S(1)} collective-permute-done((bf16[18,128,128]{2,1,0:T(8,128)(2,1)S(1)}, bf16[18,128,128]{2,1,0:T(8,128)(2,1)S(1)}, u32[]{:S(2)}, u32[]{:S(2)}) %collective-permute-start.14) | collective-permute-done | bytes 589856 | tf_op jit(solution)/shard_map/ppermute | solution.py:172
  152.5 5.2 %shard_map.56 = bf16[16,3,128,128]{3,2,1,0:T(8,128)(2,1)} custom-call(s32[1]{0:T(128)} %bitcast.refs_0_, s32[3,16]{1,0:T(4,128)S(1)} %bitcast.49, s32[2,16]{1,0:T(2,128)S(1)} %get-tuple-element.18.refs_2_, s32[2,16]{1,0:T(2,128)S(1)} %get-tuple-element.17.refs_3_, s32[2,32]{1,0:T(2,128)S(1)} %bitcast_convert_fusion.2.refs_4_, s32[2,32]{1,0:T(2,128)S(1)} %fusion.2.refs_5_, ...), custom_call_target="tpu_custom_call" | custom-call | flops 805306368 | bytes 12582912 | tf_op jit(solution)/shard_map/pallas_call | solution.py:96
  (43 shorter events, 10.7 us)
Async XLA Ops:
  1.1 22.5 %collective-permute-start.4 = (bf16[14,128,128]{2,1,0:T(8,128)(2,1)S(1)}, bf16[14,128,128]{2,1,0:T(8,128)(2,1)}, u32[]{:S(2)}, u32[]{:S(2)}) collective-permute-start(bf16[14,128,128]{2,1,0:T(8,128)(2,1)S(1)} %bitcast.44), channel_id=1, source_target_pairs={{128,0},{129,1},{130,2},{131,3},{132,4},{133,5},{134,6},{135,7},{3... | collective-permute-start | bytes 1376264 | tf_op jit(solution)/shard_map/ppermute | solution.py:172
  14.0 2.9 %copy-start.3 = (s32[1,32,2]{1,2,0:T(2,128)S(1)}, s32[1,32,2]{1,2,0:T(2,128)}, u32[]{:S(2)}) copy-start(s32[1,32,2]{1,2,0:T(2,128)} %param.8) | copy-start | bytes 772
  14.0 2.9 %slice-start = ((bf16[1,32,2,128,128]{4,3,2,1,0:T(8,128)(2,1)}), bf16[1,16,2,128,128]{4,3,2,1,0:T(8,128)(2,1)S(1)}, s32[]{:S(2)}) async-start(bf16[1,32,2,128,128]{4,3,2,1,0:T(8,128)(2,1)} %param.7), calls=%async_computation | async-start | bytes 2097152 | tf_op jit(solution)/shard_map/slice | solution.py:183
  14.0 40.2 %collective-permute-start.1 = (bf16[33,128,128]{2,1,0:T(8,128)(2,1)S(1)}, bf16[33,128,128]{2,1,0:T(8,128)(2,1)}, u32[]{:S(2)}, u32[]{:S(2)}) collective-permute-start(bf16[33,128,128]{2,1,0:T(8,128)(2,1)S(1)} %pad_maximum_fusion.refs_6_), channel_id=1, source_target_pairs={{2,0},{3,1},{4,2},{5,3},{6,4},{7,5},{8,6},{9,7},{10,8},{11,9},{12,... | collective-permute-start | bytes 3244040 | tf_op jit(solution)/shard_map/ppermute | solution.py:172
  17.0 4.6 %copy-start.4 = (bf16[1,32,2,128,128]{4,3,2,1,0:T(8,128)(2,1)S(1)}, bf16[1,32,2,128,128]{4,3,2,1,0:T(8,128)(2,1)}, u32[]{:S(2)}) copy-start(bf16[1,32,2,128,128]{4,3,2,1,0:T(8,128)(2,1)} %param.7) | copy-start | bytes 6291460
  17.1 37.1 %collective-permute-start.3 = (bf16[33,128,128]{2,1,0:T(8,128)(2,1)S(1)}, bf16[33,128,128]{2,1,0:T(8,128)(2,1)}, u32[]{:S(2)}, u32[]{:S(2)}) collective-permute-start(bf16[33,128,128]{2,1,0:T(8,128)(2,1)S(1)} %pad_maximum_fusion.1.refs_8_), channel_id=1, source_target_pairs={{16,0},{17,1},{18,2},{19,3},{20,4},{21,5},{22,6},{23,7},{24,8},{25... | collective-permute-start | bytes 3244040 | tf_op jit(solution)/shard_map/ppermute | solution.py:172
  21.6 30.1 %collective-permute-start.6 = (bf16[18,128,128]{2,1,0:T(8,128)(2,1)S(1)}, bf16[18,128,128]{2,1,0:T(8,128)(2,1)}, u32[]{:S(2)}, u32[]{:S(2)}) collective-permute-start(bf16[18,128,128]{2,1,0:T(8,128)(2,1)S(1)} %bitcast.46), channel_id=1, source_target_pairs={{96,0},{97,1},{98,2},{99,3},{100,4},{101,5},{102,6},{103,7},{104,8... | collective-permute-start | bytes 1769480 | tf_op jit(solution)/shard_map/ppermute | solution.py:172
  23.6 69.8 %copy-start.5 = (s32[16,1,3]{0,1,2:T(1,128)S(1)}, s32[16,1,3]{0,1,2:T(1,128)}, u32[]{:S(2)}) copy-start(s32[16,1,3]{0,1,2:T(1,128)} %param.9) | copy-start | bytes 580
  24.7 116.9 %copy-start.2 = (s32[16,1,2]{0,2,1:T(2,128)S(1)}, s32[16,1,2]{0,2,1:T(2,128)}, u32[]{:S(2)}) copy-start(s32[16,1,2]{0,2,1:T(2,128)} %param.6) | copy-start | bytes 388
  24.7 29.5 %collective-permute-start.5 = (bf16[14,128,128]{2,1,0:T(8,128)(2,1)S(1)}, bf16[14,128,128]{2,1,0:T(8,128)(2,1)S(1)}, u32[]{:S(2)}, u32[]{:S(2)}) collective-permute-start(bf16[14,128,128]{2,1,0:T(8,128)(2,1)S(1)} %broadcast_select_fusion.2), channel_id=1, source_target_pairs={{16,0},{17,1},{18,2},{19,3},{20,4},{21,5},{22,6},{23,7},{24,8},{25... | collective-permute-start | bytes 1376264 | tf_op jit(solution)/shard_map/ppermute | solution.py:172
  54.2 24.2 %collective-permute-start.10 = (bf16[18,128,128]{2,1,0:T(8,128)(2,1)}, bf16[18,128,128]{2,1,0:T(8,128)(2,1)}, u32[]{:S(2)}, u32[]{:S(2)}) collective-permute-start(bf16[18,128,128]{2,1,0:T(8,128)(2,1)} %collective-permute-done.6), channel_id=1, source_target_pairs={{96,0},{97,1},{98,2},{99,3},{100,4},{101,5},{102,6},{103,7},{104,8... | collective-permute-start | bytes 1769480 | tf_op jit(solution)/shard_map/ppermute | solution.py:172
  56.1 32.3 %collective-permute-start.8 = (bf16[14,128,128]{2,1,0:T(8,128)(2,1)S(1)}, bf16[14,128,128]{2,1,0:T(8,128)(2,1)S(1)}, u32[]{:S(2)}, u32[]{:S(2)}) collective-permute-start(bf16[14,128,128]{2,1,0:T(8,128)(2,1)S(1)} %collective-permute-done.5.refs_9_), channel_id=1, source_target_pairs={{128,0},{129,1},{130,2},{131,3},{132,4},{133,5},{134,6},{135,7},{3... | collective-permute-start | bytes 1376264 | tf_op jit(solution)/shard_map/ppermute | solution.py:172
  60.2 46.2 %collective-permute-start.7 = (bf16[33,128,128]{2,1,0:T(8,128)(2,1)}, bf16[33,128,128]{2,1,0:T(8,128)(2,1)}, u32[]{:S(2)}, u32[]{:S(2)}) collective-permute-start(bf16[33,128,128]{2,1,0:T(8,128)(2,1)} %collective-permute-done.3.refs_8_), channel_id=1, source_target_pairs={{16,0},{17,1},{18,2},{19,3},{20,4},{21,5},{22,6},{23,7},{24,8},{25... | collective-permute-start | bytes 3244040 | tf_op jit(solution)/shard_map/ppermute | solution.py:172
  74.0 42.0 %collective-permute-start = (bf16[33,128,128]{2,1,0:T(8,128)(2,1)S(1)}, bf16[33,128,128]{2,1,0:T(8,128)(2,1)}, u32[]{:S(2)}, u32[]{:S(2)}) collective-permute-start(bf16[33,128,128]{2,1,0:T(8,128)(2,1)S(1)} %pad_maximum_fusion.refs_6_), channel_id=1, source_target_pairs={{1,0},{4,1},{3,2},{6,3},{5,4},{8,5},{7,6},{10,7},{9,8},{12,9},{11,... | collective-permute-start | bytes 3244040 | tf_op jit(solution)/shard_map/ppermute | solution.py:172
  76.0 40.1 %collective-permute-start.2 = (bf16[33,128,128]{2,1,0:T(8,128)(2,1)}, bf16[33,128,128]{2,1,0:T(8,128)(2,1)}, u32[]{:S(2)}, u32[]{:S(2)}) collective-permute-start(bf16[33,128,128]{2,1,0:T(8,128)(2,1)} %collective-permute-done.1.refs_7_), channel_id=1, source_target_pairs={{1,0},{0,1},{3,2},{2,3},{5,4},{4,5},{7,6},{6,7},{9,8},{8,9},{11,10... | collective-permute-start | bytes 3244040 | tf_op jit(solution)/shard_map/ppermute | solution.py:172
  78.4 34.3 %collective-permute-start.12 = (bf16[18,128,128]{2,1,0:T(8,128)(2,1)}, bf16[18,128,128]{2,1,0:T(8,128)(2,1)}, u32[]{:S(2)}, u32[]{:S(2)}) collective-permute-start(bf16[18,128,128]{2,1,0:T(8,128)(2,1)} %collective-permute-done.10), channel_id=1, source_target_pairs={{112,0},{113,1},{114,2},{115,3},{116,4},{117,5},{118,6},{119,7},{1... | collective-permute-start | bytes 1769480 | tf_op jit(solution)/shard_map/ppermute | solution.py:172
  89.2 0.8 copy-start
  90.0 16.4 %collective-permute-start.9 = (bf16[14,128,128]{2,1,0:T(8,128)(2,1)}, bf16[14,128,128]{2,1,0:T(8,128)(2,1)}, u32[]{:S(2)}, u32[]{:S(2)}) collective-permute-start(bf16[14,128,128]{2,1,0:T(8,128)(2,1)} %broadcast_select_fusion.1), channel_id=1, source_target_pairs={{16,0},{17,1},{18,2},{19,3},{20,4},{21,5},{22,6},{23,7},{24,8},{25... | collective-permute-start | bytes 1376264 | tf_op jit(solution)/shard_map/ppermute | solution.py:172
  106.4 29.6 %collective-permute-start.15 = (bf16[14,128,128]{2,1,0:T(8,128)(2,1)}, bf16[14,128,128]{2,1,0:T(8,128)(2,1)S(1)}, u32[]{:S(2)}, u32[]{:S(2)}) collective-permute-start(bf16[14,128,128]{2,1,0:T(8,128)(2,1)} %collective-permute-done.9.refs_12_), channel_id=1, source_target_pairs={{128,0},{129,1},{130,2},{131,3},{132,4},{133,5},{134,6},{135,7},{3... | collective-permute-start | bytes 1376264 | tf_op jit(solution)/shard_map/ppermute | solution.py:172
  108.8 36.3 %collective-permute-start.11 = (bf16[33,128,128]{2,1,0:T(8,128)(2,1)}, bf16[33,128,128]{2,1,0:T(8,128)(2,1)S(1)}, u32[]{:S(2)}, u32[]{:S(2)}) collective-permute-start(bf16[33,128,128]{2,1,0:T(8,128)(2,1)} %collective-permute-done.7.refs_11_), channel_id=1, source_target_pairs={{16,0},{17,1},{18,2},{19,3},{20,4},{21,5},{22,6},{23,7},{24,8},{25... | collective-permute-start | bytes 3244040 | tf_op jit(solution)/shard_map/ppermute | solution.py:172
  112.7 21.4 %collective-permute-start.13 = (bf16[18,128,128]{2,1,0:T(8,128)(2,1)}, bf16[18,128,128]{2,1,0:T(8,128)(2,1)S(1)}, u32[]{:S(2)}, u32[]{:S(2)}) collective-permute-start(bf16[18,128,128]{2,1,0:T(8,128)(2,1)} %collective-permute-done.12.refs_13_), channel_id=1, source_target_pairs={{496,0},{497,1},{498,2},{499,3},{500,4},{501,5},{502,6},{503,7},{2... | collective-permute-start | bytes 1769480 | tf_op jit(solution)/shard_map/ppermute | solution.py:172
  134.1 18.4 %collective-permute-start.14 = (bf16[18,128,128]{2,1,0:T(8,128)(2,1)S(1)}, bf16[18,128,128]{2,1,0:T(8,128)(2,1)S(1)}, u32[]{:S(2)}, u32[]{:S(2)}) collective-permute-start(bf16[18,128,128]{2,1,0:T(8,128)(2,1)S(1)} %collective-permute-done.13.refs_13_), channel_id=1, source_target_pairs={{496,0},{497,1},{498,2},{499,3},{500,4},{501,5},{502,6},{503,7},{2... | collective-permute-start | bytes 1769480 | tf_op jit(solution)/shard_map/ppermute | solution.py:172
  136.1 11.3 %collective-permute-start.16 = (bf16[14,128,128]{2,1,0:T(8,128)(2,1)S(1)}, bf16[14,128,128]{2,1,0:T(8,128)(2,1)S(1)}, u32[]{:S(2)}, u32[]{:S(2)}) collective-permute-start(bf16[14,128,128]{2,1,0:T(8,128)(2,1)S(1)} %broadcast_select_fusion), channel_id=1, source_target_pairs={{16,0},{17,1},{18,2},{19,3},{20,4},{21,5},{22,6},{23,7},{24,8},{25... | collective-permute-start | bytes 1376264 | tf_op jit(solution)/shard_map/ppermute | solution.py:172
  141.6 10.9 %copy-start.1 = (bf16[14,128,128]{2,1,0:T(8,128)(2,1)S(1)}, bf16[14,128,128]{2,1,0:T(8,128)(2,1)}, u32[]{:S(2)}) copy-start(bf16[14,128,128]{2,1,0:T(8,128)(2,1)} %copy-done) | copy-start | bytes 1376260

commit v7 on v6

--- a/solution.py
+++ b/solution.py
@@ -11,7 +11,7 @@
 HALF = 16
 RING = 8
 AXES = ("row", "col")
-CUTS = (32, 46)
+CUTS = (28, 46)
 
 
 def block_kernel(first, flip, count, sizes, *refs):

time: 159 us -> 160 us (level)
  waiting for transfers between devices: 64 us -> 77.8 us
  starting transfers between devices: 75.9 us -> 65.7 us
    ppermute x17, waiting for transfers between devices: 64 us -> 77.8 us  [local(): send = lambda value, pairs: lax.ppermute(value, AXES, pairs)]
    ppermute x17, starting transfers between devices: 75.9 us -> 65.7 us  [local(): send = lambda value, pairs: lax.ppermute(value, AXES, pairs)]
  transfers between devices with their start and end apart: 17 -> 17, of which waited for: 6 -> 8; matrix products, arithmetic and copies ran while one was open for 4% -> 3% of each run, Pallas kernels for 2% -> 2%
where the time goes in v7:
time: 160 us; the launch traced here: 159 us
  waiting for transfers between devices  77.8 us (49%)
  starting transfers between devices  65.7 us (41%)
  Pallas kernels  8.72 us (5%)
  other arithmetic  5.23 us (3%)
    ppermute x17, waiting for transfers between devices, local(): send = lambda value, pairs: lax.ppermute(value, AXES, pairs)  77.8 us
    ppermute x17, starting transfers between devices, local(): send = lambda value, pairs: lax.ppermute(value, AXES, pairs)  65.7 us
    pallas_call x2, Pallas kernels, contribute(): pl.pallas_call(functools.partial(block_kernel, first, flip is not None, c...  8.72 us
  transfers between devices with their start and end apart: 17, of which 8 were waited for; matrix products, arithmetic and copies ran while one was open for 3% of the time, Pallas kernels for 2%

profile of v7, /device:TPU:6, one launch (start us, length us, event | category | flops | bytes accessed | tf_op | source)
XLA Modules:
  0.0 159.2 jit_solution(5894540638493904352)
XLA Ops:
  1.4 10.9 %collective-permute-start.4 = (bf16[18,128,128]{2,1,0:T(8,128)(2,1)S(1)}, bf16[18,128,128]{2,1,0:T(8,128)(2,1)}, u32[]{:S(2)}, u32[]{:S(2)}) collective-permute-start(bf16[18,128,128]{2,1,0:T(8,128)(2,1)S(1)} %bitcast.44), channel_id=1, source_target_pairs={{128,0},{129,1},{130,2},{131,3},{132,4},{133,5},{134,6},{135,7},{3... | collective-permute-start | bytes 1769480 | tf_op jit(solution)/shard_map/ppermute | solution.py:172
  12.5 2.9 %collective-permute-start.1 = (bf16[33,128,128]{2,1,0:T(8,128)(2,1)S(1)}, bf16[33,128,128]{2,1,0:T(8,128)(2,1)}, u32[]{:S(2)}, u32[]{:S(2)}) collective-permute-start(bf16[33,128,128]{2,1,0:T(8,128)(2,1)S(1)} %pad_maximum_fusion.refs_6_), channel_id=1, source_target_pairs={{2,0},{3,1},{4,2},{5,3},{6,4},{7,5},{8,6},{9,7},{10,8},{11,9},{12,... | collective-permute-start | bytes 3244040 | tf_op jit(solution)/shard_map/ppermute | solution.py:172
  15.6 4.4 %collective-permute-start.3 = (bf16[29,128,128]{2,1,0:T(8,128)(2,1)S(1)}, bf16[29,128,128]{2,1,0:T(8,128)(2,1)}, u32[]{:S(2)}, u32[]{:S(2)}) collective-permute-start(bf16[29,128,128]{2,1,0:T(8,128)(2,1)S(1)} %pad_maximum_fusion.1.refs_8_), channel_id=1, source_target_pairs={{16,0},{17,1},{18,2},{19,3},{20,4},{21,5},{22,6},{23,7},{24,8},{25... | collective-permute-start | bytes 2850824 | tf_op jit(solution)/shard_map/ppermute | solution.py:172
  19.9 1.9 %collective-permute-start.6 = (bf16[18,128,128]{2,1,0:T(8,128)(2,1)S(1)}, bf16[18,128,128]{2,1,0:T(8,128)(2,1)}, u32[]{:S(2)}, u32[]{:S(2)}) collective-permute-start(bf16[18,128,128]{2,1,0:T(8,128)(2,1)S(1)} %bitcast.46), channel_id=1, source_target_pairs={{96,0},{97,1},{98,2},{99,3},{100,4},{101,5},{102,6},{103,7},{104,8... | collective-permute-start | bytes 1769480 | tf_op jit(solution)/shard_map/ppermute | solution.py:172
  21.9 3.0 %collective-permute-done.4 = bf16[18,128,128]{2,1,0:T(8,128)(2,1)} collective-permute-done((bf16[18,128,128]{2,1,0:T(8,128)(2,1)S(1)}, bf16[18,128,128]{2,1,0:T(8,128)(2,1)}, u32[]{:S(2)}, u32[]{:S(2)}) %collective-permute-start.4) | collective-permute-done | bytes 589856 | tf_op jit(solution)/shard_map/ppermute | solution.py:172
  26.1 1.9 %collective-permute-start.5 = (bf16[18,128,128]{2,1,0:T(8,128)(2,1)S(1)}, bf16[18,128,128]{2,1,0:T(8,128)(2,1)S(1)}, u32[]{:S(2)}, u32[]{:S(2)}) collective-permute-start(bf16[18,128,128]{2,1,0:T(8,128)(2,1)S(1)} %broadcast_select_fusion.2), channel_id=1, source_target_pairs={{16,0},{17,1},{18,2},{19,3},{20,4},{21,5},{22,6},{23,7},{24,8},{25... | collective-permute-start | bytes 1769480 | tf_op jit(solution)/shard_map/ppermute | solution.py:172
  28.0 22.0 %collective-permute-done.6 = bf16[18,128,128]{2,1,0:T(8,128)(2,1)} collective-permute-done((bf16[18,128,128]{2,1,0:T(8,128)(2,1)S(1)}, bf16[18,128,128]{2,1,0:T(8,128)(2,1)}, u32[]{:S(2)}, u32[]{:S(2)}) %collective-permute-start.6) | collective-permute-done | bytes 589856 | tf_op jit(solution)/shard_map/ppermute | solution.py:172
  50.0 2.6 %collective-permute-done.5.refs_9_ = bf16[18,128,128]{2,1,0:T(8,128)(2,1)S(1)} collective-permute-done((bf16[18,128,128]{2,1,0:T(8,128)(2,1)S(1)}, bf16[18,128,128]{2,1,0:T(8,128)(2,1)S(1)}, u32[]{:S(2)}, u32[]{:S(2)}) %collective-permute-start.5) | collective-permute-done | bytes 589856 | tf_op jit(solution)/shard_map/ppermute | solution.py:172
  52.6 2.4 %collective-permute-start.8 = (bf16[18,128,128]{2,1,0:T(8,128)(2,1)S(1)}, bf16[18,128,128]{2,1,0:T(8,128)(2,1)S(1)}, u32[]{:S(2)}, u32[]{:S(2)}) collective-permute-start(bf16[18,128,128]{2,1,0:T(8,128)(2,1)S(1)} %collective-permute-done.5.refs_9_), channel_id=1, source_target_pairs={{128,0},{129,1},{130,2},{131,3},{132,4},{133,5},{134,6},{135,7},{3... | collective-permute-start | bytes 1769480 | tf_op jit(solution)/shard_map/ppermute | solution.py:172
  55.0 1.9 %collective-permute-start.10 = (bf16[18,128,128]{2,1,0:T(8,128)(2,1)}, bf16[18,128,128]{2,1,0:T(8,128)(2,1)}, u32[]{:S(2)}, u32[]{:S(2)}) collective-permute-start(bf16[18,128,128]{2,1,0:T(8,128)(2,1)} %collective-permute-done.6), channel_id=1, source_target_pairs={{96,0},{97,1},{98,2},{99,3},{100,4},{101,5},{102,6},{103,7},{104,8... | collective-permute-start | bytes 1769480 | tf_op jit(solution)/shard_map/ppermute | solution.py:172
  57.0 12.8 %collective-permute-start.7 = (bf16[29,128,128]{2,1,0:T(8,128)(2,1)}, bf16[29,128,128]{2,1,0:T(8,128)(2,1)}, u32[]{:S(2)}, u32[]{:S(2)}) collective-permute-start(bf16[29,128,128]{2,1,0:T(8,128)(2,1)} %collective-permute-done.3.refs_8_), channel_id=1, source_target_pairs={{16,0},{17,1},{18,2},{19,3},{20,4},{21,5},{22,6},{23,7},{24,8},{25... | collective-permute-start | bytes 2850824 | tf_op jit(solution)/shard_map/ppermute | solution.py:172
  69.9 1.9 %collective-permute-start.9 = (bf16[18,128,128]{2,1,0:T(8,128)(2,1)S(1)}, bf16[18,128,128]{2,1,0:T(8,128)(2,1)}, u32[]{:S(2)}, u32[]{:S(2)}) collective-permute-start(bf16[18,128,128]{2,1,0:T(8,128)(2,1)S(1)} %broadcast_select_fusion.1), channel_id=1, source_target_pairs={{16,0},{17,1},{18,2},{19,3},{20,4},{21,5},{22,6},{23,7},{24,8},{25... | collective-permute-start | bytes 1769480 | tf_op jit(solution)/shard_map/ppermute | solution.py:172
  71.8 14.9 %collective-permute-done.10 = bf16[18,128,128]{2,1,0:T(8,128)(2,1)} collective-permute-done((bf16[18,128,128]{2,1,0:T(8,128)(2,1)}, bf16[18,128,128]{2,1,0:T(8,128)(2,1)}, u32[]{:S(2)}, u32[]{:S(2)}) %collective-permute-start.10) | collective-permute-done | bytes 589856 | tf_op jit(solution)/shard_map/ppermute | solution.py:172
  88.6 1.9 %collective-permute-start = (bf16[33,128,128]{2,1,0:T(8,128)(2,1)S(1)}, bf16[33,128,128]{2,1,0:T(8,128)(2,1)}, u32[]{:S(2)}, u32[]{:S(2)}) collective-permute-start(bf16[33,128,128]{2,1,0:T(8,128)(2,1)S(1)} %pad_maximum_fusion.refs_6_), channel_id=1, source_target_pairs={{1,0},{4,1},{3,2},{6,3},{5,4},{8,5},{7,6},{10,7},{9,8},{12,9},{11,... | collective-permute-start | bytes 3244040 | tf_op jit(solution)/shard_map/ppermute | solution.py:172
  90.5 2.4 %collective-permute-start.2 = (bf16[33,128,128]{2,1,0:T(8,128)(2,1)}, bf16[33,128,128]{2,1,0:T(8,128)(2,1)}, u32[]{:S(2)}, u32[]{:S(2)}) collective-permute-start(bf16[33,128,128]{2,1,0:T(8,128)(2,1)} %collective-permute-done.1.refs_7_), channel_id=1, source_target_pairs={{1,0},{0,1},{3,2},{2,3},{5,4},{4,5},{7,6},{6,7},{9,8},{8,9},{11,10... | collective-permute-start | bytes 3244040 | tf_op jit(solution)/shard_map/ppermute | solution.py:172
  93.0 9.1 %collective-permute-done.9.refs_12_ = bf16[18,128,128]{2,1,0:T(8,128)(2,1)} collective-permute-done((bf16[18,128,128]{2,1,0:T(8,128)(2,1)S(1)}, bf16[18,128,128]{2,1,0:T(8,128)(2,1)}, u32[]{:S(2)}, u32[]{:S(2)}) %collective-permute-start.9) | collective-permute-done | bytes 589856 | tf_op jit(solution)/shard_map/ppermute | solution.py:172
  102.0 2.4 %collective-permute-start.15 = (bf16[18,128,128]{2,1,0:T(8,128)(2,1)}, bf16[18,128,128]{2,1,0:T(8,128)(2,1)}, u32[]{:S(2)}, u32[]{:S(2)}) collective-permute-start(bf16[18,128,128]{2,1,0:T(8,128)(2,1)} %collective-permute-done.9.refs_12_), channel_id=1, source_target_pairs={{128,0},{129,1},{130,2},{131,3},{132,4},{133,5},{134,6},{135,7},{3... | collective-permute-start | bytes 1769480 | tf_op jit(solution)/shard_map/ppermute | solution.py:172
  107.1 8.1 %collective-permute-start.11 = (bf16[29,128,128]{2,1,0:T(8,128)(2,1)}, bf16[29,128,128]{2,1,0:T(8,128)(2,1)S(1)}, u32[]{:S(2)}, u32[]{:S(2)}) collective-permute-start(bf16[29,128,128]{2,1,0:T(8,128)(2,1)} %collective-permute-done.7.refs_11_), channel_id=1, source_target_pairs={{16,0},{17,1},{18,2},{19,3},{20,4},{21,5},{22,6},{23,7},{24,8},{25... | collective-permute-start | bytes 2850824 | tf_op jit(solution)/shard_map/ppermute | solution.py:172
  116.0 16.6 %collective-permute-done.15 = bf16[18,128,128]{2,1,0:T(8,128)(2,1)} collective-permute-done((bf16[18,128,128]{2,1,0:T(8,128)(2,1)}, bf16[18,128,128]{2,1,0:T(8,128)(2,1)}, u32[]{:S(2)}, u32[]{:S(2)}) %collective-permute-start.15) | collective-permute-done | bytes 589856 | tf_op jit(solution)/shard_map/ppermute | solution.py:172
  135.6 3.9 %collective-permute-start.14 = (bf16[18,128,128]{2,1,0:T(8,128)(2,1)S(1)}, bf16[18,128,128]{2,1,0:T(8,128)(2,1)S(1)}, u32[]{:S(2)}, u32[]{:S(2)}) collective-permute-start(bf16[18,128,128]{2,1,0:T(8,128)(2,1)S(1)} %collective-permute-done.13.refs_13_), channel_id=1, source_target_pairs={{496,0},{497,1},{498,2},{499,3},{500,4},{501,5},{502,6},{503,7},{2... | collective-permute-start | bytes 1769480 | tf_op jit(solution)/shard_map/ppermute | solution.py:172
  140.9 3.5 %shard_map.55.refs_14_ = f32[16,3,128,128]{3,2,1,0:T(8,128)S(1)} custom-call(s32[1]{0:T(128)} %constant.36.clone.1.refs_0_, s32[3,16]{1,0:T(4,128)S(1)} %bitcast.48, s32[2,16]{1,0:T(2,128)S(1)} %bitcast.50, s32[2,16]{1,0:T(2,128)S(1)} %bitcast_convert_fusion.1.refs_3_, s32[2,32]{1,0:T(2,128)S(1)} %bitcast.51, s32[2,32]{1,0:T(2,128)S(1)} %bitcast_convert_fusion.refs_5_, ...), custom_call_target="tpu_custom_call" | custom-call | flops 805306368 | bytes 12582912 | tf_op jit(solution)/shard_map/pallas_call | solution.py:96
  144.5 3.4 %collective-permute-done.16.refs_12_ = bf16[18,128,128]{2,1,0:T(8,128)(2,1)S(1)} collective-permute-done((bf16[18,128,128]{2,1,0:T(8,128)(2,1)S(1)}, bf16[18,128,128]{2,1,0:T(8,128)(2,1)S(1)}, u32[]{:S(2)}, u32[]{:S(2)}) %collective-permute-start.16) | collective-permute-done | bytes 589856 | tf_op jit(solution)/shard_map/ppermute | solution.py:172
  147.9 6.2 %collective-permute-done.14.refs_10_ = bf16[18,128,128]{2,1,0:T(8,128)(2,1)S(1)} collective-permute-done((bf16[18,128,128]{2,1,0:T(8,128)(2,1)S(1)}, bf16[18,128,128]{2,1,0:T(8,128)(2,1)S(1)}, u32[]{:S(2)}, u32[]{:S(2)}) %collective-permute-start.14) | collective-permute-done | bytes 589856 | tf_op jit(solution)/shard_map/ppermute | solution.py:172
  154.1 5.2 %shard_map.56 = bf16[16,3,128,128]{3,2,1,0:T(8,128)(2,1)} custom-call(s32[1]{0:T(128)} %bitcast.refs_0_, s32[3,16]{1,0:T(4,128)S(1)} %bitcast.49, s32[2,16]{1,0:T(2,128)S(1)} %get-tuple-element.18.refs_2_, s32[2,16]{1,0:T(2,128)S(1)} %get-tuple-element.17.refs_3_, s32[2,32]{1,0:T(2,128)S(1)} %bitcast_convert_fusion.2.refs_4_, s32[2,32]{1,0:T(2,128)S(1)} %fusion.2.refs_5_, ...), custom_call_target="tpu_custom_call" | custom-call | flops 805306368 | bytes 12582912 | tf_op jit(solution)/shard_map/pallas_call | solution.py:96
  (42 shorter events, 12.5 us)
Async XLA Ops:
  0.0 12.4 %copy-start.2 = (s32[16,1,2]{0,2,1:T(2,128)S(1)}, s32[16,1,2]{0,2,1:T(2,128)}, u32[]{:S(2)}) copy-start(s32[16,1,2]{0,2,1:T(2,128)} %param.6) | copy-start | bytes 388
  0.0 12.4 %copy-start.4 = (bf16[16,1,2,128,128]{4,3,2,1,0:T(8,128)(2,1)S(1)}, bf16[16,1,2,128,128]{4,3,2,1,0:T(8,128)(2,1)}, u32[]{:S(2)}) copy-start(bf16[16,1,2,128,128]{4,3,2,1,0:T(8,128)(2,1)} %param.5) | copy-start | bytes 3145732
  1.4 23.5 %collective-permute-start.4 = (bf16[18,128,128]{2,1,0:T(8,128)(2,1)S(1)}, bf16[18,128,128]{2,1,0:T(8,128)(2,1)}, u32[]{:S(2)}, u32[]{:S(2)}) collective-permute-start(bf16[18,128,128]{2,1,0:T(8,128)(2,1)S(1)} %bitcast.44), channel_id=1, source_target_pairs={{128,0},{129,1},{130,2},{131,3},{132,4},{133,5},{134,6},{135,7},{3... | collective-permute-start | bytes 1769480 | tf_op jit(solution)/shard_map/ppermute | solution.py:172
  12.5 2.9 %copy-start.3 = (s32[1,32,2]{1,2,0:T(2,128)S(1)}, s32[1,32,2]{1,2,0:T(2,128)}, u32[]{:S(2)}) copy-start(s32[1,32,2]{1,2,0:T(2,128)} %param.8) | copy-start | bytes 772
  12.5 2.9 %slice-start = ((bf16[1,32,2,128,128]{4,3,2,1,0:T(8,128)(2,1)}), bf16[1,14,2,128,128]{4,3,2,1,0:T(8,128)(2,1)S(1)}, s32[]{:S(2)}) async-start(bf16[1,32,2,128,128]{4,3,2,1,0:T(8,128)(2,1)} %param.7), calls=%async_computation | async-start | bytes 1835008 | tf_op jit(solution)/shard_map/slice | solution.py:183
  12.5 37.5 %collective-permute-start.1 = (bf16[33,128,128]{2,1,0:T(8,128)(2,1)S(1)}, bf16[33,128,128]{2,1,0:T(8,128)(2,1)}, u32[]{:S(2)}, u32[]{:S(2)}) collective-permute-start(bf16[33,128,128]{2,1,0:T(8,128)(2,1)S(1)} %pad_maximum_fusion.refs_6_), channel_id=1, source_target_pairs={{2,0},{3,1},{4,2},{5,3},{6,4},{7,5},{8,6},{9,7},{10,8},{11,9},{12,... | collective-permute-start | bytes 3244040 | tf_op jit(solution)/shard_map/ppermute | solution.py:172
  15.6 34.4 %collective-permute-start.3 = (bf16[29,128,128]{2,1,0:T(8,128)(2,1)S(1)}, bf16[29,128,128]{2,1,0:T(8,128)(2,1)}, u32[]{:S(2)}, u32[]{:S(2)}) collective-permute-start(bf16[29,128,128]{2,1,0:T(8,128)(2,1)S(1)} %pad_maximum_fusion.1.refs_8_), channel_id=1, source_target_pairs={{16,0},{17,1},{18,2},{19,3},{20,4},{21,5},{22,6},{23,7},{24,8},{25... | collective-permute-start | bytes 2850824 | tf_op jit(solution)/shard_map/ppermute | solution.py:172
  19.9 30.0 %collective-permute-start.6 = (bf16[18,128,128]{2,1,0:T(8,128)(2,1)S(1)}, bf16[18,128,128]{2,1,0:T(8,128)(2,1)}, u32[]{:S(2)}, u32[]{:S(2)}) collective-permute-start(bf16[18,128,128]{2,1,0:T(8,128)(2,1)S(1)} %bitcast.46), channel_id=1, source_target_pairs={{96,0},{97,1},{98,2},{99,3},{100,4},{101,5},{102,6},{103,7},{104,8... | collective-permute-start | bytes 1769480 | tf_op jit(solution)/shard_map/ppermute | solution.py:172
  26.1 78.4 %copy-start.5 = (s32[16,1,3]{0,1,2:T(1,128)S(1)}, s32[16,1,3]{0,1,2:T(1,128)}, u32[]{:S(2)}) copy-start(s32[16,1,3]{0,1,2:T(1,128)} %param.9) | copy-start | bytes 580
  26.1 26.5 %collective-permute-start.5 = (bf16[18,128,128]{2,1,0:T(8,128)(2,1)S(1)}, bf16[18,128,128]{2,1,0:T(8,128)(2,1)S(1)}, u32[]{:S(2)}, u32[]{:S(2)}) collective-permute-start(bf16[18,128,128]{2,1,0:T(8,128)(2,1)S(1)} %broadcast_select_fusion.2), channel_id=1, source_target_pairs={{16,0},{17,1},{18,2},{19,3},{20,4},{21,5},{22,6},{23,7},{24,8},{25... | collective-permute-start | bytes 1769480 | tf_op jit(solution)/shard_map/ppermute | solution.py:172
  52.6 34.1 %copy-start = (bf16[18,128,128]{2,1,0:T(8,128)(2,1)}, bf16[18,128,128]{2,1,0:T(8,128)(2,1)S(1)}, u32[]{:S(2)}) copy-start(bf16[18,128,128]{2,1,0:T(8,128)(2,1)S(1)} %collective-permute-done.5.refs_9_) | copy-start | bytes 1769476
  52.6 17.2 %collective-permute-start.8 = (bf16[18,128,128]{2,1,0:T(8,128)(2,1)S(1)}, bf16[18,128,128]{2,1,0:T(8,128)(2,1)S(1)}, u32[]{:S(2)}, u32[]{:S(2)}) collective-permute-start(bf16[18,128,128]{2,1,0:T(8,128)(2,1)S(1)} %collective-permute-done.5.refs_9_), channel_id=1, source_target_pairs={{128,0},{129,1},{130,2},{131,3},{132,4},{133,5},{134,6},{135,7},{3... | collective-permute-start | bytes 1769480 | tf_op jit(solution)/shard_map/ppermute | solution.py:172
  55.0 31.6 %collective-permute-start.10 = (bf16[18,128,128]{2,1,0:T(8,128)(2,1)}, bf16[18,128,128]{2,1,0:T(8,128)(2,1)}, u32[]{:S(2)}, u32[]{:S(2)}) collective-permute-start(bf16[18,128,128]{2,1,0:T(8,128)(2,1)} %collective-permute-done.6), channel_id=1, source_target_pairs={{96,0},{97,1},{98,2},{99,3},{100,4},{101,5},{102,6},{103,7},{104,8... | collective-permute-start | bytes 1769480 | tf_op jit(solution)/shard_map/ppermute | solution.py:172
  57.0 36.0 %collective-permute-start.7 = (bf16[29,128,128]{2,1,0:T(8,128)(2,1)}, bf16[29,128,128]{2,1,0:T(8,128)(2,1)}, u32[]{:S(2)}, u32[]{:S(2)}) collective-permute-start(bf16[29,128,128]{2,1,0:T(8,128)(2,1)} %collective-permute-done.3.refs_8_), channel_id=1, source_target_pairs={{16,0},{17,1},{18,2},{19,3},{20,4},{21,5},{22,6},{23,7},{24,8},{25... | collective-permute-start | bytes 2850824 | tf_op jit(solution)/shard_map/ppermute | solution.py:172
  69.9 32.2 %collective-permute-start.9 = (bf16[18,128,128]{2,1,0:T(8,128)(2,1)S(1)}, bf16[18,128,128]{2,1,0:T(8,128)(2,1)}, u32[]{:S(2)}, u32[]{:S(2)}) collective-permute-start(bf16[18,128,128]{2,1,0:T(8,128)(2,1)S(1)} %broadcast_select_fusion.1), channel_id=1, source_target_pairs={{16,0},{17,1},{18,2},{19,3},{20,4},{21,5},{22,6},{23,7},{24,8},{25... | collective-permute-start | bytes 1769480 | tf_op jit(solution)/shard_map/ppermute | solution.py:172
  86.7 17.8 %collective-permute-start.12 = (bf16[18,128,128]{2,1,0:T(8,128)(2,1)}, bf16[18,128,128]{2,1,0:T(8,128)(2,1)}, u32[]{:S(2)}, u32[]{:S(2)}) collective-permute-start(bf16[18,128,128]{2,1,0:T(8,128)(2,1)} %collective-permute-done.10), channel_id=1, source_target_pairs={{112,0},{113,1},{114,2},{115,3},{116,4},{117,5},{118,6},{119,7},{1... | collective-permute-start | bytes 1769480 | tf_op jit(solution)/shard_map/ppermute | solution.py:172
  88.6 50.9 %collective-permute-start = (bf16[33,128,128]{2,1,0:T(8,128)(2,1)S(1)}, bf16[33,128,128]{2,1,0:T(8,128)(2,1)}, u32[]{:S(2)}, u32[]{:S(2)}) collective-permute-start(bf16[33,128,128]{2,1,0:T(8,128)(2,1)S(1)} %pad_maximum_fusion.refs_6_), channel_id=1, source_target_pairs={{1,0},{4,1},{3,2},{6,3},{5,4},{8,5},{7,6},{10,7},{9,8},{12,9},{11,... | collective-permute-start | bytes 3244040 | tf_op jit(solution)/shard_map/ppermute | solution.py:172
  90.5 49.0 %collective-permute-start.2 = (bf16[33,128,128]{2,1,0:T(8,128)(2,1)}, bf16[33,128,128]{2,1,0:T(8,128)(2,1)}, u32[]{:S(2)}, u32[]{:S(2)}) collective-permute-start(bf16[33,128,128]{2,1,0:T(8,128)(2,1)} %collective-permute-done.1.refs_7_), channel_id=1, source_target_pairs={{1,0},{0,1},{3,2},{2,3},{5,4},{4,5},{7,6},{6,7},{9,8},{8,9},{11,10... | collective-permute-start | bytes 3244040 | tf_op jit(solution)/shard_map/ppermute | solution.py:172
  102.0 30.5 %collective-permute-start.15 = (bf16[18,128,128]{2,1,0:T(8,128)(2,1)}, bf16[18,128,128]{2,1,0:T(8,128)(2,1)}, u32[]{:S(2)}, u32[]{:S(2)}) collective-permute-start(bf16[18,128,128]{2,1,0:T(8,128)(2,1)} %collective-permute-done.9.refs_12_), channel_id=1, source_target_pairs={{128,0},{129,1},{130,2},{131,3},{132,4},{133,5},{134,6},{135,7},{3... | collective-permute-start | bytes 1769480 | tf_op jit(solution)/shard_map/ppermute | solution.py:172
  104.5 31.0 %collective-permute-start.13 = (bf16[18,128,128]{2,1,0:T(8,128)(2,1)}, bf16[18,128,128]{2,1,0:T(8,128)(2,1)S(1)}, u32[]{:S(2)}, u32[]{:S(2)}) collective-permute-start(bf16[18,128,128]{2,1,0:T(8,128)(2,1)} %collective-permute-done.12.refs_13_), channel_id=1, source_target_pairs={{496,0},{497,1},{498,2},{499,3},{500,4},{501,5},{502,6},{503,7},{2... | collective-permute-start | bytes 1769480 | tf_op jit(solution)/shard_map/ppermute | solution.py:172
  107.1 37.3 %collective-permute-start.11 = (bf16[29,128,128]{2,1,0:T(8,128)(2,1)}, bf16[29,128,128]{2,1,0:T(8,128)(2,1)S(1)}, u32[]{:S(2)}, u32[]{:S(2)}) collective-permute-start(bf16[29,128,128]{2,1,0:T(8,128)(2,1)} %collective-permute-done.7.refs_11_), channel_id=1, source_target_pairs={{16,0},{17,1},{18,2},{19,3},{20,4},{21,5},{22,6},{23,7},{24,8},{25... | collective-permute-start | bytes 2850824 | tf_op jit(solution)/shard_map/ppermute | solution.py:172
  133.6 14.2 %collective-permute-start.16 = (bf16[18,128,128]{2,1,0:T(8,128)(2,1)S(1)}, bf16[18,128,128]{2,1,0:T(8,128)(2,1)S(1)}, u32[]{:S(2)}, u32[]{:S(2)}) collective-permute-start(bf16[18,128,128]{2,1,0:T(8,128)(2,1)S(1)} %broadcast_select_fusion), channel_id=1, source_target_pairs={{16,0},{17,1},{18,2},{19,3},{20,4},{21,5},{22,6},{23,7},{24,8},{25... | collective-permute-start | bytes 1769480 | tf_op jit(solution)/shard_map/ppermute | solution.py:172
  135.6 18.5 %collective-permute-start.14 = (bf16[18,128,128]{2,1,0:T(8,128)(2,1)S(1)}, bf16[18,128,128]{2,1,0:T(8,128)(2,1)S(1)}, u32[]{:S(2)}, u32[]{:S(2)}) collective-permute-start(bf16[18,128,128]{2,1,0:T(8,128)(2,1)S(1)} %collective-permute-done.13.refs_13_), channel_id=1, source_target_pairs={{496,0},{497,1},{498,2},{499,3},{500,4},{501,5},{502,6},{503,7},{2... | collective-permute-start | bytes 1769480 | tf_op jit(solution)/shard_map/ppermute | solution.py:172
  140.9 13.2 %copy-start.1 = (bf16[18,128,128]{2,1,0:T(8,128)(2,1)S(1)}, bf16[18,128,128]{2,1,0:T(8,128)(2,1)}, u32[]{:S(2)}) copy-start(bf16[18,128,128]{2,1,0:T(8,128)(2,1)} %copy-done) | copy-start | bytes 1769476

commit v8 on v7

--- a/solution.py
+++ b/solution.py
@@ -11,7 +11,7 @@
 HALF = 16
 RING = 8
 AXES = ("row", "col")
-CUTS = (28, 46)
+CUTS = (30, 46)
 
 
 def block_kernel(first, flip, count, sizes, *refs):
@@ -60,7 +60,7 @@
         for copy in copies[slot]:
             copy.wait()
 
-        @pl.loop(0, rows, unroll=8)
+        @pl.loop(0, rows, unroll=16)
         def _(i):
             left = jnp.concatenate([a[slot, 2 * i], a[slot, 2 * i + 1]], axis=1)
             right = []
@@ -195,7 +195,7 @@
     third = send(up_two, paths.up_in)
     most.append(send(most[1], paths.down))
     some.append(inside(some[1]))
-    most[2], some[2], _ = lax.optimization_barrier((most[2], some[2], up_two))
+    most[2], some[2], left_odd, _ = lax.optimization_barrier((most[2], some[2], left_odd, up_two))
     most.append(send(most[2], paths.down))
     some.append(inside(some[2]))
     second = send(third, paths.up)

time: 160 us -> 167 us (1.044)
  starting transfers between devices: 65.7 us -> 75.6 us
  waiting for transfers between devices: 77.8 us -> 72.9 us
    ppermute x17, starting transfers between devices: 65.7 us -> 75.6 us  [local(): send = lambda value, pairs: lax.ppermute(value, AXES, pairs)]
    ppermute x17, waiting for transfers between devices: 77.8 us -> 72.9 us  [local(): send = lambda value, pairs: lax.ppermute(value, AXES, pairs)]
  transfers between devices with their start and end apart: 17 -> 17, of which waited for: 8 -> 9; matrix products, arithmetic and copies ran while one was open for 3% -> 4% of each run, Pallas kernels for 2% -> 2%
where the time goes in v8:
time: 167 us; the launch traced here: 166 us
  starting transfers between devices  75.6 us (45%)
  waiting for transfers between devices  72.9 us (44%)
  Pallas kernels  8.35 us (5%)
  other arithmetic  5.86 us (4%)
  local copies, waits for them, and re-layouts  2.5 us (1%)
    ppermute x17, starting transfers between devices, local(): send = lambda value, pairs: lax.ppermute(value, AXES, pairs)  75.6 us
    ppermute x17, waiting for transfers between devices, local(): send = lambda value, pairs: lax.ppermute(value, AXES, pairs)  72.9 us
    pallas_call x2, Pallas kernels, contribute(): pl.pallas_call(functools.partial(block_kernel, first, flip is not None, c...  8.35 us
  transfers between devices with their start and end apart: 17, of which 9 were waited for; matrix products, arithmetic and copies ran while one was open for 4% of the time, Pallas kernels for 2%

profile of v8, /device:TPU:6, one launch (start us, length us, event | category | flops | bytes accessed | tf_op | source)
XLA Modules:
  0.0 165.6 jit_solution(2061312681827888754)
XLA Ops:
  1.2 10.9 %collective-permute-start.1 = (bf16[16,128,128]{2,1,0:T(8,128)(2,1)S(1)}, bf16[16,128,128]{2,1,0:T(8,128)(2,1)}, u32[]{:S(2)}, u32[]{:S(2)}) collective-permute-start(bf16[16,128,128]{2,1,0:T(8,128)(2,1)S(1)} %bitcast.44), channel_id=1, source_target_pairs={{128,0},{129,1},{130,2},{131,3},{132,4},{133,5},{134,6},{135,7},{3... | collective-permute-start | bytes 1572872 | tf_op jit(solution)/shard_map/ppermute | solution.py:172
  13.0 2.9 %collective-permute-start.3 = (bf16[33,128,128]{2,1,0:T(8,128)(2,1)S(1)}, bf16[33,128,128]{2,1,0:T(8,128)(2,1)}, u32[]{:S(2)}, u32[]{:S(2)}) collective-permute-start(bf16[33,128,128]{2,1,0:T(8,128)(2,1)S(1)} %pad_maximum_fusion.refs_6_), channel_id=1, source_target_pairs={{2,0},{3,1},{4,2},{5,3},{6,4},{7,5},{8,6},{9,7},{10,8},{11,9},{12,... | collective-permute-start | bytes 3244040 | tf_op jit(solution)/shard_map/ppermute | solution.py:172
  16.0 4.5 %collective-permute-start = (bf16[31,128,128]{2,1,0:T(8,128)(2,1)S(1)}, bf16[31,128,128]{2,1,0:T(8,128)(2,1)}, u32[]{:S(2)}, u32[]{:S(2)}) collective-permute-start(bf16[31,128,128]{2,1,0:T(8,128)(2,1)S(1)} %pad_maximum_fusion.1.refs_8_), channel_id=1, source_target_pairs={{16,0},{17,1},{18,2},{19,3},{20,4},{21,5},{22,6},{23,7},{24,8},{25... | collective-permute-start | bytes 3047432 | tf_op jit(solution)/shard_map/ppermute | solution.py:172
  20.6 1.9 %collective-permute-start.4 = (bf16[18,128,128]{2,1,0:T(8,128)(2,1)S(1)}, bf16[18,128,128]{2,1,0:T(8,128)(2,1)}, u32[]{:S(2)}, u32[]{:S(2)}) collective-permute-start(bf16[18,128,128]{2,1,0:T(8,128)(2,1)S(1)} %bitcast.46), channel_id=1, source_target_pairs={{96,0},{97,1},{98,2},{99,3},{100,4},{101,5},{102,6},{103,7},{104,8... | collective-permute-start | bytes 1769480 | tf_op jit(solution)/shard_map/ppermute | solution.py:172
  24.4 2.4 %collective-permute-start.2 = (bf16[16,128,128]{2,1,0:T(8,128)(2,1)S(1)}, bf16[16,128,128]{2,1,0:T(8,128)(2,1)S(1)}, u32[]{:S(2)}, u32[]{:S(2)}) collective-permute-start(bf16[16,128,128]{2,1,0:T(8,128)(2,1)S(1)} %broadcast_select_fusion.2), channel_id=1, source_target_pairs={{16,0},{17,1},{18,2},{19,3},{20,4},{21,5},{22,6},{23,7},{24,8},{25... | collective-permute-start | bytes 1572872 | tf_op jit(solution)/shard_map/ppermute | solution.py:172
  26.8 23.9 %collective-permute-done.4 = bf16[18,128,128]{2,1,0:T(8,128)(2,1)} collective-permute-done((bf16[18,128,128]{2,1,0:T(8,128)(2,1)S(1)}, bf16[18,128,128]{2,1,0:T(8,128)(2,1)}, u32[]{:S(2)}, u32[]{:S(2)}) %collective-permute-start.4) | collective-permute-done | bytes 589856 | tf_op jit(solution)/shard_map/ppermute | solution.py:172
  50.6 2.5 %collective-permute-done.2.refs_9_ = bf16[16,128,128]{2,1,0:T(8,128)(2,1)S(1)} collective-permute-done((bf16[16,128,128]{2,1,0:T(8,128)(2,1)S(1)}, bf16[16,128,128]{2,1,0:T(8,128)(2,1)S(1)}, u32[]{:S(2)}, u32[]{:S(2)}) %collective-permute-start.2) | collective-permute-done | bytes 524320 | tf_op jit(solution)/shard_map/ppermute | solution.py:172
  53.2 2.4 %collective-permute-start.6 = (bf16[16,128,128]{2,1,0:T(8,128)(2,1)S(1)}, bf16[16,128,128]{2,1,0:T(8,128)(2,1)S(1)}, u32[]{:S(2)}, u32[]{:S(2)}) collective-permute-start(bf16[16,128,128]{2,1,0:T(8,128)(2,1)S(1)} %collective-permute-done.2.refs_9_), channel_id=1, source_target_pairs={{128,0},{129,1},{130,2},{131,3},{132,4},{133,5},{134,6},{135,7},{3... | collective-permute-start | bytes 1572872 | tf_op jit(solution)/shard_map/ppermute | solution.py:172
  55.6 1.9 %collective-permute-start.9 = (bf16[18,128,128]{2,1,0:T(8,128)(2,1)}, bf16[18,128,128]{2,1,0:T(8,128)(2,1)}, u32[]{:S(2)}, u32[]{:S(2)}) collective-permute-start(bf16[18,128,128]{2,1,0:T(8,128)(2,1)} %collective-permute-done.4), channel_id=1, source_target_pairs={{96,0},{97,1},{98,2},{99,3},{100,4},{101,5},{102,6},{103,7},{104,8... | collective-permute-start | bytes 1769480 | tf_op jit(solution)/shard_map/ppermute | solution.py:172
  59.5 14.0 %collective-permute-start.5 = (bf16[31,128,128]{2,1,0:T(8,128)(2,1)}, bf16[31,128,128]{2,1,0:T(8,128)(2,1)S(1)}, u32[]{:S(2)}, u32[]{:S(2)}) collective-permute-start(bf16[31,128,128]{2,1,0:T(8,128)(2,1)} %collective-permute-done.refs_8_), channel_id=1, source_target_pairs={{16,0},{17,1},{18,2},{19,3},{20,4},{21,5},{22,6},{23,7},{24,8},{25... | collective-permute-start | bytes 3047432 | tf_op jit(solution)/shard_map/ppermute | solution.py:172
  73.6 1.9 %collective-permute-start.7 = (bf16[16,128,128]{2,1,0:T(8,128)(2,1)S(1)}, bf16[16,128,128]{2,1,0:T(8,128)(2,1)}, u32[]{:S(2)}, u32[]{:S(2)}) collective-permute-start(bf16[16,128,128]{2,1,0:T(8,128)(2,1)S(1)} %broadcast_select_fusion.1), channel_id=1, source_target_pairs={{16,0},{17,1},{18,2},{19,3},{20,4},{21,5},{22,6},{23,7},{24,8},{25... | collective-permute-start | bytes 1572872 | tf_op jit(solution)/shard_map/ppermute | solution.py:172
  75.7 13.8 %collective-permute-start.12 = (bf16[18,128,128]{2,1,0:T(8,128)(2,1)}, bf16[18,128,128]{2,1,0:T(8,128)(2,1)}, u32[]{:S(2)}, u32[]{:S(2)}) collective-permute-start(bf16[18,128,128]{2,1,0:T(8,128)(2,1)} %collective-permute-done.9), channel_id=1, source_target_pairs={{112,0},{113,1},{114,2},{115,3},{116,4},{117,5},{118,6},{119,7},{1... | collective-permute-start | bytes 1769480 | tf_op jit(solution)/shard_map/ppermute | solution.py:172
  89.5 1.9 %collective-permute-start.10 = (bf16[33,128,128]{2,1,0:T(8,128)(2,1)}, bf16[33,128,128]{2,1,0:T(8,128)(2,1)}, u32[]{:S(2)}, u32[]{:S(2)}) collective-permute-start(bf16[33,128,128]{2,1,0:T(8,128)(2,1)} %collective-permute-done.3.refs_7_), channel_id=1, source_target_pairs={{1,0},{0,1},{3,2},{2,3},{5,4},{4,5},{7,6},{6,7},{9,8},{8,9},{11,10... | collective-permute-start | bytes 3244040 | tf_op jit(solution)/shard_map/ppermute | solution.py:172
  91.5 5.1 %collective-permute-done.5.refs_11_ = bf16[31,128,128]{2,1,0:T(8,128)(2,1)S(1)} collective-permute-done((bf16[31,128,128]{2,1,0:T(8,128)(2,1)}, bf16[31,128,128]{2,1,0:T(8,128)(2,1)S(1)}, u32[]{:S(2)}, u32[]{:S(2)}) %collective-permute-start.5) | collective-permute-done | bytes 1015840 | tf_op jit(solution)/shard_map/ppermute | solution.py:172
  96.6 10.7 %collective-permute-done.7.refs_12_ = bf16[16,128,128]{2,1,0:T(8,128)(2,1)} collective-permute-done((bf16[16,128,128]{2,1,0:T(8,128)(2,1)S(1)}, bf16[16,128,128]{2,1,0:T(8,128)(2,1)}, u32[]{:S(2)}, u32[]{:S(2)}) %collective-permute-start.7) | collective-permute-done | bytes 524320 | tf_op jit(solution)/shard_map/ppermute | solution.py:172
  107.3 2.4 %collective-permute-start.15 = (bf16[16,128,128]{2,1,0:T(8,128)(2,1)}, bf16[16,128,128]{2,1,0:T(8,128)(2,1)}, u32[]{:S(2)}, u32[]{:S(2)}) collective-permute-start(bf16[16,128,128]{2,1,0:T(8,128)(2,1)} %collective-permute-done.7.refs_12_), channel_id=1, source_target_pairs={{128,0},{129,1},{130,2},{131,3},{132,4},{133,5},{134,6},{135,7},{3... | collective-permute-start | bytes 1572872 | tf_op jit(solution)/shard_map/ppermute | solution.py:172
  109.8 4.8 %collective-permute-start.11 = (bf16[31,128,128]{2,1,0:T(8,128)(2,1)}, bf16[31,128,128]{2,1,0:T(8,128)(2,1)S(1)}, u32[]{:S(2)}, u32[]{:S(2)}) collective-permute-start(bf16[31,128,128]{2,1,0:T(8,128)(2,1)} %copy-done.4), channel_id=1, source_target_pairs={{16,0},{17,1},{18,2},{19,3},{20,4},{21,5},{22,6},{23,7},{24,8},{25... | collective-permute-start | bytes 3047432 | tf_op jit(solution)/shard_map/ppermute | solution.py:172
  117.9 19.5 %collective-permute-done.15 = bf16[16,128,128]{2,1,0:T(8,128)(2,1)} collective-permute-done((bf16[16,128,128]{2,1,0:T(8,128)(2,1)}, bf16[16,128,128]{2,1,0:T(8,128)(2,1)}, u32[]{:S(2)}, u32[]{:S(2)}) %collective-permute-start.15) | collective-permute-done | bytes 524320 | tf_op jit(solution)/shard_map/ppermute | solution.py:172
  138.5 1.9 %collective-permute-start.16 = (bf16[16,128,128]{2,1,0:T(8,128)(2,1)S(1)}, bf16[16,128,128]{2,1,0:T(8,128)(2,1)S(1)}, u32[]{:S(2)}, u32[]{:S(2)}) collective-permute-start(bf16[16,128,128]{2,1,0:T(8,128)(2,1)S(1)} %broadcast_select_fusion), channel_id=1, source_target_pairs={{16,0},{17,1},{18,2},{19,3},{20,4},{21,5},{22,6},{23,7},{24,8},{25... | collective-permute-start | bytes 1572872 | tf_op jit(solution)/shard_map/ppermute | solution.py:172
  140.5 3.9 %collective-permute-start.14 = (bf16[18,128,128]{2,1,0:T(8,128)(2,1)S(1)}, bf16[18,128,128]{2,1,0:T(8,128)(2,1)S(1)}, u32[]{:S(2)}, u32[]{:S(2)}) collective-permute-start(bf16[18,128,128]{2,1,0:T(8,128)(2,1)S(1)} %collective-permute-done.13.refs_13_), channel_id=1, source_target_pairs={{496,0},{497,1},{498,2},{499,3},{500,4},{501,5},{502,6},{503,7},{2... | collective-permute-start | bytes 1769480 | tf_op jit(solution)/shard_map/ppermute | solution.py:172
  147.0 3.4 %shard_map.55.refs_14_ = f32[16,3,128,128]{3,2,1,0:T(8,128)S(1)} custom-call(s32[1]{0:T(128)} %constant.36.clone.1.refs_0_, s32[3,16]{1,0:T(4,128)S(1)} %bitcast.48, s32[2,16]{1,0:T(2,128)S(1)} %bitcast.50, s32[2,16]{1,0:T(2,128)S(1)} %bitcast_convert_fusion.1.refs_3_, s32[2,32]{1,0:T(2,128)S(1)} %bitcast.51, s32[2,32]{1,0:T(2,128)S(1)} %bitcast_convert_fusion.refs_5_, ...), custom_call_target="tpu_custom_call" | custom-call | flops 805306368 | bytes 12582912 | tf_op jit(solution)/shard_map/pallas_call | solution.py:96
  150.4 2.7 %collective-permute-done.16.refs_12_ = bf16[16,128,128]{2,1,0:T(8,128)(2,1)S(1)} collective-permute-done((bf16[16,128,128]{2,1,0:T(8,128)(2,1)S(1)}, bf16[16,128,128]{2,1,0:T(8,128)(2,1)S(1)}, u32[]{:S(2)}, u32[]{:S(2)}) %collective-permute-start.16) | collective-permute-done | bytes 524320 | tf_op jit(solution)/shard_map/ppermute | solution.py:172
  153.1 7.6 %collective-permute-done.14.refs_10_ = bf16[18,128,128]{2,1,0:T(8,128)(2,1)S(1)} collective-permute-done((bf16[18,128,128]{2,1,0:T(8,128)(2,1)S(1)}, bf16[18,128,128]{2,1,0:T(8,128)(2,1)S(1)}, u32[]{:S(2)}, u32[]{:S(2)}) %collective-permute-start.14) | collective-permute-done | bytes 589856 | tf_op jit(solution)/shard_map/ppermute | solution.py:172
  160.7 5.0 %shard_map.56 = bf16[16,3,128,128]{3,2,1,0:T(8,128)(2,1)} custom-call(s32[1]{0:T(128)} %bitcast.refs_0_, s32[3,16]{1,0:T(4,128)S(1)} %bitcast.49, s32[2,16]{1,0:T(2,128)S(1)} %get-tuple-element.20.refs_2_, s32[2,16]{1,0:T(2,128)S(1)} %get-tuple-element.19.refs_3_, s32[2,32]{1,0:T(2,128)S(1)} %bitcast_convert_fusion.2.refs_4_, s32[2,32]{1,0:T(2,128)S(1)} %fusion.2.refs_5_, ...), custom_call_target="tpu_custom_call" | custom-call | flops 805306368 | bytes 12582912 | tf_op jit(solution)/shard_map/pallas_call | solution.py:96
  (53 shorter events, 13.2 us)
Async XLA Ops:
  0.0 12.8 %copy-start.9 = (bf16[16,1,2,128,128]{4,3,2,1,0:T(8,128)(2,1)S(1)}, bf16[16,1,2,128,128]{4,3,2,1,0:T(8,128)(2,1)}, u32[]{:S(2)}) copy-start(bf16[16,1,2,128,128]{4,3,2,1,0:T(8,128)(2,1)} %param.5) | copy-start | bytes 3145732
  1.2 22.1 %collective-permute-start.1 = (bf16[16,128,128]{2,1,0:T(8,128)(2,1)S(1)}, bf16[16,128,128]{2,1,0:T(8,128)(2,1)}, u32[]{:S(2)}, u32[]{:S(2)}) collective-permute-start(bf16[16,128,128]{2,1,0:T(8,128)(2,1)S(1)} %bitcast.44), channel_id=1, source_target_pairs={{128,0},{129,1},{130,2},{131,3},{132,4},{133,5},{134,6},{135,7},{3... | collective-permute-start | bytes 1572872 | tf_op jit(solution)/shard_map/ppermute | solution.py:172
  13.0 40.2 %collective-permute-start.3 = (bf16[33,128,128]{2,1,0:T(8,128)(2,1)S(1)}, bf16[33,128,128]{2,1,0:T(8,128)(2,1)}, u32[]{:S(2)}, u32[]{:S(2)}) collective-permute-start(bf16[33,128,128]{2,1,0:T(8,128)(2,1)S(1)} %pad_maximum_fusion.refs_6_), channel_id=1, source_target_pairs={{2,0},{3,1},{4,2},{5,3},{6,4},{7,5},{8,6},{9,7},{10,8},{11,9},{12,... | collective-permute-start | bytes 3244040 | tf_op jit(solution)/shard_map/ppermute | solution.py:172
  16.0 34.6 %collective-permute-start = (bf16[31,128,128]{2,1,0:T(8,128)(2,1)S(1)}, bf16[31,128,128]{2,1,0:T(8,128)(2,1)}, u32[]{:S(2)}, u32[]{:S(2)}) collective-permute-start(bf16[31,128,128]{2,1,0:T(8,128)(2,1)S(1)} %pad_maximum_fusion.1.refs_8_), channel_id=1, source_target_pairs={{16,0},{17,1},{18,2},{19,3},{20,4},{21,5},{22,6},{23,7},{24,8},{25... | collective-permute-start | bytes 3047432 | tf_op jit(solution)/shard_map/ppermute | solution.py:172
  20.6 30.1 %collective-permute-start.4 = (bf16[18,128,128]{2,1,0:T(8,128)(2,1)S(1)}, bf16[18,128,128]{2,1,0:T(8,128)(2,1)}, u32[]{:S(2)}, u32[]{:S(2)}) collective-permute-start(bf16[18,128,128]{2,1,0:T(8,128)(2,1)S(1)} %bitcast.46), channel_id=1, source_target_pairs={{96,0},{97,1},{98,2},{99,3},{100,4},{101,5},{102,6},{103,7},{104,8... | collective-permute-start | bytes 1769480 | tf_op jit(solution)/shard_map/ppermute | solution.py:172
  24.4 85.4 %copy-start.10 = (s32[16,1,3]{0,1,2:T(1,128)S(1)}, s32[16,1,3]{0,1,2:T(1,128)}, u32[]{:S(2)}) copy-start(s32[16,1,3]{0,1,2:T(1,128)} %param.9) | copy-start | bytes 580
  24.4 28.7 %collective-permute-start.2 = (bf16[16,128,128]{2,1,0:T(8,128)(2,1)S(1)}, bf16[16,128,128]{2,1,0:T(8,128)(2,1)S(1)}, u32[]{:S(2)}, u32[]{:S(2)}) collective-permute-start(bf16[16,128,128]{2,1,0:T(8,128)(2,1)S(1)} %broadcast_select_fusion.2), channel_id=1, source_target_pairs={{16,0},{17,1},{18,2},{19,3},{20,4},{21,5},{22,6},{23,7},{24,8},{25... | collective-permute-start | bytes 1572872 | tf_op jit(solution)/shard_map/ppermute | solution.py:172
  53.1 38.3 %copy-start = (bf16[16,128,128]{2,1,0:T(8,128)(2,1)}, bf16[16,128,128]{2,1,0:T(8,128)(2,1)S(1)}, u32[]{:S(2)}) copy-start(bf16[16,128,128]{2,1,0:T(8,128)(2,1)S(1)} %collective-permute-done.2.refs_9_) | copy-start | bytes 1572868
  53.2 20.3 %collective-permute-start.6 = (bf16[16,128,128]{2,1,0:T(8,128)(2,1)S(1)}, bf16[16,128,128]{2,1,0:T(8,128)(2,1)S(1)}, u32[]{:S(2)}, u32[]{:S(2)}) collective-permute-start(bf16[16,128,128]{2,1,0:T(8,128)(2,1)S(1)} %collective-permute-done.2.refs_9_), channel_id=1, source_target_pairs={{128,0},{129,1},{130,2},{131,3},{132,4},{133,5},{134,6},{135,7},{3... | collective-permute-start | bytes 1572872 | tf_op jit(solution)/shard_map/ppermute | solution.py:172
  55.6 20.1 %collective-permute-start.9 = (bf16[18,128,128]{2,1,0:T(8,128)(2,1)}, bf16[18,128,128]{2,1,0:T(8,128)(2,1)}, u32[]{:S(2)}, u32[]{:S(2)}) collective-permute-start(bf16[18,128,128]{2,1,0:T(8,128)(2,1)} %collective-permute-done.4), channel_id=1, source_target_pairs={{96,0},{97,1},{98,2},{99,3},{100,4},{101,5},{102,6},{103,7},{104,8... | collective-permute-start | bytes 1769480 | tf_op jit(solution)/shard_map/ppermute | solution.py:172
  57.5 33.9 %collective-permute-start.8 = (bf16[33,128,128]{2,1,0:T(8,128)(2,1)S(1)}, bf16[33,128,128]{2,1,0:T(8,128)(2,1)S(1)}, u32[]{:S(2)}, u32[]{:S(2)}) collective-permute-start(bf16[33,128,128]{2,1,0:T(8,128)(2,1)S(1)} %pad_maximum_fusion.refs_6_), channel_id=1, source_target_pairs={{1,0},{4,1},{3,2},{6,3},{5,4},{8,5},{7,6},{10,7},{9,8},{12,9},{11,... | collective-permute-start | bytes 3244040 | tf_op jit(solution)/shard_map/ppermute | solution.py:172
  59.5 37.1 %collective-permute-start.5 = (bf16[31,128,128]{2,1,0:T(8,128)(2,1)}, bf16[31,128,128]{2,1,0:T(8,128)(2,1)S(1)}, u32[]{:S(2)}, u32[]{:S(2)}) collective-permute-start(bf16[31,128,128]{2,1,0:T(8,128)(2,1)} %collective-permute-done.refs_8_), channel_id=1, source_target_pairs={{16,0},{17,1},{18,2},{19,3},{20,4},{21,5},{22,6},{23,7},{24,8},{25... | collective-permute-start | bytes 3047432 | tf_op jit(solution)/shard_map/ppermute | solution.py:172
  73.6 72.2 %copy-start.6 = (s32[16,1,2]{0,2,1:T(2,128)S(1)}, s32[16,1,2]{0,2,1:T(2,128)}, u32[]{:S(2)}) copy-start(s32[16,1,2]{0,2,1:T(2,128)} %param.6) | copy-start | bytes 388
  73.6 33.7 %collective-permute-start.7 = (bf16[16,128,128]{2,1,0:T(8,128)(2,1)S(1)}, bf16[16,128,128]{2,1,0:T(8,128)(2,1)}, u32[]{:S(2)}, u32[]{:S(2)}) collective-permute-start(bf16[16,128,128]{2,1,0:T(8,128)(2,1)S(1)} %broadcast_select_fusion.1), channel_id=1, source_target_pairs={{16,0},{17,1},{18,2},{19,3},{20,4},{21,5},{22,6},{23,7},{24,8},{25... | collective-permute-start | bytes 1572872 | tf_op jit(solution)/shard_map/ppermute | solution.py:172
  75.7 38.9 %collective-permute-start.12 = (bf16[18,128,128]{2,1,0:T(8,128)(2,1)}, bf16[18,128,128]{2,1,0:T(8,128)(2,1)}, u32[]{:S(2)}, u32[]{:S(2)}) collective-permute-start(bf16[18,128,128]{2,1,0:T(8,128)(2,1)} %collective-permute-done.9), channel_id=1, source_target_pairs={{112,0},{113,1},{114,2},{115,3},{116,4},{117,5},{118,6},{119,7},{1... | collective-permute-start | bytes 1769480 | tf_op jit(solution)/shard_map/ppermute | solution.py:172
  89.5 55.6 %collective-permute-start.10 = (bf16[33,128,128]{2,1,0:T(8,128)(2,1)}, bf16[33,128,128]{2,1,0:T(8,128)(2,1)}, u32[]{:S(2)}, u32[]{:S(2)}) collective-permute-start(bf16[33,128,128]{2,1,0:T(8,128)(2,1)} %collective-permute-done.3.refs_7_), channel_id=1, source_target_pairs={{1,0},{0,1},{3,2},{2,3},{5,4},{4,5},{7,6},{6,7},{9,8},{8,9},{11,10... | collective-permute-start | bytes 3244040 | tf_op jit(solution)/shard_map/ppermute | solution.py:172
  96.6 10.7 %copy-start.4 = (bf16[31,128,128]{2,1,0:T(8,128)(2,1)}, bf16[31,128,128]{2,1,0:T(8,128)(2,1)S(1)}, u32[]{:S(2)}) copy-start(bf16[31,128,128]{2,1,0:T(8,128)(2,1)S(1)} %collective-permute-done.5.refs_11_) | copy-start | bytes 3047428
  107.3 30.1 %collective-permute-start.15 = (bf16[16,128,128]{2,1,0:T(8,128)(2,1)}, bf16[16,128,128]{2,1,0:T(8,128)(2,1)}, u32[]{:S(2)}, u32[]{:S(2)}) collective-permute-start(bf16[16,128,128]{2,1,0:T(8,128)(2,1)} %collective-permute-done.7.refs_12_), channel_id=1, source_target_pairs={{128,0},{129,1},{130,2},{131,3},{132,4},{133,5},{134,6},{135,7},{3... | collective-permute-start | bytes 1572872 | tf_op jit(solution)/shard_map/ppermute | solution.py:172
  109.8 35.3 %copy-start.3 = (bf16[33,128,128]{2,1,0:T(8,128)(2,1)S(1)}, bf16[33,128,128]{2,1,0:T(8,128)(2,1)}, u32[]{:S(2)}) copy-start(bf16[33,128,128]{2,1,0:T(8,128)(2,1)} %copy-done.2) | copy-start | bytes 3244036
  109.8 40.6 %collective-permute-start.11 = (bf16[31,128,128]{2,1,0:T(8,128)(2,1)}, bf16[31,128,128]{2,1,0:T(8,128)(2,1)S(1)}, u32[]{:S(2)}, u32[]{:S(2)}) collective-permute-start(bf16[31,128,128]{2,1,0:T(8,128)(2,1)} %copy-done.4), channel_id=1, source_target_pairs={{16,0},{17,1},{18,2},{19,3},{20,4},{21,5},{22,6},{23,7},{24,8},{25... | collective-permute-start | bytes 3047432 | tf_op jit(solution)/shard_map/ppermute | solution.py:172
  114.6 25.9 %collective-permute-start.13 = (bf16[18,128,128]{2,1,0:T(8,128)(2,1)}, bf16[18,128,128]{2,1,0:T(8,128)(2,1)S(1)}, u32[]{:S(2)}, u32[]{:S(2)}) collective-permute-start(bf16[18,128,128]{2,1,0:T(8,128)(2,1)} %collective-permute-done.12.refs_13_), channel_id=1, source_target_pairs={{496,0},{497,1},{498,2},{499,3},{500,4},{501,5},{502,6},{503,7},{2... | collective-permute-start | bytes 1769480 | tf_op jit(solution)/shard_map/ppermute | solution.py:172
  138.5 14.5 %collective-permute-start.16 = (bf16[16,128,128]{2,1,0:T(8,128)(2,1)S(1)}, bf16[16,128,128]{2,1,0:T(8,128)(2,1)S(1)}, u32[]{:S(2)}, u32[]{:S(2)}) collective-permute-start(bf16[16,128,128]{2,1,0:T(8,128)(2,1)S(1)} %broadcast_select_fusion), channel_id=1, source_target_pairs={{16,0},{17,1},{18,2},{19,3},{20,4},{21,5},{22,6},{23,7},{24,8},{25... | collective-permute-start | bytes 1572872 | tf_op jit(solution)/shard_map/ppermute | solution.py:172
  140.5 20.2 %collective-permute-start.14 = (bf16[18,128,128]{2,1,0:T(8,128)(2,1)S(1)}, bf16[18,128,128]{2,1,0:T(8,128)(2,1)S(1)}, u32[]{:S(2)}, u32[]{:S(2)}) collective-permute-start(bf16[18,128,128]{2,1,0:T(8,128)(2,1)S(1)} %collective-permute-done.13.refs_13_), channel_id=1, source_target_pairs={{496,0},{497,1},{498,2},{499,3},{500,4},{501,5},{502,6},{503,7},{2... | collective-permute-start | bytes 1769480 | tf_op jit(solution)/shard_map/ppermute | solution.py:172
  147.0 13.7 %copy-start.1 = (bf16[16,128,128]{2,1,0:T(8,128)(2,1)S(1)}, bf16[16,128,128]{2,1,0:T(8,128)(2,1)}, u32[]{:S(2)}) copy-start(bf16[16,128,128]{2,1,0:T(8,128)(2,1)} %copy-done) | copy-start | bytes 1572868
  (5 other events, 16.9 us)

commit v9 on v7

--- a/solution.py
+++ b/solution.py
@@ -60,7 +60,7 @@
         for copy in copies[slot]:
             copy.wait()
 
-        @pl.loop(0, rows, unroll=8)
+        @pl.loop(0, rows, unroll=16)
         def _(i):
             left = jnp.concatenate([a[slot, 2 * i], a[slot, 2 * i + 1]], axis=1)
             right = []
@@ -197,8 +197,9 @@
     some.append(inside(some[1]))
     most[2], some[2], _ = lax.optimization_barrier((most[2], some[2], up_two))
     most.append(send(most[2], paths.down))
-    some.append(inside(some[2]))
-    second = send(third, paths.up)
+    some.append(send(some[2], paths.down))
+    later, _ = lax.optimization_barrier((third, most[2]))
+    second = send(later, paths.up)
     first = send(second, paths.up)
     parts = list(zip(most, some, [rest, first, second, third]))
 

time: 160 us -> 154 us (0.963)
  the two profiles are of different devices: /device:TPU:6 before, /device:TPU:56 now
where the time goes in v9:
time: 154 us; the launch traced here: 153 us
  waiting for transfers between devices  78.8 us (51%)
  starting transfers between devices  61.3 us (40%)
  Pallas kernels  8.47 us (6%)
  other arithmetic  3.09 us (2%)
    ppermute x16, waiting for transfers between devices, local(): send = lambda value, pairs: lax.ppermute(value, AXES, pairs)  78.8 us
    ppermute x16, starting transfers between devices, local(): send = lambda value, pairs: lax.ppermute(value, AXES, pairs)  61.3 us
    pallas_call x2, Pallas kernels, contribute(): pl.pallas_call(functools.partial(block_kernel, first, flip is not None, c...  8.47 us
  transfers between devices with their start and end apart: 16, of which 10 were waited for; matrix products, arithmetic and copies ran while one was open for 2% of the time, Pallas kernels for 2%

profile of v9, /device:TPU:56, one launch (start us, length us, event | category | flops | bytes accessed | tf_op | source)
XLA Modules:
  0.0 153.4 jit_solution(17206461698765070528)
XLA Ops:
  3.1 6.6 %collective-permute-start.1 = (bf16[33,128,128]{2,1,0:T(8,128)(2,1)S(1)}, bf16[33,128,128]{2,1,0:T(8,128)(2,1)}, u32[]{:S(2)}, u32[]{:S(2)}) collective-permute-start(bf16[33,128,128]{2,1,0:T(8,128)(2,1)S(1)} %pad_maximum_fusion.refs_6_), channel_id=1, source_target_pairs={{2,0},{3,1},{4,2},{5,3},{6,4},{7,5},{8,6},{9,7},{10,8},{11,9},{12,... | collective-permute-start | bytes 3244040 | tf_op jit(solution)/shard_map/ppermute | solution.py:172
  9.8 3.3 %collective-permute-start.3 = (bf16[29,128,128]{2,1,0:T(8,128)(2,1)S(1)}, bf16[29,128,128]{2,1,0:T(8,128)(2,1)}, u32[]{:S(2)}, u32[]{:S(2)}) collective-permute-start(bf16[29,128,128]{2,1,0:T(8,128)(2,1)S(1)} %pad_maximum_fusion.1.refs_8_), channel_id=1, source_target_pairs={{16,0},{17,1},{18,2},{19,3},{20,4},{21,5},{22,6},{23,7},{24,8},{25... | collective-permute-start | bytes 2850824 | tf_op jit(solution)/shard_map/ppermute | solution.py:172
  13.1 6.7 %collective-permute-start.6 = (bf16[18,128,128]{2,1,0:T(8,128)(2,1)S(1)}, bf16[18,128,128]{2,1,0:T(8,128)(2,1)}, u32[]{:S(2)}, u32[]{:S(2)}) collective-permute-start(bf16[18,128,128]{2,1,0:T(8,128)(2,1)S(1)} %bitcast.46), channel_id=1, source_target_pairs={{96,0},{97,1},{98,2},{99,3},{100,4},{101,5},{102,6},{103,7},{104,8... | collective-permute-start | bytes 1769480 | tf_op jit(solution)/shard_map/ppermute | solution.py:172
  20.0 8.0 %collective-permute-start.5 = (bf16[18,128,128]{2,1,0:T(8,128)(2,1)S(1)}, bf16[18,128,128]{2,1,0:T(8,128)(2,1)S(1)}, u32[]{:S(2)}, u32[]{:S(2)}) collective-permute-start(bf16[18,128,128]{2,1,0:T(8,128)(2,1)S(1)} %broadcast_select_fusion.1), channel_id=1, source_target_pairs={{16,0},{17,1},{18,2},{19,3},{20,4},{21,5},{22,6},{23,7},{24,8},{25... | collective-permute-start | bytes 1769480 | tf_op jit(solution)/shard_map/ppermute | solution.py:172
  28.0 5.9 %collective-permute-done.6 = bf16[18,128,128]{2,1,0:T(8,128)(2,1)} collective-permute-done((bf16[18,128,128]{2,1,0:T(8,128)(2,1)S(1)}, bf16[18,128,128]{2,1,0:T(8,128)(2,1)}, u32[]{:S(2)}, u32[]{:S(2)}) %collective-permute-start.6) | collective-permute-done | bytes 589856 | tf_op jit(solution)/shard_map/ppermute | solution.py:172
  33.9 8.2 %collective-permute-done.3.refs_8_ = bf16[29,128,128]{2,1,0:T(8,128)(2,1)} collective-permute-done((bf16[29,128,128]{2,1,0:T(8,128)(2,1)S(1)}, bf16[29,128,128]{2,1,0:T(8,128)(2,1)}, u32[]{:S(2)}, u32[]{:S(2)}) %collective-permute-start.3) | collective-permute-done | bytes 950304 | tf_op jit(solution)/shard_map/ppermute | solution.py:172
  42.1 11.0 %collective-permute-done.1.refs_7_ = bf16[33,128,128]{2,1,0:T(8,128)(2,1)} collective-permute-done((bf16[33,128,128]{2,1,0:T(8,128)(2,1)S(1)}, bf16[33,128,128]{2,1,0:T(8,128)(2,1)}, u32[]{:S(2)}, u32[]{:S(2)}) %collective-permute-start.1) | collective-permute-done | bytes 1081376 | tf_op jit(solution)/shard_map/ppermute | solution.py:172
  53.2 2.5 %collective-permute-done.5.refs_9_ = bf16[18,128,128]{2,1,0:T(8,128)(2,1)S(1)} collective-permute-done((bf16[18,128,128]{2,1,0:T(8,128)(2,1)S(1)}, bf16[18,128,128]{2,1,0:T(8,128)(2,1)S(1)}, u32[]{:S(2)}, u32[]{:S(2)}) %collective-permute-start.5) | collective-permute-done | bytes 589856 | tf_op jit(solution)/shard_map/ppermute | solution.py:172
  56.4 1.9 %collective-permute-start.10 = (bf16[18,128,128]{2,1,0:T(8,128)(2,1)}, bf16[18,128,128]{2,1,0:T(8,128)(2,1)S(1)}, u32[]{:S(2)}, u32[]{:S(2)}) collective-permute-start(bf16[18,128,128]{2,1,0:T(8,128)(2,1)} %collective-permute-done.6), channel_id=1, source_target_pairs={{96,0},{97,1},{98,2},{99,3},{100,4},{101,5},{102,6},{103,7},{104,8... | collective-permute-start | bytes 1769480 | tf_op jit(solution)/shard_map/ppermute | solution.py:172
  58.3 4.7 %collective-permute-start.7 = (bf16[29,128,128]{2,1,0:T(8,128)(2,1)}, bf16[29,128,128]{2,1,0:T(8,128)(2,1)}, u32[]{:S(2)}, u32[]{:S(2)}) collective-permute-start(bf16[29,128,128]{2,1,0:T(8,128)(2,1)} %collective-permute-done.3.refs_8_), channel_id=1, source_target_pairs={{16,0},{17,1},{18,2},{19,3},{20,4},{21,5},{22,6},{23,7},{24,8},{25... | collective-permute-start | bytes 2850824 | tf_op jit(solution)/shard_map/ppermute | solution.py:172
  63.0 2.7 %collective-permute-start.9 = (bf16[18,128,128]{2,1,0:T(8,128)(2,1)S(1)}, bf16[18,128,128]{2,1,0:T(8,128)(2,1)}, u32[]{:S(2)}, u32[]{:S(2)}) collective-permute-start(bf16[18,128,128]{2,1,0:T(8,128)(2,1)S(1)} %broadcast_select_fusion), channel_id=1, source_target_pairs={{16,0},{17,1},{18,2},{19,3},{20,4},{21,5},{22,6},{23,7},{24,8},{25... | collective-permute-start | bytes 1769480 | tf_op jit(solution)/shard_map/ppermute | solution.py:172
  65.7 19.8 %collective-permute-done.10 = bf16[18,128,128]{2,1,0:T(8,128)(2,1)S(1)} collective-permute-done((bf16[18,128,128]{2,1,0:T(8,128)(2,1)}, bf16[18,128,128]{2,1,0:T(8,128)(2,1)S(1)}, u32[]{:S(2)}, u32[]{:S(2)}) %collective-permute-start.10) | collective-permute-done | bytes 589856 | tf_op jit(solution)/shard_map/ppermute | solution.py:172
  85.5 1.9 %collective-permute-start.12 = (bf16[18,128,128]{2,1,0:T(8,128)(2,1)S(1)}, bf16[18,128,128]{2,1,0:T(8,128)(2,1)}, u32[]{:S(2)}, u32[]{:S(2)}) collective-permute-start(bf16[18,128,128]{2,1,0:T(8,128)(2,1)S(1)} %collective-permute-done.10), channel_id=1, source_target_pairs={{112,0},{113,1},{114,2},{115,3},{116,4},{117,5},{118,6},{119,7},{1... | collective-permute-start | bytes 1769480 | tf_op jit(solution)/shard_map/ppermute | solution.py:172
  87.4 2.8 %collective-permute-start = (bf16[33,128,128]{2,1,0:T(8,128)(2,1)S(1)}, bf16[33,128,128]{2,1,0:T(8,128)(2,1)}, u32[]{:S(2)}, u32[]{:S(2)}) collective-permute-start(bf16[33,128,128]{2,1,0:T(8,128)(2,1)S(1)} %pad_maximum_fusion.refs_6_), channel_id=1, source_target_pairs={{1,0},{4,1},{3,2},{6,3},{5,4},{8,5},{7,6},{10,7},{9,8},{12,9},{11,... | collective-permute-start | bytes 3244040 | tf_op jit(solution)/shard_map/ppermute | solution.py:172
  90.2 1.9 %collective-permute-start.2 = (bf16[33,128,128]{2,1,0:T(8,128)(2,1)}, bf16[33,128,128]{2,1,0:T(8,128)(2,1)}, u32[]{:S(2)}, u32[]{:S(2)}) collective-permute-start(bf16[33,128,128]{2,1,0:T(8,128)(2,1)} %collective-permute-done.1.refs_7_), channel_id=1, source_target_pairs={{1,0},{0,1},{3,2},{2,3},{5,4},{4,5},{7,6},{6,7},{9,8},{8,9},{11,10... | collective-permute-start | bytes 3244040 | tf_op jit(solution)/shard_map/ppermute | solution.py:172
  92.2 9.2 %collective-permute-done.9.refs_12_ = bf16[18,128,128]{2,1,0:T(8,128)(2,1)} collective-permute-done((bf16[18,128,128]{2,1,0:T(8,128)(2,1)S(1)}, bf16[18,128,128]{2,1,0:T(8,128)(2,1)}, u32[]{:S(2)}, u32[]{:S(2)}) %collective-permute-start.9) | collective-permute-done | bytes 589856 | tf_op jit(solution)/shard_map/ppermute | solution.py:172
  102.2 7.5 %collective-permute-start.13 = (bf16[18,128,128]{2,1,0:T(8,128)(2,1)}, bf16[18,128,128]{2,1,0:T(8,128)(2,1)}, u32[]{:S(2)}, u32[]{:S(2)}) collective-permute-start(bf16[18,128,128]{2,1,0:T(8,128)(2,1)} %collective-permute-done.12.refs_13_), channel_id=1, source_target_pairs={{496,0},{497,1},{498,2},{499,3},{500,4},{501,5},{502,6},{503,7},{2... | collective-permute-start | bytes 1769480 | tf_op jit(solution)/shard_map/ppermute | solution.py:172
  109.7 1.9 %collective-permute-start.11 = (bf16[29,128,128]{2,1,0:T(8,128)(2,1)}, bf16[29,128,128]{2,1,0:T(8,128)(2,1)S(1)}, u32[]{:S(2)}, u32[]{:S(2)}) collective-permute-start(bf16[29,128,128]{2,1,0:T(8,128)(2,1)} %collective-permute-done.7.refs_11_), channel_id=1, source_target_pairs={{16,0},{17,1},{18,2},{19,3},{20,4},{21,5},{22,6},{23,7},{24,8},{25... | collective-permute-start | bytes 2850824 | tf_op jit(solution)/shard_map/ppermute | solution.py:172
  114.9 6.2 %collective-permute-done.13.refs_13_ = bf16[18,128,128]{2,1,0:T(8,128)(2,1)} collective-permute-done((bf16[18,128,128]{2,1,0:T(8,128)(2,1)}, bf16[18,128,128]{2,1,0:T(8,128)(2,1)}, u32[]{:S(2)}, u32[]{:S(2)}) %collective-permute-start.13) | collective-permute-done | bytes 589856 | tf_op jit(solution)/shard_map/ppermute | solution.py:172
  121.1 7.4 %collective-permute-start.14 = (bf16[18,128,128]{2,1,0:T(8,128)(2,1)}, bf16[18,128,128]{2,1,0:T(8,128)(2,1)S(1)}, u32[]{:S(2)}, u32[]{:S(2)}) collective-permute-start(bf16[18,128,128]{2,1,0:T(8,128)(2,1)} %collective-permute-done.13.refs_13_), channel_id=1, source_target_pairs={{496,0},{497,1},{498,2},{499,3},{500,4},{501,5},{502,6},{503,7},{2... | collective-permute-start | bytes 1769480 | tf_op jit(solution)/shard_map/ppermute | solution.py:172
  129.9 3.5 %shard_map.55.refs_14_ = f32[16,3,128,128]{3,2,1,0:T(8,128)S(1)} custom-call(s32[1]{0:T(128)} %constant.36.clone.1.refs_0_, s32[3,16]{1,0:T(4,128)S(1)} %bitcast.48, s32[2,16]{1,0:T(2,128)S(1)} %bitcast.50, s32[2,16]{1,0:T(2,128)S(1)} %bitcast_convert_fusion.1.refs_3_, s32[2,32]{1,0:T(2,128)S(1)} %bitcast.51, s32[2,32]{1,0:T(2,128)S(1)} %bitcast_convert_fusion.refs_5_, ...), custom_call_target="tpu_custom_call" | custom-call | flops 805306368 | bytes 12582912 | tf_op jit(solution)/shard_map/pallas_call | solution.py:96
  133.4 5.4 %collective-permute-done.11.refs_11_ = bf16[29,128,128]{2,1,0:T(8,128)(2,1)S(1)} collective-permute-done((bf16[29,128,128]{2,1,0:T(8,128)(2,1)}, bf16[29,128,128]{2,1,0:T(8,128)(2,1)S(1)}, u32[]{:S(2)}, u32[]{:S(2)}) %collective-permute-start.11) | collective-permute-done | bytes 950304 | tf_op jit(solution)/shard_map/ppermute | solution.py:172
  138.8 9.7 %collective-permute-done.15.refs_12_ = bf16[18,128,128]{2,1,0:T(8,128)(2,1)S(1)} collective-permute-done((bf16[18,128,128]{2,1,0:T(8,128)(2,1)}, bf16[18,128,128]{2,1,0:T(8,128)(2,1)S(1)}, u32[]{:S(2)}, u32[]{:S(2)}) %collective-permute-start.15) | collective-permute-done | bytes 589856 | tf_op jit(solution)/shard_map/ppermute | solution.py:172
  148.5 4.9 %shard_map.56 = bf16[16,3,128,128]{3,2,1,0:T(8,128)(2,1)} custom-call(s32[1]{0:T(128)} %bitcast.refs_0_, s32[3,16]{1,0:T(4,128)S(1)} %bitcast.49, s32[2,16]{1,0:T(2,128)S(1)} %get-tuple-element.20.refs_2_, s32[2,16]{1,0:T(2,128)S(1)} %get-tuple-element.19.refs_3_, s32[2,32]{1,0:T(2,128)S(1)} %bitcast_convert_fusion.2.refs_4_, s32[2,32]{1,0:T(2,128)S(1)} %fusion.2.refs_5_, ...), custom_call_target="tpu_custom_call" | custom-call | flops 805306368 | bytes 12582912 | tf_op jit(solution)/shard_map/pallas_call | solution.py:96
  (39 shorter events, 9.5 us)
Async XLA Ops:
  0.0 2.9 %copy-start.2 = (s32[16,1,2]{0,2,1:T(2,128)S(1)}, s32[16,1,2]{0,2,1:T(2,128)}, u32[]{:S(2)}) copy-start(s32[16,1,2]{0,2,1:T(2,128)} %param.6) | copy-start | bytes 388
  0.0 2.9 %copy-start.4 = (bf16[16,1,2,128,128]{4,3,2,1,0:T(8,128)(2,1)S(1)}, bf16[16,1,2,128,128]{4,3,2,1,0:T(8,128)(2,1)}, u32[]{:S(2)}) copy-start(bf16[16,1,2,128,128]{4,3,2,1,0:T(8,128)(2,1)} %param.5) | copy-start | bytes 3145732
  1.4 18.4 %collective-permute-start.4 = (bf16[18,128,128]{2,1,0:T(8,128)(2,1)S(1)}, bf16[18,128,128]{2,1,0:T(8,128)(2,1)}, u32[]{:S(2)}, u32[]{:S(2)}) collective-permute-start(bf16[18,128,128]{2,1,0:T(8,128)(2,1)S(1)} %bitcast.44), channel_id=1, source_target_pairs={{128,0},{129,1},{130,2},{131,3},{132,4},{133,5},{134,6},{135,7},{3... | collective-permute-start | bytes 1769480 | tf_op jit(solution)/shard_map/ppermute | solution.py:172
  3.1 6.6 %copy-start.3 = (s32[1,32,2]{1,2,0:T(2,128)S(1)}, s32[1,32,2]{1,2,0:T(2,128)}, u32[]{:S(2)}) copy-start(s32[1,32,2]{1,2,0:T(2,128)} %param.8) | copy-start | bytes 772
  3.1 6.7 %slice-start = ((bf16[1,32,2,128,128]{4,3,2,1,0:T(8,128)(2,1)}), bf16[1,14,2,128,128]{4,3,2,1,0:T(8,128)(2,1)S(1)}, s32[]{:S(2)}) async-start(bf16[1,32,2,128,128]{4,3,2,1,0:T(8,128)(2,1)} %param.7), calls=%async_computation | async-start | bytes 1835008 | tf_op jit(solution)/shard_map/slice | solution.py:183
  3.1 50.1 %collective-permute-start.1 = (bf16[33,128,128]{2,1,0:T(8,128)(2,1)S(1)}, bf16[33,128,128]{2,1,0:T(8,128)(2,1)}, u32[]{:S(2)}, u32[]{:S(2)}) collective-permute-start(bf16[33,128,128]{2,1,0:T(8,128)(2,1)S(1)} %pad_maximum_fusion.refs_6_), channel_id=1, source_target_pairs={{2,0},{3,1},{4,2},{5,3},{6,4},{7,5},{8,6},{9,7},{10,8},{11,9},{12,... | collective-permute-start | bytes 3244040 | tf_op jit(solution)/shard_map/ppermute | solution.py:172
  9.8 32.3 %collective-permute-start.3 = (bf16[29,128,128]{2,1,0:T(8,128)(2,1)S(1)}, bf16[29,128,128]{2,1,0:T(8,128)(2,1)}, u32[]{:S(2)}, u32[]{:S(2)}) collective-permute-start(bf16[29,128,128]{2,1,0:T(8,128)(2,1)S(1)} %pad_maximum_fusion.1.refs_8_), channel_id=1, source_target_pairs={{16,0},{17,1},{18,2},{19,3},{20,4},{21,5},{22,6},{23,7},{24,8},{25... | collective-permute-start | bytes 2850824 | tf_op jit(solution)/shard_map/ppermute | solution.py:172
  13.1 20.8 %collective-permute-start.6 = (bf16[18,128,128]{2,1,0:T(8,128)(2,1)S(1)}, bf16[18,128,128]{2,1,0:T(8,128)(2,1)}, u32[]{:S(2)}, u32[]{:S(2)}) collective-permute-start(bf16[18,128,128]{2,1,0:T(8,128)(2,1)S(1)} %bitcast.46), channel_id=1, source_target_pairs={{96,0},{97,1},{98,2},{99,3},{100,4},{101,5},{102,6},{103,7},{104,8... | collective-permute-start | bytes 1769480 | tf_op jit(solution)/shard_map/ppermute | solution.py:172
  19.9 89.7 %copy-start.5 = (s32[16,1,3]{0,1,2:T(1,128)S(1)}, s32[16,1,3]{0,1,2:T(1,128)}, u32[]{:S(2)}) copy-start(s32[16,1,3]{0,1,2:T(1,128)} %param.9) | copy-start | bytes 580
  20.0 35.7 %collective-permute-start.5 = (bf16[18,128,128]{2,1,0:T(8,128)(2,1)S(1)}, bf16[18,128,128]{2,1,0:T(8,128)(2,1)S(1)}, u32[]{:S(2)}, u32[]{:S(2)}) collective-permute-start(bf16[18,128,128]{2,1,0:T(8,128)(2,1)S(1)} %broadcast_select_fusion.1), channel_id=1, source_target_pairs={{16,0},{17,1},{18,2},{19,3},{20,4},{21,5},{22,6},{23,7},{24,8},{25... | collective-permute-start | bytes 1769480 | tf_op jit(solution)/shard_map/ppermute | solution.py:172
  55.7 29.8 %copy-start = (bf16[18,128,128]{2,1,0:T(8,128)(2,1)}, bf16[18,128,128]{2,1,0:T(8,128)(2,1)S(1)}, u32[]{:S(2)}) copy-start(bf16[18,128,128]{2,1,0:T(8,128)(2,1)S(1)} %collective-permute-done.5.refs_9_) | copy-start | bytes 1769476
  55.7 7.3 %collective-permute-start.8 = (bf16[18,128,128]{2,1,0:T(8,128)(2,1)S(1)}, bf16[18,128,128]{2,1,0:T(8,128)(2,1)S(1)}, u32[]{:S(2)}, u32[]{:S(2)}) collective-permute-start(bf16[18,128,128]{2,1,0:T(8,128)(2,1)S(1)} %collective-permute-done.5.refs_9_), channel_id=1, source_target_pairs={{128,0},{129,1},{130,2},{131,3},{132,4},{133,5},{134,6},{135,7},{3... | collective-permute-start | bytes 1769480 | tf_op jit(solution)/shard_map/ppermute | solution.py:172
  56.4 29.1 %collective-permute-start.10 = (bf16[18,128,128]{2,1,0:T(8,128)(2,1)}, bf16[18,128,128]{2,1,0:T(8,128)(2,1)S(1)}, u32[]{:S(2)}, u32[]{:S(2)}) collective-permute-start(bf16[18,128,128]{2,1,0:T(8,128)(2,1)} %collective-permute-done.6), channel_id=1, source_target_pairs={{96,0},{97,1},{98,2},{99,3},{100,4},{101,5},{102,6},{103,7},{104,8... | collective-permute-start | bytes 1769480 | tf_op jit(solution)/shard_map/ppermute | solution.py:172
  58.3 33.9 %collective-permute-start.7 = (bf16[29,128,128]{2,1,0:T(8,128)(2,1)}, bf16[29,128,128]{2,1,0:T(8,128)(2,1)}, u32[]{:S(2)}, u32[]{:S(2)}) collective-permute-start(bf16[29,128,128]{2,1,0:T(8,128)(2,1)} %collective-permute-done.3.refs_8_), channel_id=1, source_target_pairs={{16,0},{17,1},{18,2},{19,3},{20,4},{21,5},{22,6},{23,7},{24,8},{25... | collective-permute-start | bytes 2850824 | tf_op jit(solution)/shard_map/ppermute | solution.py:172
  63.0 38.3 %collective-permute-start.9 = (bf16[18,128,128]{2,1,0:T(8,128)(2,1)S(1)}, bf16[18,128,128]{2,1,0:T(8,128)(2,1)}, u32[]{:S(2)}, u32[]{:S(2)}) collective-permute-start(bf16[18,128,128]{2,1,0:T(8,128)(2,1)S(1)} %broadcast_select_fusion), channel_id=1, source_target_pairs={{16,0},{17,1},{18,2},{19,3},{20,4},{21,5},{22,6},{23,7},{24,8},{25... | collective-permute-start | bytes 1769480 | tf_op jit(solution)/shard_map/ppermute | solution.py:172
  85.5 16.7 %collective-permute-start.12 = (bf16[18,128,128]{2,1,0:T(8,128)(2,1)S(1)}, bf16[18,128,128]{2,1,0:T(8,128)(2,1)}, u32[]{:S(2)}, u32[]{:S(2)}) collective-permute-start(bf16[18,128,128]{2,1,0:T(8,128)(2,1)S(1)} %collective-permute-done.10), channel_id=1, source_target_pairs={{112,0},{113,1},{114,2},{115,3},{116,4},{117,5},{118,6},{119,7},{1... | collective-permute-start | bytes 1769480 | tf_op jit(solution)/shard_map/ppermute | solution.py:172
  87.4 41.1 %collective-permute-start = (bf16[33,128,128]{2,1,0:T(8,128)(2,1)S(1)}, bf16[33,128,128]{2,1,0:T(8,128)(2,1)}, u32[]{:S(2)}, u32[]{:S(2)}) collective-permute-start(bf16[33,128,128]{2,1,0:T(8,128)(2,1)S(1)} %pad_maximum_fusion.refs_6_), channel_id=1, source_target_pairs={{1,0},{4,1},{3,2},{6,3},{5,4},{8,5},{7,6},{10,7},{9,8},{12,9},{11,... | collective-permute-start | bytes 3244040 | tf_op jit(solution)/shard_map/ppermute | solution.py:172
  90.2 38.3 %collective-permute-start.2 = (bf16[33,128,128]{2,1,0:T(8,128)(2,1)}, bf16[33,128,128]{2,1,0:T(8,128)(2,1)}, u32[]{:S(2)}, u32[]{:S(2)}) collective-permute-start(bf16[33,128,128]{2,1,0:T(8,128)(2,1)} %collective-permute-done.1.refs_7_), channel_id=1, source_target_pairs={{1,0},{0,1},{3,2},{2,3},{5,4},{4,5},{7,6},{6,7},{9,8},{8,9},{11,10... | collective-permute-start | bytes 3244040 | tf_op jit(solution)/shard_map/ppermute | solution.py:172
  102.2 18.9 %collective-permute-start.13 = (bf16[18,128,128]{2,1,0:T(8,128)(2,1)}, bf16[18,128,128]{2,1,0:T(8,128)(2,1)}, u32[]{:S(2)}, u32[]{:S(2)}) collective-permute-start(bf16[18,128,128]{2,1,0:T(8,128)(2,1)} %collective-permute-done.12.refs_13_), channel_id=1, source_target_pairs={{496,0},{497,1},{498,2},{499,3},{500,4},{501,5},{502,6},{503,7},{2... | collective-permute-start | bytes 1769480 | tf_op jit(solution)/shard_map/ppermute | solution.py:172
  109.7 29.1 %collective-permute-start.11 = (bf16[29,128,128]{2,1,0:T(8,128)(2,1)}, bf16[29,128,128]{2,1,0:T(8,128)(2,1)S(1)}, u32[]{:S(2)}, u32[]{:S(2)}) collective-permute-start(bf16[29,128,128]{2,1,0:T(8,128)(2,1)} %collective-permute-done.7.refs_11_), channel_id=1, source_target_pairs={{16,0},{17,1},{18,2},{19,3},{20,4},{21,5},{22,6},{23,7},{24,8},{25... | collective-permute-start | bytes 2850824 | tf_op jit(solution)/shard_map/ppermute | solution.py:172
  113.0 35.5 %collective-permute-start.15 = (bf16[18,128,128]{2,1,0:T(8,128)(2,1)}, bf16[18,128,128]{2,1,0:T(8,128)(2,1)S(1)}, u32[]{:S(2)}, u32[]{:S(2)}) collective-permute-start(bf16[18,128,128]{2,1,0:T(8,128)(2,1)} %collective-permute-done.9.refs_12_), channel_id=1, source_target_pairs={{16,0},{17,1},{18,2},{19,3},{20,4},{21,5},{22,6},{23,7},{24,8},{25... | collective-permute-start | bytes 1769480 | tf_op jit(solution)/shard_map/ppermute | solution.py:172
  121.1 27.4 %collective-permute-start.14 = (bf16[18,128,128]{2,1,0:T(8,128)(2,1)}, bf16[18,128,128]{2,1,0:T(8,128)(2,1)S(1)}, u32[]{:S(2)}, u32[]{:S(2)}) collective-permute-start(bf16[18,128,128]{2,1,0:T(8,128)(2,1)} %collective-permute-done.13.refs_13_), channel_id=1, source_target_pairs={{496,0},{497,1},{498,2},{499,3},{500,4},{501,5},{502,6},{503,7},{2... | collective-permute-start | bytes 1769480 | tf_op jit(solution)/shard_map/ppermute | solution.py:172
  129.9 18.7 %copy-start.1 = (bf16[18,128,128]{2,1,0:T(8,128)(2,1)S(1)}, bf16[18,128,128]{2,1,0:T(8,128)(2,1)}, u32[]{:S(2)}) copy-start(bf16[18,128,128]{2,1,0:T(8,128)(2,1)} %copy-done) | copy-start | bytes 1769476

commit v10 on v9

--- a/solution.py
+++ b/solution.py
@@ -14,7 +14,7 @@
 CUTS = (28, 46)
 
 
-def block_kernel(first, flip, count, sizes, *refs):
+def block_kernel(first, flip, count, sizes, begins, *refs):
     flip_ref, cols, *rest = refs
     kas, kbs, rest = rest[:2], rest[2:4], rest[4:]
     lefts, rest = rest[:2], rest[2:]
@@ -33,7 +33,7 @@
         for n, size in enumerate(sizes):
             part = parts[slot * len(sizes) + n]
             copies[slot].append(
-                pltpu.make_async_copy(part.at[pl.ds(0, size)], held.at[pl.ds(at, size)], sems.at[slot, n])
+                pltpu.make_async_copy(part.at[pl.ds(begins[slot][n], size)], held.at[pl.ds(at, size)], sems.at[slot, n])
             )
             at += size
     if flip:
@@ -83,7 +83,7 @@
                     made_so_far[i, o] = value if first else value + total[i, o]
 
 
-def contribute(total, flip, cols, ka, kb, lefts, parts, sizes, last):
+def contribute(total, flip, cols, ka, kb, lefts, parts, sizes, begins, last):
     kept, rows = cols.shape
     block = lefts[0].shape[1:]
     count = sum(sizes)
@@ -94,7 +94,7 @@
     tall = (rows, kept) + block
     flat = [part for step in parts for part in step]
     return pl.pallas_call(
-        functools.partial(block_kernel, first, flip is not None, count, sizes),
+        functools.partial(block_kernel, first, flip is not None, count, sizes, begins),
         out_shape=jax.ShapeDtypeStruct(tall, jnp.bfloat16 if last else jnp.float32),
         in_specs=[smem] * 6 + [whole] * (2 + len(flat)) + ([] if first else [vmem]),
         out_specs=vmem,
@@ -126,8 +126,8 @@
     return jnp.concatenate([blocks, extra[None]], axis=0)
 
 
-def indices_of(blocks, shape):
-    return blocks[-1, : shape[0], : shape[1]].astype(jnp.int32)
+def indices_of(blocks, shape, at=-1):
+    return blocks[at, : shape[0], : shape[1]].astype(jnp.int32)
 
 
 class Paths:
@@ -196,8 +196,9 @@
     most.append(send(most[1], paths.down))
     some.append(inside(some[1]))
     most[2], some[2], _ = lax.optimization_barrier((most[2], some[2], up_two))
-    most.append(send(most[2], paths.down))
-    some.append(send(some[2], paths.down))
+    both = send(jnp.concatenate([most[2], some[2]], axis=0), paths.down)
+    most.append(both)
+    some.append(both)
     later, _ = lax.optimization_barrier((third, most[2]))
     second = send(later, paths.up)
     first = send(second, paths.up)
@@ -215,6 +216,7 @@
         [left, left_two],
         [parts[0], parts[2]],
         sizes,
+        ((0, 0, 0), (0, 0, 0)),
         False,
     )
     total = contribute(
@@ -222,10 +224,11 @@
         odd.reshape(1),
         cols,
         [ka_one, ka_three],
-        [rows_of(most[1]), rows_of(most[3])],
+        [rows_of(most[1]), indices_of(both, kb.shape, cut)],
         [left_odd, left_other],
         [parts[1], parts[3]],
         sizes,
+        ((0, 0, 0), (0, cut + 1, 0)),
         True,
     )
     return total[:, None]

time: 154 us -> 159 us (1.032)
  the two profiles are of different devices: /device:TPU:56 before, /device:TPU:6 now
where the time goes in v10:
time: 159 us; the launch traced here: 158 us
  waiting for transfers between devices  76.9 us (48%)
  starting transfers between devices  60.6 us (38%)
  Pallas kernels  8.32 us (5%)
  local copies, waits for them, and re-layouts  6 us (4%)
  other arithmetic  5.41 us (3%)
    ppermute x15, waiting for transfers between devices, local(): send = lambda value, pairs: lax.ppermute(value, AXES, pairs)  76.9 us
    ppermute x15, starting transfers between devices, local(): send = lambda value, pairs: lax.ppermute(value, AXES, pairs)  60.6 us
    pallas_call x2, Pallas kernels, contribute(): pl.pallas_call(functools.partial(block_kernel, first, flip is not None, c...  8.32 us
    unnamed x29, local copies, waits for them, and re-layouts  4.55 us
  transfers between devices with their start and end apart: 15, of which 8 were waited for; matrix products, arithmetic and copies ran while one was open for 3% of the time, Pallas kernels for 2%

profile of v10, /device:TPU:6, one launch (start us, length us, event | category | flops | bytes accessed | tf_op | source)
XLA Modules:
  0.0 157.6 jit_solution(3675549710145133962)
XLA Ops:
  1.4 10.9 %collective-permute-start.4 = (bf16[18,128,128]{2,1,0:T(8,128)(2,1)S(1)}, bf16[18,128,128]{2,1,0:T(8,128)(2,1)}, u32[]{:S(2)}, u32[]{:S(2)}) collective-permute-start(bf16[18,128,128]{2,1,0:T(8,128)(2,1)S(1)} %bitcast.44), channel_id=1, source_target_pairs={{128,0},{129,1},{130,2},{131,3},{132,4},{133,5},{134,6},{135,7},{3... | collective-permute-start | bytes 1769480 | tf_op jit(solution)/shard_map/ppermute | solution.py:172
  12.6 2.9 %collective-permute-start.1 = (bf16[33,128,128]{2,1,0:T(8,128)(2,1)S(1)}, bf16[33,128,128]{2,1,0:T(8,128)(2,1)}, u32[]{:S(2)}, u32[]{:S(2)}) collective-permute-start(bf16[33,128,128]{2,1,0:T(8,128)(2,1)S(1)} %pad_maximum_fusion.1.refs_6_), channel_id=1, source_target_pairs={{2,0},{3,1},{4,2},{5,3},{6,4},{7,5},{8,6},{9,7},{10,8},{11,9},{12,... | collective-permute-start | bytes 3244040 | tf_op jit(solution)/shard_map/ppermute | solution.py:172
  15.6 4.4 %collective-permute-start.3 = (bf16[29,128,128]{2,1,0:T(8,128)(2,1)S(1)}, bf16[29,128,128]{2,1,0:T(8,128)(2,1)}, u32[]{:S(2)}, u32[]{:S(2)}) collective-permute-start(bf16[29,128,128]{2,1,0:T(8,128)(2,1)S(1)} %pad_maximum_fusion.2.refs_8_), channel_id=1, source_target_pairs={{16,0},{17,1},{18,2},{19,3},{20,4},{21,5},{22,6},{23,7},{24,8},{25... | collective-permute-start | bytes 2850824 | tf_op jit(solution)/shard_map/ppermute | solution.py:172
  20.0 1.9 %collective-permute-start.6 = (bf16[18,128,128]{2,1,0:T(8,128)(2,1)S(1)}, bf16[18,128,128]{2,1,0:T(8,128)(2,1)}, u32[]{:S(2)}, u32[]{:S(2)}) collective-permute-start(bf16[18,128,128]{2,1,0:T(8,128)(2,1)S(1)} %bitcast.46), channel_id=1, source_target_pairs={{96,0},{97,1},{98,2},{99,3},{100,4},{101,5},{102,6},{103,7},{104,8... | collective-permute-start | bytes 1769480 | tf_op jit(solution)/shard_map/ppermute | solution.py:172
  21.9 3.0 %collective-permute-done.4 = bf16[18,128,128]{2,1,0:T(8,128)(2,1)} collective-permute-done((bf16[18,128,128]{2,1,0:T(8,128)(2,1)S(1)}, bf16[18,128,128]{2,1,0:T(8,128)(2,1)}, u32[]{:S(2)}, u32[]{:S(2)}) %collective-permute-start.4) | collective-permute-done | bytes 589856 | tf_op jit(solution)/shard_map/ppermute | solution.py:172
  26.1 1.9 %collective-permute-start.5 = (bf16[18,128,128]{2,1,0:T(8,128)(2,1)S(1)}, bf16[18,128,128]{2,1,0:T(8,128)(2,1)S(1)}, u32[]{:S(2)}, u32[]{:S(2)}) collective-permute-start(bf16[18,128,128]{2,1,0:T(8,128)(2,1)S(1)} %broadcast_select_fusion.1), channel_id=1, source_target_pairs={{16,0},{17,1},{18,2},{19,3},{20,4},{21,5},{22,6},{23,7},{24,8},{25... | collective-permute-start | bytes 1769480 | tf_op jit(solution)/shard_map/ppermute | solution.py:172
  28.0 22.0 %collective-permute-done.6 = bf16[18,128,128]{2,1,0:T(8,128)(2,1)} collective-permute-done((bf16[18,128,128]{2,1,0:T(8,128)(2,1)S(1)}, bf16[18,128,128]{2,1,0:T(8,128)(2,1)}, u32[]{:S(2)}, u32[]{:S(2)}) %collective-permute-start.6) | collective-permute-done | bytes 589856 | tf_op jit(solution)/shard_map/ppermute | solution.py:172
  50.1 2.6 %collective-permute-done.5.refs_9_ = bf16[18,128,128]{2,1,0:T(8,128)(2,1)S(1)} collective-permute-done((bf16[18,128,128]{2,1,0:T(8,128)(2,1)S(1)}, bf16[18,128,128]{2,1,0:T(8,128)(2,1)S(1)}, u32[]{:S(2)}, u32[]{:S(2)}) %collective-permute-start.5) | collective-permute-done | bytes 589856 | tf_op jit(solution)/shard_map/ppermute | solution.py:172
  52.6 2.4 %collective-permute-start.8 = (bf16[18,128,128]{2,1,0:T(8,128)(2,1)S(1)}, bf16[18,128,128]{2,1,0:T(8,128)(2,1)S(1)}, u32[]{:S(2)}, u32[]{:S(2)}) collective-permute-start(bf16[18,128,128]{2,1,0:T(8,128)(2,1)S(1)} %collective-permute-done.5.refs_9_), channel_id=1, source_target_pairs={{128,0},{129,1},{130,2},{131,3},{132,4},{133,5},{134,6},{135,7},{3... | collective-permute-start | bytes 1769480 | tf_op jit(solution)/shard_map/ppermute | solution.py:172
  55.1 12.8 %collective-permute-start.7 = (bf16[29,128,128]{2,1,0:T(8,128)(2,1)}, bf16[29,128,128]{2,1,0:T(8,128)(2,1)S(1)}, u32[]{:S(2)}, u32[]{:S(2)}) collective-permute-start(bf16[29,128,128]{2,1,0:T(8,128)(2,1)} %collective-permute-done.3.refs_8_), channel_id=1, source_target_pairs={{16,0},{17,1},{18,2},{19,3},{20,4},{21,5},{22,6},{23,7},{24,8},{25... | collective-permute-start | bytes 2850824 | tf_op jit(solution)/shard_map/ppermute | solution.py:172
  67.9 1.9 %collective-permute-start.10 = (bf16[18,128,128]{2,1,0:T(8,128)(2,1)}, bf16[18,128,128]{2,1,0:T(8,128)(2,1)S(1)}, u32[]{:S(2)}, u32[]{:S(2)}) collective-permute-start(bf16[18,128,128]{2,1,0:T(8,128)(2,1)} %collective-permute-done.6), channel_id=1, source_target_pairs={{96,0},{97,1},{98,2},{99,3},{100,4},{101,5},{102,6},{103,7},{104,8... | collective-permute-start | bytes 1769480 | tf_op jit(solution)/shard_map/ppermute | solution.py:172
  69.9 1.9 %collective-permute-start.9 = (bf16[18,128,128]{2,1,0:T(8,128)(2,1)S(1)}, bf16[18,128,128]{2,1,0:T(8,128)(2,1)S(1)}, u32[]{:S(2)}, u32[]{:S(2)}) collective-permute-start(bf16[18,128,128]{2,1,0:T(8,128)(2,1)S(1)} %broadcast_select_fusion), channel_id=1, source_target_pairs={{16,0},{17,1},{18,2},{19,3},{20,4},{21,5},{22,6},{23,7},{24,8},{25... | collective-permute-start | bytes 1769480 | tf_op jit(solution)/shard_map/ppermute | solution.py:172
  71.8 18.8 %collective-permute-done.10 = bf16[18,128,128]{2,1,0:T(8,128)(2,1)S(1)} collective-permute-done((bf16[18,128,128]{2,1,0:T(8,128)(2,1)}, bf16[18,128,128]{2,1,0:T(8,128)(2,1)S(1)}, u32[]{:S(2)}, u32[]{:S(2)}) %collective-permute-start.10) | collective-permute-done | bytes 589856 | tf_op jit(solution)/shard_map/ppermute | solution.py:172
  90.6 1.9 %collective-permute-start.12 = (bf16[18,128,128]{2,1,0:T(8,128)(2,1)S(1)}, bf16[18,128,128]{2,1,0:T(8,128)(2,1)}, u32[]{:S(2)}, u32[]{:S(2)}) collective-permute-start(bf16[18,128,128]{2,1,0:T(8,128)(2,1)S(1)} %collective-permute-done.10), channel_id=1, source_target_pairs={{112,0},{113,1},{114,2},{115,3},{116,4},{117,5},{118,6},{119,7},{1... | collective-permute-start | bytes 1769480 | tf_op jit(solution)/shard_map/ppermute | solution.py:172
  92.5 1.9 %collective-permute-start = (bf16[33,128,128]{2,1,0:T(8,128)(2,1)S(1)}, bf16[33,128,128]{2,1,0:T(8,128)(2,1)}, u32[]{:S(2)}, u32[]{:S(2)}) collective-permute-start(bf16[33,128,128]{2,1,0:T(8,128)(2,1)S(1)} %pad_maximum_fusion.1.refs_6_), channel_id=1, source_target_pairs={{1,0},{4,1},{3,2},{6,3},{5,4},{8,5},{7,6},{10,7},{9,8},{12,9},{11,... | collective-permute-start | bytes 3244040 | tf_op jit(solution)/shard_map/ppermute | solution.py:172
  94.4 2.4 %collective-permute-start.2 = (bf16[33,128,128]{2,1,0:T(8,128)(2,1)}, bf16[33,128,128]{2,1,0:T(8,128)(2,1)}, u32[]{:S(2)}, u32[]{:S(2)}) collective-permute-start(bf16[33,128,128]{2,1,0:T(8,128)(2,1)} %collective-permute-done.1.refs_7_), channel_id=1, source_target_pairs={{1,0},{0,1},{3,2},{2,3},{5,4},{4,5},{7,6},{6,7},{9,8},{8,9},{11,10... | collective-permute-start | bytes 3244040 | tf_op jit(solution)/shard_map/ppermute | solution.py:172
  96.9 3.2 %collective-permute-done.9.refs_12_ = bf16[18,128,128]{2,1,0:T(8,128)(2,1)S(1)} collective-permute-done((bf16[18,128,128]{2,1,0:T(8,128)(2,1)S(1)}, bf16[18,128,128]{2,1,0:T(8,128)(2,1)S(1)}, u32[]{:S(2)}, u32[]{:S(2)}) %collective-permute-start.9) | collective-permute-done | bytes 589856 | tf_op jit(solution)/shard_map/ppermute | solution.py:172
  101.5 9.4 %collective-permute-start.11 = (bf16[47,128,128]{2,1,0:T(8,128)(2,1)}, bf16[47,128,128]{2,1,0:T(8,128)(2,1)S(1)}, u32[]{:S(2)}, u32[]{:S(2)}) collective-permute-start(bf16[47,128,128]{2,1,0:T(8,128)(2,1)} %pad_maximum_fusion), channel_id=1, source_target_pairs={{16,0},{17,1},{18,2},{19,3},{20,4},{21,5},{22,6},{23,7},{24,8},{25... | collective-permute-start | bytes 4620296 | tf_op jit(solution)/shard_map/ppermute | solution.py:172
  110.9 1.9 %collective-permute-start.13 = (bf16[18,128,128]{2,1,0:T(8,128)(2,1)}, bf16[18,128,128]{2,1,0:T(8,128)(2,1)}, u32[]{:S(2)}, u32[]{:S(2)}) collective-permute-start(bf16[18,128,128]{2,1,0:T(8,128)(2,1)} %collective-permute-done.12.refs_13_), channel_id=1, source_target_pairs={{496,0},{497,1},{498,2},{499,3},{500,4},{501,5},{502,6},{503,7},{2... | collective-permute-start | bytes 1769480 | tf_op jit(solution)/shard_map/ppermute | solution.py:172
  114.2 18.1 %collective-permute-done.13.refs_13_ = bf16[18,128,128]{2,1,0:T(8,128)(2,1)} collective-permute-done((bf16[18,128,128]{2,1,0:T(8,128)(2,1)}, bf16[18,128,128]{2,1,0:T(8,128)(2,1)}, u32[]{:S(2)}, u32[]{:S(2)}) %collective-permute-start.13) | collective-permute-done | bytes 589856 | tf_op jit(solution)/shard_map/ppermute | solution.py:172
  132.3 1.9 %collective-permute-start.14 = (bf16[18,128,128]{2,1,0:T(8,128)(2,1)}, bf16[18,128,128]{2,1,0:T(8,128)(2,1)S(1)}, u32[]{:S(2)}, u32[]{:S(2)}) collective-permute-start(bf16[18,128,128]{2,1,0:T(8,128)(2,1)} %collective-permute-done.13.refs_13_), channel_id=1, source_target_pairs={{496,0},{497,1},{498,2},{499,3},{500,4},{501,5},{502,6},{503,7},{2... | collective-permute-start | bytes 1769480 | tf_op jit(solution)/shard_map/ppermute | solution.py:172
  140.1 3.4 %shard_map.55.refs_14_ = f32[16,3,128,128]{3,2,1,0:T(8,128)S(1)} custom-call(s32[1]{0:T(128)} %constant.36.clone.1.refs_0_, s32[3,16]{1,0:T(4,128)S(1)} %bitcast.48, s32[2,16]{1,0:T(2,128)S(1)} %bitcast.50, s32[2,16]{1,0:T(2,128)S(1)} %bitcast_convert_fusion.1.refs_3_, s32[2,32]{1,0:T(2,128)S(1)} %bitcast.51, s32[2,32]{1,0:T(2,128)S(1)} %bitcast_convert_fusion.refs_5_, ...), custom_call_target="tpu_custom_call" | custom-call | flops 805306368 | bytes 12582912 | tf_op jit(solution)/shard_map/pallas_call | solution.py:96
  144.3 8.4 %collective-permute-done.14.refs_10_ = bf16[18,128,128]{2,1,0:T(8,128)(2,1)S(1)} collective-permute-done((bf16[18,128,128]{2,1,0:T(8,128)(2,1)}, bf16[18,128,128]{2,1,0:T(8,128)(2,1)S(1)}, u32[]{:S(2)}, u32[]{:S(2)}) %collective-permute-start.14) | collective-permute-done | bytes 589856 | tf_op jit(solution)/shard_map/ppermute | solution.py:172
  152.7 4.9 %shard_map.56 = bf16[16,3,128,128]{3,2,1,0:T(8,128)(2,1)} custom-call(s32[1]{0:T(128)} %bitcast.refs_0_, s32[3,16]{1,0:T(4,128)S(1)} %bitcast.49, s32[2,16]{1,0:T(2,128)S(1)} %get-tuple-element.20.refs_2_, s32[2,16]{1,0:T(2,128)S(1)} %get-tuple-element.19.refs_3_, s32[2,32]{1,0:T(2,128)S(1)} %bitcast_convert_fusion.2.refs_4_, s32[2,32]{1,0:T(2,128)S(1)} %fusion.2.refs_5_, ...), custom_call_target="tpu_custom_call" | custom-call | flops 805306368 | bytes 12582912 | tf_op jit(solution)/shard_map/pallas_call | solution.py:96
  (54 shorter events, 12.2 us)
Async XLA Ops:
  0.0 12.4 %copy-start.10 = (s32[16,1,2]{0,2,1:T(2,128)S(1)}, s32[16,1,2]{0,2,1:T(2,128)}, u32[]{:S(2)}) copy-start(s32[16,1,2]{0,2,1:T(2,128)} %param.6) | copy-start | bytes 388
  0.0 12.4 %copy-start.12 = (bf16[16,1,2,128,128]{4,3,2,1,0:T(8,128)(2,1)S(1)}, bf16[16,1,2,128,128]{4,3,2,1,0:T(8,128)(2,1)}, u32[]{:S(2)}) copy-start(bf16[16,1,2,128,128]{4,3,2,1,0:T(8,128)(2,1)} %param.5) | copy-start | bytes 3145732
  1.4 18.5 %copy-start.4 = (bf16[1,9,2,128,128]{4,3,2,1,0:T(8,128)(2,1)}, bf16[1,9,2,128,128]{4,3,2,1,0:T(8,128)(2,1)S(1)}, u32[]{:S(2)}) copy-start(bf16[1,9,2,128,128]{4,3,2,1,0:T(8,128)(2,1)S(1)} %get-tuple-element.21) | copy-start | bytes 1769476
  1.4 23.5 %collective-permute-start.4 = (bf16[18,128,128]{2,1,0:T(8,128)(2,1)S(1)}, bf16[18,128,128]{2,1,0:T(8,128)(2,1)}, u32[]{:S(2)}, u32[]{:S(2)}) collective-permute-start(bf16[18,128,128]{2,1,0:T(8,128)(2,1)S(1)} %bitcast.44), channel_id=1, source_target_pairs={{128,0},{129,1},{130,2},{131,3},{132,4},{133,5},{134,6},{135,7},{3... | collective-permute-start | bytes 1769480 | tf_op jit(solution)/shard_map/ppermute | solution.py:172
  12.5 3.0 %slice-start = ((bf16[1,32,2,128,128]{4,3,2,1,0:T(8,128)(2,1)}), bf16[1,14,2,128,128]{4,3,2,1,0:T(8,128)(2,1)S(1)}, s32[]{:S(2)}) async-start(bf16[1,32,2,128,128]{4,3,2,1,0:T(8,128)(2,1)} %param.7), calls=%async_computation | async-start | bytes 1835008 | tf_op jit(solution)/shard_map/slice | solution.py:183
  12.6 37.5 %collective-permute-start.1 = (bf16[33,128,128]{2,1,0:T(8,128)(2,1)S(1)}, bf16[33,128,128]{2,1,0:T(8,128)(2,1)}, u32[]{:S(2)}, u32[]{:S(2)}) collective-permute-start(bf16[33,128,128]{2,1,0:T(8,128)(2,1)S(1)} %pad_maximum_fusion.1.refs_6_), channel_id=1, source_target_pairs={{2,0},{3,1},{4,2},{5,3},{6,4},{7,5},{8,6},{9,7},{10,8},{11,9},{12,... | collective-permute-start | bytes 3244040 | tf_op jit(solution)/shard_map/ppermute | solution.py:172
  15.6 54.3 %copy-start.2 = (bf16[29,128,128]{2,1,0:T(8,128)(2,1)}, bf16[29,128,128]{2,1,0:T(8,128)(2,1)S(1)}, u32[]{:S(2)}) copy-start(bf16[29,128,128]{2,1,0:T(8,128)(2,1)S(1)} %pad_maximum_fusion.2.refs_8_) | copy-start | bytes 2850820
  15.6 34.5 %collective-permute-start.3 = (bf16[29,128,128]{2,1,0:T(8,128)(2,1)S(1)}, bf16[29,128,128]{2,1,0:T(8,128)(2,1)}, u32[]{:S(2)}, u32[]{:S(2)}) collective-permute-start(bf16[29,128,128]{2,1,0:T(8,128)(2,1)S(1)} %pad_maximum_fusion.2.refs_8_), channel_id=1, source_target_pairs={{16,0},{17,1},{18,2},{19,3},{20,4},{21,5},{22,6},{23,7},{24,8},{25... | collective-permute-start | bytes 2850824 | tf_op jit(solution)/shard_map/ppermute | solution.py:172
  20.0 30.1 %collective-permute-start.6 = (bf16[18,128,128]{2,1,0:T(8,128)(2,1)S(1)}, bf16[18,128,128]{2,1,0:T(8,128)(2,1)}, u32[]{:S(2)}, u32[]{:S(2)}) collective-permute-start(bf16[18,128,128]{2,1,0:T(8,128)(2,1)S(1)} %bitcast.46), channel_id=1, source_target_pairs={{96,0},{97,1},{98,2},{99,3},{100,4},{101,5},{102,6},{103,7},{104,8... | collective-permute-start | bytes 1769480 | tf_op jit(solution)/shard_map/ppermute | solution.py:172
  26.1 26.5 %collective-permute-start.5 = (bf16[18,128,128]{2,1,0:T(8,128)(2,1)S(1)}, bf16[18,128,128]{2,1,0:T(8,128)(2,1)S(1)}, u32[]{:S(2)}, u32[]{:S(2)}) collective-permute-start(bf16[18,128,128]{2,1,0:T(8,128)(2,1)S(1)} %broadcast_select_fusion.1), channel_id=1, source_target_pairs={{16,0},{17,1},{18,2},{19,3},{20,4},{21,5},{22,6},{23,7},{24,8},{25... | collective-permute-start | bytes 1769480 | tf_op jit(solution)/shard_map/ppermute | solution.py:172
  52.6 44.2 %copy-start.6 = (bf16[18,128,128]{2,1,0:T(8,128)(2,1)}, bf16[18,128,128]{2,1,0:T(8,128)(2,1)S(1)}, u32[]{:S(2)}) copy-start(bf16[18,128,128]{2,1,0:T(8,128)(2,1)S(1)} %collective-permute-done.5.refs_9_) | copy-start | bytes 1769476
  52.6 17.2 %collective-permute-start.8 = (bf16[18,128,128]{2,1,0:T(8,128)(2,1)S(1)}, bf16[18,128,128]{2,1,0:T(8,128)(2,1)S(1)}, u32[]{:S(2)}, u32[]{:S(2)}) collective-permute-start(bf16[18,128,128]{2,1,0:T(8,128)(2,1)S(1)} %collective-permute-done.5.refs_9_), channel_id=1, source_target_pairs={{128,0},{129,1},{130,2},{131,3},{132,4},{133,5},{134,6},{135,7},{3... | collective-permute-start | bytes 1769480 | tf_op jit(solution)/shard_map/ppermute | solution.py:172
  55.1 41.8 %collective-permute-start.7 = (bf16[29,128,128]{2,1,0:T(8,128)(2,1)}, bf16[29,128,128]{2,1,0:T(8,128)(2,1)S(1)}, u32[]{:S(2)}, u32[]{:S(2)}) collective-permute-start(bf16[29,128,128]{2,1,0:T(8,128)(2,1)} %collective-permute-done.3.refs_8_), channel_id=1, source_target_pairs={{16,0},{17,1},{18,2},{19,3},{20,4},{21,5},{22,6},{23,7},{24,8},{25... | collective-permute-start | bytes 2850824 | tf_op jit(solution)/shard_map/ppermute | solution.py:172
  67.9 22.7 %collective-permute-start.10 = (bf16[18,128,128]{2,1,0:T(8,128)(2,1)}, bf16[18,128,128]{2,1,0:T(8,128)(2,1)S(1)}, u32[]{:S(2)}, u32[]{:S(2)}) collective-permute-start(bf16[18,128,128]{2,1,0:T(8,128)(2,1)} %collective-permute-done.6), channel_id=1, source_target_pairs={{96,0},{97,1},{98,2},{99,3},{100,4},{101,5},{102,6},{103,7},{104,8... | collective-permute-start | bytes 1769480 | tf_op jit(solution)/shard_map/ppermute | solution.py:172
  69.9 42.9 %copy-start.13 = (s32[16,1,3]{0,1,2:T(1,128)S(1)}, s32[16,1,3]{0,1,2:T(1,128)}, u32[]{:S(2)}) copy-start(s32[16,1,3]{0,1,2:T(1,128)} %param.9) | copy-start | bytes 580
  69.9 30.2 %collective-permute-start.9 = (bf16[18,128,128]{2,1,0:T(8,128)(2,1)S(1)}, bf16[18,128,128]{2,1,0:T(8,128)(2,1)S(1)}, u32[]{:S(2)}, u32[]{:S(2)}) collective-permute-start(bf16[18,128,128]{2,1,0:T(8,128)(2,1)S(1)} %broadcast_select_fusion), channel_id=1, source_target_pairs={{16,0},{17,1},{18,2},{19,3},{20,4},{21,5},{22,6},{23,7},{24,8},{25... | collective-permute-start | bytes 1769480 | tf_op jit(solution)/shard_map/ppermute | solution.py:172
  90.6 20.3 %collective-permute-start.12 = (bf16[18,128,128]{2,1,0:T(8,128)(2,1)S(1)}, bf16[18,128,128]{2,1,0:T(8,128)(2,1)}, u32[]{:S(2)}, u32[]{:S(2)}) collective-permute-start(bf16[18,128,128]{2,1,0:T(8,128)(2,1)S(1)} %collective-permute-done.10), channel_id=1, source_target_pairs={{112,0},{113,1},{114,2},{115,3},{116,4},{117,5},{118,6},{119,7},{1... | collective-permute-start | bytes 1769480 | tf_op jit(solution)/shard_map/ppermute | solution.py:172
  92.5 41.7 %collective-permute-start = (bf16[33,128,128]{2,1,0:T(8,128)(2,1)S(1)}, bf16[33,128,128]{2,1,0:T(8,128)(2,1)}, u32[]{:S(2)}, u32[]{:S(2)}) collective-permute-start(bf16[33,128,128]{2,1,0:T(8,128)(2,1)S(1)} %pad_maximum_fusion.1.refs_6_), channel_id=1, source_target_pairs={{1,0},{4,1},{3,2},{6,3},{5,4},{8,5},{7,6},{10,7},{9,8},{12,9},{11,... | collective-permute-start | bytes 3244040 | tf_op jit(solution)/shard_map/ppermute | solution.py:172
  94.4 39.8 %collective-permute-start.2 = (bf16[33,128,128]{2,1,0:T(8,128)(2,1)}, bf16[33,128,128]{2,1,0:T(8,128)(2,1)}, u32[]{:S(2)}, u32[]{:S(2)}) collective-permute-start(bf16[33,128,128]{2,1,0:T(8,128)(2,1)} %collective-permute-done.1.refs_7_), channel_id=1, source_target_pairs={{1,0},{0,1},{3,2},{2,3},{5,4},{4,5},{7,6},{6,7},{9,8},{8,9},{11,10... | collective-permute-start | bytes 3244040 | tf_op jit(solution)/shard_map/ppermute | solution.py:172
  96.9 3.3 %copy-start = (bf16[29,128,128]{2,1,0:T(8,128)(2,1)}, bf16[29,128,128]{2,1,0:T(8,128)(2,1)S(1)}, u32[]{:S(2)}) copy-start(bf16[29,128,128]{2,1,0:T(8,128)(2,1)S(1)} %collective-permute-done.7.refs_11_) | copy-start | bytes 2850820
  101.5 42.8 %collective-permute-start.11 = (bf16[47,128,128]{2,1,0:T(8,128)(2,1)}, bf16[47,128,128]{2,1,0:T(8,128)(2,1)S(1)}, u32[]{:S(2)}, u32[]{:S(2)}) collective-permute-start(bf16[47,128,128]{2,1,0:T(8,128)(2,1)} %pad_maximum_fusion), channel_id=1, source_target_pairs={{16,0},{17,1},{18,2},{19,3},{20,4},{21,5},{22,6},{23,7},{24,8},{25... | collective-permute-start | bytes 4620296 | tf_op jit(solution)/shard_map/ppermute | solution.py:172
  110.9 21.4 %collective-permute-start.13 = (bf16[18,128,128]{2,1,0:T(8,128)(2,1)}, bf16[18,128,128]{2,1,0:T(8,128)(2,1)}, u32[]{:S(2)}, u32[]{:S(2)}) collective-permute-start(bf16[18,128,128]{2,1,0:T(8,128)(2,1)} %collective-permute-done.12.refs_13_), channel_id=1, source_target_pairs={{496,0},{497,1},{498,2},{499,3},{500,4},{501,5},{502,6},{503,7},{2... | collective-permute-start | bytes 1769480 | tf_op jit(solution)/shard_map/ppermute | solution.py:172
  132.3 20.4 %collective-permute-start.14 = (bf16[18,128,128]{2,1,0:T(8,128)(2,1)}, bf16[18,128,128]{2,1,0:T(8,128)(2,1)S(1)}, u32[]{:S(2)}, u32[]{:S(2)}) collective-permute-start(bf16[18,128,128]{2,1,0:T(8,128)(2,1)} %collective-permute-done.13.refs_13_), channel_id=1, source_target_pairs={{496,0},{497,1},{498,2},{499,3},{500,4},{501,5},{502,6},{503,7},{2... | collective-permute-start | bytes 1769480 | tf_op jit(solution)/shard_map/ppermute | solution.py:172
  140.1 12.6 %copy-start.7 = (bf16[18,128,128]{2,1,0:T(8,128)(2,1)S(1)}, bf16[18,128,128]{2,1,0:T(8,128)(2,1)}, u32[]{:S(2)}) copy-start(bf16[18,128,128]{2,1,0:T(8,128)(2,1)} %copy-done.6) | copy-start | bytes 1769476
  (6 other events, 8.8 us)

commit v11 on v10

--- a/solution.py
+++ b/solution.py
@@ -11,7 +11,7 @@
 HALF = 16
 RING = 8
 AXES = ("row", "col")
-CUTS = (28, 46)
+CUTS = (30, 47)
 
 
 def block_kernel(first, flip, count, sizes, begins, *refs):

time: 159 us -> 154 us (0.969)
  the two profiles are of different devices: /device:TPU:6 before, /device:TPU:1 now
where the time goes in v11:
time: 154 us; the launch traced here: 153 us
  waiting for transfers between devices  72.8 us (47%)
  starting transfers between devices  56.8 us (37%)
  Pallas kernels  8.53 us (6%)
  local copies, waits for them, and re-layouts  8.1 us (5%)
  other arithmetic  6.32 us (4%)
    ppermute x15, waiting for transfers between devices, local(): send = lambda value, pairs: lax.ppermute(value, AXES, pairs)  72.8 us
    ppermute x15, starting transfers between devices, local(): send = lambda value, pairs: lax.ppermute(value, AXES, pairs)  56.8 us
    pallas_call x2, Pallas kernels, contribute(): pl.pallas_call(functools.partial(block_kernel, first, flip is not None, c...  8.53 us
    unnamed x29, local copies, waits for them, and re-layouts  5.63 us
  transfers between devices with their start and end apart: 15, of which 10 were waited for; matrix products, arithmetic and copies ran while one was open for 5% of the time, Pallas kernels for 2%

profile of v11, /device:TPU:1, one launch (start us, length us, event | category | flops | bytes accessed | tf_op | source)
XLA Modules:
  0.0 152.8 jit_solution(8306797601411776628)
XLA Ops:
  1.2 11.5 %collective-permute-start.4 = (bf16[17,128,128]{2,1,0:T(8,128)(2,1)S(1)}, bf16[17,128,128]{2,1,0:T(8,128)(2,1)S(1)}, u32[]{:S(2)}, u32[]{:S(2)}) collective-permute-start(bf16[17,128,128]{2,1,0:T(8,128)(2,1)S(1)} %slice.42.refs_9_), channel_id=1, source_target_pairs={{128,0},{129,1},{130,2},{131,3},{132,4},{133,5},{134,6},{135,7},{3... | collective-permute-start | bytes 1671176 | tf_op jit(solution)/shard_map/ppermute | solution.py:172
  13.5 1.9 %collective-permute-start.1 = (bf16[33,128,128]{2,1,0:T(8,128)(2,1)S(1)}, bf16[33,128,128]{2,1,0:T(8,128)(2,1)}, u32[]{:S(2)}, u32[]{:S(2)}) collective-permute-start(bf16[33,128,128]{2,1,0:T(8,128)(2,1)S(1)} %pad_maximum_fusion.1.refs_6_), channel_id=1, source_target_pairs={{2,0},{3,1},{4,2},{5,3},{6,4},{7,5},{8,6},{9,7},{10,8},{11,9},{12,... | collective-permute-start | bytes 3244040 | tf_op jit(solution)/shard_map/ppermute | solution.py:172
  16.9 7.0 %collective-permute-start.3 = (bf16[31,128,128]{2,1,0:T(8,128)(2,1)S(1)}, bf16[31,128,128]{2,1,0:T(8,128)(2,1)}, u32[]{:S(2)}, u32[]{:S(2)}) collective-permute-start(bf16[31,128,128]{2,1,0:T(8,128)(2,1)S(1)} %pad_maximum_fusion.2.refs_8_), channel_id=1, source_target_pairs={{16,0},{17,1},{18,2},{19,3},{20,4},{21,5},{22,6},{23,7},{24,8},{25... | collective-permute-start | bytes 3047432 | tf_op jit(solution)/shard_map/ppermute | solution.py:172
  25.4 1.9 %collective-permute-start.5 = (bf16[17,128,128]{2,1,0:T(8,128)(2,1)S(1)}, bf16[17,128,128]{2,1,0:T(8,128)(2,1)S(1)}, u32[]{:S(2)}, u32[]{:S(2)}) collective-permute-start(bf16[17,128,128]{2,1,0:T(8,128)(2,1)S(1)} %get-tuple-element.22), channel_id=1, source_target_pairs={{16,0},{17,1},{18,2},{19,3},{20,4},{21,5},{22,6},{23,7},{24,8},{25... | collective-permute-start | bytes 1671176 | tf_op jit(solution)/shard_map/ppermute | solution.py:172
  27.3 1.9 %collective-permute-start.6 = (bf16[17,128,128]{2,1,0:T(8,128)(2,1)S(1)}, bf16[17,128,128]{2,1,0:T(8,128)(2,1)S(1)}, u32[]{:S(2)}, u32[]{:S(2)}) collective-permute-start(bf16[17,128,128]{2,1,0:T(8,128)(2,1)S(1)} %get-tuple-element.21.refs_10_), channel_id=1, source_target_pairs={{96,0},{97,1},{98,2},{99,3},{100,4},{101,5},{102,6},{103,7},{104,8... | collective-permute-start | bytes 1671176 | tf_op jit(solution)/shard_map/ppermute | solution.py:172
  29.2 15.4 %collective-permute-done.3.refs_8_ = bf16[31,128,128]{2,1,0:T(8,128)(2,1)} collective-permute-done((bf16[31,128,128]{2,1,0:T(8,128)(2,1)S(1)}, bf16[31,128,128]{2,1,0:T(8,128)(2,1)}, u32[]{:S(2)}, u32[]{:S(2)}) %collective-permute-start.3) | collective-permute-done | bytes 1015840 | tf_op jit(solution)/shard_map/ppermute | solution.py:172
  44.6 3.3 %collective-permute-done.1.refs_7_ = bf16[33,128,128]{2,1,0:T(8,128)(2,1)} collective-permute-done((bf16[33,128,128]{2,1,0:T(8,128)(2,1)S(1)}, bf16[33,128,128]{2,1,0:T(8,128)(2,1)}, u32[]{:S(2)}, u32[]{:S(2)}) %collective-permute-start.1) | collective-permute-done | bytes 1081376 | tf_op jit(solution)/shard_map/ppermute | solution.py:172
  47.9 8.6 %collective-permute-done.5.refs_9_ = bf16[17,128,128]{2,1,0:T(8,128)(2,1)S(1)} collective-permute-done((bf16[17,128,128]{2,1,0:T(8,128)(2,1)S(1)}, bf16[17,128,128]{2,1,0:T(8,128)(2,1)S(1)}, u32[]{:S(2)}, u32[]{:S(2)}) %collective-permute-start.5) | collective-permute-done | bytes 557088 | tf_op jit(solution)/shard_map/ppermute | solution.py:172
  56.6 4.5 %collective-permute-start.8 = (bf16[17,128,128]{2,1,0:T(8,128)(2,1)S(1)}, bf16[17,128,128]{2,1,0:T(8,128)(2,1)S(1)}, u32[]{:S(2)}, u32[]{:S(2)}) collective-permute-start(bf16[17,128,128]{2,1,0:T(8,128)(2,1)S(1)} %collective-permute-done.5.refs_9_), channel_id=1, source_target_pairs={{128,0},{129,1},{130,2},{131,3},{132,4},{133,5},{134,6},{135,7},{3... | collective-permute-start | bytes 1671176 | tf_op jit(solution)/shard_map/ppermute | solution.py:172
  61.1 6.3 %collective-permute-start.7 = (bf16[31,128,128]{2,1,0:T(8,128)(2,1)}, bf16[31,128,128]{2,1,0:T(8,128)(2,1)S(1)}, u32[]{:S(2)}, u32[]{:S(2)}) collective-permute-start(bf16[31,128,128]{2,1,0:T(8,128)(2,1)} %collective-permute-done.3.refs_8_), channel_id=1, source_target_pairs={{16,0},{17,1},{18,2},{19,3},{20,4},{21,5},{22,6},{23,7},{24,8},{25... | collective-permute-start | bytes 3047432 | tf_op jit(solution)/shard_map/ppermute | solution.py:172
  67.4 1.9 %collective-permute-start.10 = (bf16[17,128,128]{2,1,0:T(8,128)(2,1)S(1)}, bf16[17,128,128]{2,1,0:T(8,128)(2,1)S(1)}, u32[]{:S(2)}, u32[]{:S(2)}) collective-permute-start(bf16[17,128,128]{2,1,0:T(8,128)(2,1)S(1)} %collective-permute-done.6), channel_id=1, source_target_pairs={{96,0},{97,1},{98,2},{99,3},{100,4},{101,5},{102,6},{103,7},{104,8... | collective-permute-start | bytes 1671176 | tf_op jit(solution)/shard_map/ppermute | solution.py:172
  69.3 2.3 %collective-permute-done.8 = bf16[17,128,128]{2,1,0:T(8,128)(2,1)S(1)} collective-permute-done((bf16[17,128,128]{2,1,0:T(8,128)(2,1)S(1)}, bf16[17,128,128]{2,1,0:T(8,128)(2,1)S(1)}, u32[]{:S(2)}, u32[]{:S(2)}) %collective-permute-start.8) | collective-permute-done | bytes 557088 | tf_op jit(solution)/shard_map/ppermute | solution.py:172
  71.7 1.9 %collective-permute-start.9 = (bf16[17,128,128]{2,1,0:T(8,128)(2,1)S(1)}, bf16[17,128,128]{2,1,0:T(8,128)(2,1)S(1)}, u32[]{:S(2)}, u32[]{:S(2)}) collective-permute-start(bf16[17,128,128]{2,1,0:T(8,128)(2,1)S(1)} %broadcast_select_fusion), channel_id=1, source_target_pairs={{16,0},{17,1},{18,2},{19,3},{20,4},{21,5},{22,6},{23,7},{24,8},{25... | collective-permute-start | bytes 1671176 | tf_op jit(solution)/shard_map/ppermute | solution.py:172
  73.6 4.7 %collective-permute-start = (bf16[33,128,128]{2,1,0:T(8,128)(2,1)S(1)}, bf16[33,128,128]{2,1,0:T(8,128)(2,1)}, u32[]{:S(2)}, u32[]{:S(2)}) collective-permute-start(bf16[33,128,128]{2,1,0:T(8,128)(2,1)S(1)} %pad_maximum_fusion.1.refs_6_), channel_id=1, source_target_pairs={{1,0},{4,1},{3,2},{6,3},{5,4},{8,5},{7,6},{10,7},{9,8},{12,9},{11,... | collective-permute-start | bytes 3244040 | tf_op jit(solution)/shard_map/ppermute | solution.py:172
  78.3 2.2 %collective-permute-start.2 = (bf16[33,128,128]{2,1,0:T(8,128)(2,1)}, bf16[33,128,128]{2,1,0:T(8,128)(2,1)}, u32[]{:S(2)}, u32[]{:S(2)}) collective-permute-start(bf16[33,128,128]{2,1,0:T(8,128)(2,1)} %collective-permute-done.1.refs_7_), channel_id=1, source_target_pairs={{1,0},{0,1},{3,2},{2,3},{5,4},{4,5},{7,6},{6,7},{9,8},{8,9},{11,10... | collective-permute-start | bytes 3244040 | tf_op jit(solution)/shard_map/ppermute | solution.py:172
  80.5 13.2 %collective-permute-done.10 = bf16[17,128,128]{2,1,0:T(8,128)(2,1)S(1)} collective-permute-done((bf16[17,128,128]{2,1,0:T(8,128)(2,1)S(1)}, bf16[17,128,128]{2,1,0:T(8,128)(2,1)S(1)}, u32[]{:S(2)}, u32[]{:S(2)}) %collective-permute-start.10) | collective-permute-done | bytes 557088 | tf_op jit(solution)/shard_map/ppermute | solution.py:172
  93.7 1.9 %collective-permute-start.12 = (bf16[17,128,128]{2,1,0:T(8,128)(2,1)S(1)}, bf16[17,128,128]{2,1,0:T(8,128)(2,1)}, u32[]{:S(2)}, u32[]{:S(2)}) collective-permute-start(bf16[17,128,128]{2,1,0:T(8,128)(2,1)S(1)} %collective-permute-done.10), channel_id=1, source_target_pairs={{112,0},{113,1},{114,2},{115,3},{116,4},{117,5},{118,6},{119,7},{1... | collective-permute-start | bytes 1671176 | tf_op jit(solution)/shard_map/ppermute | solution.py:172
  95.7 4.1 %collective-permute-done.9.refs_12_ = bf16[17,128,128]{2,1,0:T(8,128)(2,1)S(1)} collective-permute-done((bf16[17,128,128]{2,1,0:T(8,128)(2,1)S(1)}, bf16[17,128,128]{2,1,0:T(8,128)(2,1)S(1)}, u32[]{:S(2)}, u32[]{:S(2)}) %collective-permute-start.9) | collective-permute-done | bytes 557088 | tf_op jit(solution)/shard_map/ppermute | solution.py:172
  101.1 5.3 %collective-permute-start.11 = (bf16[48,128,128]{2,1,0:T(8,128)(2,1)}, bf16[48,128,128]{2,1,0:T(8,128)(2,1)S(1)}, u32[]{:S(2)}, u32[]{:S(2)}) collective-permute-start(bf16[48,128,128]{2,1,0:T(8,128)(2,1)} %pad_maximum_fusion), channel_id=1, source_target_pairs={{16,0},{17,1},{18,2},{19,3},{20,4},{21,5},{22,6},{23,7},{24,8},{25... | collective-permute-start | bytes 4718600 | tf_op jit(solution)/shard_map/ppermute | solution.py:172
  106.4 4.2 %collective-permute-done.12.refs_13_ = bf16[17,128,128]{2,1,0:T(8,128)(2,1)} collective-permute-done((bf16[17,128,128]{2,1,0:T(8,128)(2,1)S(1)}, bf16[17,128,128]{2,1,0:T(8,128)(2,1)}, u32[]{:S(2)}, u32[]{:S(2)}) %collective-permute-start.12) | collective-permute-done | bytes 557088 | tf_op jit(solution)/shard_map/ppermute | solution.py:172
  113.9 15.8 %collective-permute-done.13.refs_13_ = bf16[17,128,128]{2,1,0:T(8,128)(2,1)} collective-permute-done((bf16[17,128,128]{2,1,0:T(8,128)(2,1)}, bf16[17,128,128]{2,1,0:T(8,128)(2,1)}, u32[]{:S(2)}, u32[]{:S(2)}) %collective-permute-start.13) | collective-permute-done | bytes 557088 | tf_op jit(solution)/shard_map/ppermute | solution.py:172
  138.6 3.5 %shard_map.55.refs_14_ = f32[16,3,128,128]{3,2,1,0:T(8,128)S(1)} custom-call(s32[1]{0:T(128)} %constant.36.clone.1.refs_0_, s32[3,16]{1,0:T(4,128)S(1)} %bitcast.42, s32[2,16]{1,0:T(2,128)S(1)} %bitcast.44, s32[2,16]{1,0:T(2,128)S(1)} %bitcast_convert_fusion.1.refs_3_, s32[2,32]{1,0:T(2,128)S(1)} %bitcast.45, s32[2,32]{1,0:T(2,128)S(1)} %bitcast_convert_fusion.refs_5_, ...), custom_call_target="tpu_custom_call" | custom-call | flops 805306368 | bytes 12582912 | tf_op jit(solution)/shard_map/pallas_call | solution.py:96
  142.1 5.7 %collective-permute-done.14.refs_10_ = bf16[17,128,128]{2,1,0:T(8,128)(2,1)S(1)} collective-permute-done((bf16[17,128,128]{2,1,0:T(8,128)(2,1)}, bf16[17,128,128]{2,1,0:T(8,128)(2,1)S(1)}, u32[]{:S(2)}, u32[]{:S(2)}) %collective-permute-start.14) | collective-permute-done | bytes 557088 | tf_op jit(solution)/shard_map/ppermute | solution.py:172
  147.8 5.0 %shard_map.56 = bf16[16,3,128,128]{3,2,1,0:T(8,128)(2,1)} custom-call(s32[1]{0:T(128)} %bitcast.refs_0_, s32[3,16]{1,0:T(4,128)S(1)} %bitcast.43, s32[2,16]{1,0:T(2,128)S(1)} %get-tuple-element.20.refs_2_, s32[2,16]{1,0:T(2,128)S(1)} %get-tuple-element.19.refs_3_, s32[2,32]{1,0:T(2,128)S(1)} %bitcast_convert_fusion.2.refs_4_, s32[2,32]{1,0:T(2,128)S(1)} %fusion.2.refs_5_, ...), custom_call_target="tpu_custom_call" | custom-call | flops 805306368 | bytes 12582912 | tf_op jit(solution)/shard_map/pallas_call | solution.py:96
  (53 shorter events, 18.4 us)
Async XLA Ops:
  0.0 13.4 %copy-start.12 = (bf16[16,1,2,128,128]{4,3,2,1,0:T(8,128)(2,1)S(1)}, bf16[16,1,2,128,128]{4,3,2,1,0:T(8,128)(2,1)}, u32[]{:S(2)}) copy-start(bf16[16,1,2,128,128]{4,3,2,1,0:T(8,128)(2,1)} %param.5) | copy-start | bytes 3145732
  1.2 15.5 %copy-start.4 = (bf16[17,128,128]{2,1,0:T(8,128)(2,1)}, bf16[17,128,128]{2,1,0:T(8,128)(2,1)S(1)}, u32[]{:S(2)}) copy-start(bf16[17,128,128]{2,1,0:T(8,128)(2,1)S(1)} %slice.42.refs_9_) | copy-start | bytes 1671172
  1.2 22.8 %collective-permute-start.4 = (bf16[17,128,128]{2,1,0:T(8,128)(2,1)S(1)}, bf16[17,128,128]{2,1,0:T(8,128)(2,1)S(1)}, u32[]{:S(2)}, u32[]{:S(2)}) collective-permute-start(bf16[17,128,128]{2,1,0:T(8,128)(2,1)S(1)} %slice.42.refs_9_), channel_id=1, source_target_pairs={{128,0},{129,1},{130,2},{131,3},{132,4},{133,5},{134,6},{135,7},{3... | collective-permute-start | bytes 1671176 | tf_op jit(solution)/shard_map/ppermute | solution.py:172
  13.4 3.3 %copy-start.11 = (s32[1,32,2]{1,2,0:T(2,128)S(1)}, s32[1,32,2]{1,2,0:T(2,128)}, u32[]{:S(2)}) copy-start(s32[1,32,2]{1,2,0:T(2,128)} %param.8) | copy-start | bytes 772
  13.5 34.4 %collective-permute-start.1 = (bf16[33,128,128]{2,1,0:T(8,128)(2,1)S(1)}, bf16[33,128,128]{2,1,0:T(8,128)(2,1)}, u32[]{:S(2)}, u32[]{:S(2)}) collective-permute-start(bf16[33,128,128]{2,1,0:T(8,128)(2,1)S(1)} %pad_maximum_fusion.1.refs_6_), channel_id=1, source_target_pairs={{2,0},{3,1},{4,2},{5,3},{6,4},{7,5},{8,6},{9,7},{10,8},{11,9},{12,... | collective-permute-start | bytes 3244040 | tf_op jit(solution)/shard_map/ppermute | solution.py:172
  16.9 54.8 %copy-start.2 = (bf16[31,128,128]{2,1,0:T(8,128)(2,1)}, bf16[31,128,128]{2,1,0:T(8,128)(2,1)S(1)}, u32[]{:S(2)}) copy-start(bf16[31,128,128]{2,1,0:T(8,128)(2,1)S(1)} %pad_maximum_fusion.2.refs_8_) | copy-start | bytes 3047428
  16.9 27.8 %collective-permute-start.3 = (bf16[31,128,128]{2,1,0:T(8,128)(2,1)S(1)}, bf16[31,128,128]{2,1,0:T(8,128)(2,1)}, u32[]{:S(2)}, u32[]{:S(2)}) collective-permute-start(bf16[31,128,128]{2,1,0:T(8,128)(2,1)S(1)} %pad_maximum_fusion.2.refs_8_), channel_id=1, source_target_pairs={{16,0},{17,1},{18,2},{19,3},{20,4},{21,5},{22,6},{23,7},{24,8},{25... | collective-permute-start | bytes 3047432 | tf_op jit(solution)/shard_map/ppermute | solution.py:172
  25.4 74.4 %copy-start.6 = (bf16[17,128,128]{2,1,0:T(8,128)(2,1)}, bf16[17,128,128]{2,1,0:T(8,128)(2,1)S(1)}, u32[]{:S(2)}) copy-start(bf16[17,128,128]{2,1,0:T(8,128)(2,1)S(1)} %get-tuple-element.21.refs_10_) | copy-start | bytes 1671172
  25.4 31.2 %collective-permute-start.5 = (bf16[17,128,128]{2,1,0:T(8,128)(2,1)S(1)}, bf16[17,128,128]{2,1,0:T(8,128)(2,1)S(1)}, u32[]{:S(2)}, u32[]{:S(2)}) collective-permute-start(bf16[17,128,128]{2,1,0:T(8,128)(2,1)S(1)} %get-tuple-element.22), channel_id=1, source_target_pairs={{16,0},{17,1},{18,2},{19,3},{20,4},{21,5},{22,6},{23,7},{24,8},{25... | collective-permute-start | bytes 1671176 | tf_op jit(solution)/shard_map/ppermute | solution.py:172
  27.3 29.3 %collective-permute-start.6 = (bf16[17,128,128]{2,1,0:T(8,128)(2,1)S(1)}, bf16[17,128,128]{2,1,0:T(8,128)(2,1)S(1)}, u32[]{:S(2)}, u32[]{:S(2)}) collective-permute-start(bf16[17,128,128]{2,1,0:T(8,128)(2,1)S(1)} %get-tuple-element.21.refs_10_), channel_id=1, source_target_pairs={{96,0},{97,1},{98,2},{99,3},{100,4},{101,5},{102,6},{103,7},{104,8... | collective-permute-start | bytes 1671176 | tf_op jit(solution)/shard_map/ppermute | solution.py:172
  56.6 15.0 %collective-permute-start.8 = (bf16[17,128,128]{2,1,0:T(8,128)(2,1)S(1)}, bf16[17,128,128]{2,1,0:T(8,128)(2,1)S(1)}, u32[]{:S(2)}, u32[]{:S(2)}) collective-permute-start(bf16[17,128,128]{2,1,0:T(8,128)(2,1)S(1)} %collective-permute-done.5.refs_9_), channel_id=1, source_target_pairs={{128,0},{129,1},{130,2},{131,3},{132,4},{133,5},{134,6},{135,7},{3... | collective-permute-start | bytes 1671176 | tf_op jit(solution)/shard_map/ppermute | solution.py:172
  61.1 34.5 %collective-permute-start.7 = (bf16[31,128,128]{2,1,0:T(8,128)(2,1)}, bf16[31,128,128]{2,1,0:T(8,128)(2,1)S(1)}, u32[]{:S(2)}, u32[]{:S(2)}) collective-permute-start(bf16[31,128,128]{2,1,0:T(8,128)(2,1)} %collective-permute-done.3.refs_8_), channel_id=1, source_target_pairs={{16,0},{17,1},{18,2},{19,3},{20,4},{21,5},{22,6},{23,7},{24,8},{25... | collective-permute-start | bytes 3047432 | tf_op jit(solution)/shard_map/ppermute | solution.py:172
  67.4 26.3 %collective-permute-start.10 = (bf16[17,128,128]{2,1,0:T(8,128)(2,1)S(1)}, bf16[17,128,128]{2,1,0:T(8,128)(2,1)S(1)}, u32[]{:S(2)}, u32[]{:S(2)}) collective-permute-start(bf16[17,128,128]{2,1,0:T(8,128)(2,1)S(1)} %collective-permute-done.6), channel_id=1, source_target_pairs={{96,0},{97,1},{98,2},{99,3},{100,4},{101,5},{102,6},{103,7},{104,8... | collective-permute-start | bytes 1671176 | tf_op jit(solution)/shard_map/ppermute | solution.py:172
  71.7 40.8 %copy-start.13 = (s32[16,1,3]{0,1,2:T(1,128)S(1)}, s32[16,1,3]{0,1,2:T(1,128)}, u32[]{:S(2)}) copy-start(s32[16,1,3]{0,1,2:T(1,128)} %param.9) | copy-start | bytes 580
  71.7 61.3 %copy-start.10 = (s32[16,1,2]{0,2,1:T(2,128)S(1)}, s32[16,1,2]{0,2,1:T(2,128)}, u32[]{:S(2)}) copy-start(s32[16,1,2]{0,2,1:T(2,128)} %param.6) | copy-start | bytes 388
  71.7 28.0 %collective-permute-start.9 = (bf16[17,128,128]{2,1,0:T(8,128)(2,1)S(1)}, bf16[17,128,128]{2,1,0:T(8,128)(2,1)S(1)}, u32[]{:S(2)}, u32[]{:S(2)}) collective-permute-start(bf16[17,128,128]{2,1,0:T(8,128)(2,1)S(1)} %broadcast_select_fusion), channel_id=1, source_target_pairs={{16,0},{17,1},{18,2},{19,3},{20,4},{21,5},{22,6},{23,7},{24,8},{25... | collective-permute-start | bytes 1671176 | tf_op jit(solution)/shard_map/ppermute | solution.py:172
  73.6 58.0 %collective-permute-start = (bf16[33,128,128]{2,1,0:T(8,128)(2,1)S(1)}, bf16[33,128,128]{2,1,0:T(8,128)(2,1)}, u32[]{:S(2)}, u32[]{:S(2)}) collective-permute-start(bf16[33,128,128]{2,1,0:T(8,128)(2,1)S(1)} %pad_maximum_fusion.1.refs_6_), channel_id=1, source_target_pairs={{1,0},{4,1},{3,2},{6,3},{5,4},{8,5},{7,6},{10,7},{9,8},{12,9},{11,... | collective-permute-start | bytes 3244040 | tf_op jit(solution)/shard_map/ppermute | solution.py:172
  78.3 53.3 %collective-permute-start.2 = (bf16[33,128,128]{2,1,0:T(8,128)(2,1)}, bf16[33,128,128]{2,1,0:T(8,128)(2,1)}, u32[]{:S(2)}, u32[]{:S(2)}) collective-permute-start(bf16[33,128,128]{2,1,0:T(8,128)(2,1)} %collective-permute-done.1.refs_7_), channel_id=1, source_target_pairs={{1,0},{0,1},{3,2},{2,3},{5,4},{4,5},{7,6},{6,7},{9,8},{8,9},{11,10... | collective-permute-start | bytes 3244040 | tf_op jit(solution)/shard_map/ppermute | solution.py:172
  93.7 16.8 %collective-permute-start.12 = (bf16[17,128,128]{2,1,0:T(8,128)(2,1)S(1)}, bf16[17,128,128]{2,1,0:T(8,128)(2,1)}, u32[]{:S(2)}, u32[]{:S(2)}) collective-permute-start(bf16[17,128,128]{2,1,0:T(8,128)(2,1)S(1)} %collective-permute-done.10), channel_id=1, source_target_pairs={{112,0},{113,1},{114,2},{115,3},{116,4},{117,5},{118,6},{119,7},{1... | collective-permute-start | bytes 1671176 | tf_op jit(solution)/shard_map/ppermute | solution.py:172
  95.7 5.4 %copy-start = (bf16[31,128,128]{2,1,0:T(8,128)(2,1)}, bf16[31,128,128]{2,1,0:T(8,128)(2,1)S(1)}, u32[]{:S(2)}) copy-start(bf16[31,128,128]{2,1,0:T(8,128)(2,1)S(1)} %collective-permute-done.7.refs_11_) | copy-start | bytes 3047428
  99.7 1.3 copy-start.8
  101.1 41.0 %collective-permute-start.11 = (bf16[48,128,128]{2,1,0:T(8,128)(2,1)}, bf16[48,128,128]{2,1,0:T(8,128)(2,1)S(1)}, u32[]{:S(2)}, u32[]{:S(2)}) collective-permute-start(bf16[48,128,128]{2,1,0:T(8,128)(2,1)} %pad_maximum_fusion), channel_id=1, source_target_pairs={{16,0},{17,1},{18,2},{19,3},{20,4},{21,5},{22,6},{23,7},{24,8},{25... | collective-permute-start | bytes 4718600 | tf_op jit(solution)/shard_map/ppermute | solution.py:172
  110.6 19.1 %collective-permute-start.13 = (bf16[17,128,128]{2,1,0:T(8,128)(2,1)}, bf16[17,128,128]{2,1,0:T(8,128)(2,1)}, u32[]{:S(2)}, u32[]{:S(2)}) collective-permute-start(bf16[17,128,128]{2,1,0:T(8,128)(2,1)} %collective-permute-done.12.refs_13_), channel_id=1, source_target_pairs={{496,0},{497,1},{498,2},{499,3},{500,4},{501,5},{502,6},{503,7},{2... | collective-permute-start | bytes 1671176 | tf_op jit(solution)/shard_map/ppermute | solution.py:172
  129.7 18.1 %collective-permute-start.14 = (bf16[17,128,128]{2,1,0:T(8,128)(2,1)}, bf16[17,128,128]{2,1,0:T(8,128)(2,1)S(1)}, u32[]{:S(2)}, u32[]{:S(2)}) collective-permute-start(bf16[17,128,128]{2,1,0:T(8,128)(2,1)} %collective-permute-done.13.refs_13_), channel_id=1, source_target_pairs={{496,0},{497,1},{498,2},{499,3},{500,4},{501,5},{502,6},{503,7},{2... | collective-permute-start | bytes 1671176 | tf_op jit(solution)/shard_map/ppermute | solution.py:172
  (5 other events, 5.6 us)

commit v12 on v9

--- a/solution.py
+++ b/solution.py
@@ -11,7 +11,7 @@
 HALF = 16
 RING = 8
 AXES = ("row", "col")
-CUTS = (28, 46)
+CUTS = (30, 48)
 
 
 def block_kernel(first, flip, count, sizes, *refs):

time: 154 us -> 154 us (level)
  the two profiles are of different devices: /device:TPU:56 before, /device:TPU:6 now
where the time goes in v12:
time: 154 us; the launch traced here: 152 us
  waiting for transfers between devices  73.3 us (48%)
  starting transfers between devices  61.2 us (40%)
  Pallas kernels  8.48 us (6%)
  other arithmetic  4.77 us (3%)
  local copies, waits for them, and re-layouts  4.14 us (3%)
    ppermute x16, waiting for transfers between devices, local(): send = lambda value, pairs: lax.ppermute(value, AXES, pairs)  73.3 us
    ppermute x16, starting transfers between devices, local(): send = lambda value, pairs: lax.ppermute(value, AXES, pairs)  61.2 us
    pallas_call x2, Pallas kernels, contribute(): pl.pallas_call(functools.partial(block_kernel, first, flip is not None, c...  8.48 us
  transfers between devices with their start and end apart: 16, of which 10 were waited for; matrix products, arithmetic and copies ran while one was open for 4% of the time, Pallas kernels for 2%

profile of v12, /device:TPU:6, one launch (start us, length us, event | category | flops | bytes accessed | tf_op | source)
XLA Modules:
  0.0 152.2 jit_solution(162677402363932920)
XLA Ops:
  1.2 10.9 %collective-permute-start.4 = (bf16[18,128,128]{2,1,0:T(8,128)(2,1)S(1)}, bf16[18,128,128]{2,1,0:T(8,128)(2,1)}, u32[]{:S(2)}, u32[]{:S(2)}) collective-permute-start(bf16[18,128,128]{2,1,0:T(8,128)(2,1)S(1)} %bitcast.44), channel_id=1, source_target_pairs={{128,0},{129,1},{130,2},{131,3},{132,4},{133,5},{134,6},{135,7},{3... | collective-permute-start | bytes 1769480 | tf_op jit(solution)/shard_map/ppermute | solution.py:172
  12.3 2.9 %collective-permute-start.1 = (bf16[33,128,128]{2,1,0:T(8,128)(2,1)S(1)}, bf16[33,128,128]{2,1,0:T(8,128)(2,1)}, u32[]{:S(2)}, u32[]{:S(2)}) collective-permute-start(bf16[33,128,128]{2,1,0:T(8,128)(2,1)S(1)} %pad_maximum_fusion.refs_6_), channel_id=1, source_target_pairs={{2,0},{3,1},{4,2},{5,3},{6,4},{7,5},{8,6},{9,7},{10,8},{11,9},{12,... | collective-permute-start | bytes 3244040 | tf_op jit(solution)/shard_map/ppermute | solution.py:172
  15.3 4.4 %collective-permute-start.3 = (bf16[31,128,128]{2,1,0:T(8,128)(2,1)S(1)}, bf16[31,128,128]{2,1,0:T(8,128)(2,1)}, u32[]{:S(2)}, u32[]{:S(2)}) collective-permute-start(bf16[31,128,128]{2,1,0:T(8,128)(2,1)S(1)} %pad_maximum_fusion.1.refs_8_), channel_id=1, source_target_pairs={{16,0},{17,1},{18,2},{19,3},{20,4},{21,5},{22,6},{23,7},{24,8},{25... | collective-permute-start | bytes 3047432 | tf_op jit(solution)/shard_map/ppermute | solution.py:172
  19.8 4.9 %collective-permute-done.4 = bf16[18,128,128]{2,1,0:T(8,128)(2,1)} collective-permute-done((bf16[18,128,128]{2,1,0:T(8,128)(2,1)S(1)}, bf16[18,128,128]{2,1,0:T(8,128)(2,1)}, u32[]{:S(2)}, u32[]{:S(2)}) %collective-permute-start.4) | collective-permute-done | bytes 589856 | tf_op jit(solution)/shard_map/ppermute | solution.py:172
  25.8 1.9 %collective-permute-start.5 = (bf16[18,128,128]{2,1,0:T(8,128)(2,1)S(1)}, bf16[18,128,128]{2,1,0:T(8,128)(2,1)S(1)}, u32[]{:S(2)}, u32[]{:S(2)}) collective-permute-start(bf16[18,128,128]{2,1,0:T(8,128)(2,1)S(1)} %broadcast_select_fusion.1), channel_id=1, source_target_pairs={{16,0},{17,1},{18,2},{19,3},{20,4},{21,5},{22,6},{23,7},{24,8},{25... | collective-permute-start | bytes 1769480 | tf_op jit(solution)/shard_map/ppermute | solution.py:172
  28.9 1.9 %collective-permute-start.6 = (bf16[16,128,128]{2,1,0:T(8,128)(2,1)S(1)}, bf16[16,128,128]{2,1,0:T(8,128)(2,1)S(1)}, u32[]{:S(2)}, u32[]{:S(2)}) collective-permute-start(bf16[16,128,128]{2,1,0:T(8,128)(2,1)S(1)} %bitcast.46), channel_id=1, source_target_pairs={{96,0},{97,1},{98,2},{99,3},{100,4},{101,5},{102,6},{103,7},{104,8... | collective-permute-start | bytes 1572872 | tf_op jit(solution)/shard_map/ppermute | solution.py:172
  31.6 18.9 %collective-permute-done.6 = bf16[16,128,128]{2,1,0:T(8,128)(2,1)S(1)} collective-permute-done((bf16[16,128,128]{2,1,0:T(8,128)(2,1)S(1)}, bf16[16,128,128]{2,1,0:T(8,128)(2,1)S(1)}, u32[]{:S(2)}, u32[]{:S(2)}) %collective-permute-start.6) | collective-permute-done | bytes 524320 | tf_op jit(solution)/shard_map/ppermute | solution.py:172
  50.5 3.3 %collective-permute-done.5.refs_9_ = bf16[18,128,128]{2,1,0:T(8,128)(2,1)S(1)} collective-permute-done((bf16[18,128,128]{2,1,0:T(8,128)(2,1)S(1)}, bf16[18,128,128]{2,1,0:T(8,128)(2,1)S(1)}, u32[]{:S(2)}, u32[]{:S(2)}) %collective-permute-start.5) | collective-permute-done | bytes 589856 | tf_op jit(solution)/shard_map/ppermute | solution.py:172
  53.8 8.9 %collective-permute-start.8 = (bf16[18,128,128]{2,1,0:T(8,128)(2,1)S(1)}, bf16[18,128,128]{2,1,0:T(8,128)(2,1)S(1)}, u32[]{:S(2)}, u32[]{:S(2)}) collective-permute-start(bf16[18,128,128]{2,1,0:T(8,128)(2,1)S(1)} %collective-permute-done.5.refs_9_), channel_id=1, source_target_pairs={{128,0},{129,1},{130,2},{131,3},{132,4},{133,5},{134,6},{135,7},{3... | collective-permute-start | bytes 1769480 | tf_op jit(solution)/shard_map/ppermute | solution.py:172
  62.7 1.9 %collective-permute-start.10 = (bf16[16,128,128]{2,1,0:T(8,128)(2,1)S(1)}, bf16[16,128,128]{2,1,0:T(8,128)(2,1)S(1)}, u32[]{:S(2)}, u32[]{:S(2)}) collective-permute-start(bf16[16,128,128]{2,1,0:T(8,128)(2,1)S(1)} %collective-permute-done.6), channel_id=1, source_target_pairs={{96,0},{97,1},{98,2},{99,3},{100,4},{101,5},{102,6},{103,7},{104,8... | collective-permute-start | bytes 1572872 | tf_op jit(solution)/shard_map/ppermute | solution.py:172
  64.7 6.3 %collective-permute-start.7 = (bf16[31,128,128]{2,1,0:T(8,128)(2,1)}, bf16[31,128,128]{2,1,0:T(8,128)(2,1)}, u32[]{:S(2)}, u32[]{:S(2)}) collective-permute-start(bf16[31,128,128]{2,1,0:T(8,128)(2,1)} %collective-permute-done.3.refs_8_), channel_id=1, source_target_pairs={{16,0},{17,1},{18,2},{19,3},{20,4},{21,5},{22,6},{23,7},{24,8},{25... | collective-permute-start | bytes 3047432 | tf_op jit(solution)/shard_map/ppermute | solution.py:172
  71.0 2.5 %collective-permute-done.8 = bf16[18,128,128]{2,1,0:T(8,128)(2,1)S(1)} collective-permute-done((bf16[18,128,128]{2,1,0:T(8,128)(2,1)S(1)}, bf16[18,128,128]{2,1,0:T(8,128)(2,1)S(1)}, u32[]{:S(2)}, u32[]{:S(2)}) %collective-permute-start.8) | collective-permute-done | bytes 589856 | tf_op jit(solution)/shard_map/ppermute | solution.py:172
  73.5 1.9 %collective-permute-start.9 = (bf16[18,128,128]{2,1,0:T(8,128)(2,1)S(1)}, bf16[18,128,128]{2,1,0:T(8,128)(2,1)}, u32[]{:S(2)}, u32[]{:S(2)}) collective-permute-start(bf16[18,128,128]{2,1,0:T(8,128)(2,1)S(1)} %broadcast_select_fusion), channel_id=1, source_target_pairs={{16,0},{17,1},{18,2},{19,3},{20,4},{21,5},{22,6},{23,7},{24,8},{25... | collective-permute-start | bytes 1769480 | tf_op jit(solution)/shard_map/ppermute | solution.py:172
  75.5 1.9 %collective-permute-start = (bf16[33,128,128]{2,1,0:T(8,128)(2,1)S(1)}, bf16[33,128,128]{2,1,0:T(8,128)(2,1)}, u32[]{:S(2)}, u32[]{:S(2)}) collective-permute-start(bf16[33,128,128]{2,1,0:T(8,128)(2,1)S(1)} %pad_maximum_fusion.refs_6_), channel_id=1, source_target_pairs={{1,0},{4,1},{3,2},{6,3},{5,4},{8,5},{7,6},{10,7},{9,8},{12,9},{11,... | collective-permute-start | bytes 3244040 | tf_op jit(solution)/shard_map/ppermute | solution.py:172
  77.4 2.4 %collective-permute-start.2 = (bf16[33,128,128]{2,1,0:T(8,128)(2,1)}, bf16[33,128,128]{2,1,0:T(8,128)(2,1)}, u32[]{:S(2)}, u32[]{:S(2)}) collective-permute-start(bf16[33,128,128]{2,1,0:T(8,128)(2,1)} %collective-permute-done.1.refs_7_), channel_id=1, source_target_pairs={{1,0},{0,1},{3,2},{2,3},{5,4},{4,5},{7,6},{6,7},{9,8},{8,9},{11,10... | collective-permute-start | bytes 3244040 | tf_op jit(solution)/shard_map/ppermute | solution.py:172
  79.8 7.0 %collective-permute-done.10 = bf16[16,128,128]{2,1,0:T(8,128)(2,1)S(1)} collective-permute-done((bf16[16,128,128]{2,1,0:T(8,128)(2,1)S(1)}, bf16[16,128,128]{2,1,0:T(8,128)(2,1)S(1)}, u32[]{:S(2)}, u32[]{:S(2)}) %collective-permute-start.10) | collective-permute-done | bytes 524320 | tf_op jit(solution)/shard_map/ppermute | solution.py:172
  88.8 5.4 %collective-permute-done.7.refs_11_ = bf16[31,128,128]{2,1,0:T(8,128)(2,1)} collective-permute-done((bf16[31,128,128]{2,1,0:T(8,128)(2,1)}, bf16[31,128,128]{2,1,0:T(8,128)(2,1)}, u32[]{:S(2)}, u32[]{:S(2)}) %collective-permute-start.7) | collective-permute-done | bytes 1015840 | tf_op jit(solution)/shard_map/ppermute | solution.py:172
  94.2 10.5 %collective-permute-done.9.refs_12_ = bf16[18,128,128]{2,1,0:T(8,128)(2,1)} collective-permute-done((bf16[18,128,128]{2,1,0:T(8,128)(2,1)S(1)}, bf16[18,128,128]{2,1,0:T(8,128)(2,1)}, u32[]{:S(2)}, u32[]{:S(2)}) %collective-permute-start.9) | collective-permute-done | bytes 589856 | tf_op jit(solution)/shard_map/ppermute | solution.py:172
  106.6 8.1 %collective-permute-start.11 = (bf16[31,128,128]{2,1,0:T(8,128)(2,1)}, bf16[31,128,128]{2,1,0:T(8,128)(2,1)}, u32[]{:S(2)}, u32[]{:S(2)}) collective-permute-start(bf16[31,128,128]{2,1,0:T(8,128)(2,1)} %collective-permute-done.7.refs_11_), channel_id=1, source_target_pairs={{16,0},{17,1},{18,2},{19,3},{20,4},{21,5},{22,6},{23,7},{24,8},{25... | collective-permute-start | bytes 3047432 | tf_op jit(solution)/shard_map/ppermute | solution.py:172
  118.0 4.9 %collective-permute-done.13.refs_13_ = bf16[16,128,128]{2,1,0:T(8,128)(2,1)} collective-permute-done((bf16[16,128,128]{2,1,0:T(8,128)(2,1)}, bf16[16,128,128]{2,1,0:T(8,128)(2,1)}, u32[]{:S(2)}, u32[]{:S(2)}) %collective-permute-start.13) | collective-permute-done | bytes 524320 | tf_op jit(solution)/shard_map/ppermute | solution.py:172
  127.3 3.5 %shard_map.55.refs_14_ = f32[16,3,128,128]{3,2,1,0:T(8,128)S(1)} custom-call(s32[1]{0:T(128)} %constant.36.clone.1.refs_0_, s32[3,16]{1,0:T(4,128)S(1)} %bitcast.48, s32[2,16]{1,0:T(2,128)S(1)} %bitcast.50, s32[2,16]{1,0:T(2,128)S(1)} %bitcast_convert_fusion.1.refs_3_, s32[2,32]{1,0:T(2,128)S(1)} %bitcast.51, s32[2,32]{1,0:T(2,128)S(1)} %bitcast_convert_fusion.refs_5_, ...), custom_call_target="tpu_custom_call" | custom-call | flops 805306368 | bytes 12582912 | tf_op jit(solution)/shard_map/pallas_call | solution.py:96
  130.8 7.1 %collective-permute-done.11.refs_11_ = bf16[31,128,128]{2,1,0:T(8,128)(2,1)} collective-permute-done((bf16[31,128,128]{2,1,0:T(8,128)(2,1)}, bf16[31,128,128]{2,1,0:T(8,128)(2,1)}, u32[]{:S(2)}, u32[]{:S(2)}) %collective-permute-start.11) | collective-permute-done | bytes 1015840 | tf_op jit(solution)/shard_map/ppermute | solution.py:172
  138.6 8.7 %collective-permute-done.15.refs_12_ = bf16[18,128,128]{2,1,0:T(8,128)(2,1)S(1)} collective-permute-done((bf16[18,128,128]{2,1,0:T(8,128)(2,1)}, bf16[18,128,128]{2,1,0:T(8,128)(2,1)S(1)}, u32[]{:S(2)}, u32[]{:S(2)}) %collective-permute-start.15) | collective-permute-done | bytes 589856 | tf_op jit(solution)/shard_map/ppermute | solution.py:172
  147.3 4.9 %shard_map.56 = bf16[16,3,128,128]{3,2,1,0:T(8,128)(2,1)} custom-call(s32[1]{0:T(128)} %bitcast.refs_0_, s32[3,16]{1,0:T(4,128)S(1)} %bitcast.49, s32[2,16]{1,0:T(2,128)S(1)} %get-tuple-element.20.refs_2_, s32[2,16]{1,0:T(2,128)S(1)} %get-tuple-element.19.refs_3_, s32[2,32]{1,0:T(2,128)S(1)} %bitcast_convert_fusion.2.refs_4_, s32[2,32]{1,0:T(2,128)S(1)} %fusion.2.refs_5_, ...), custom_call_target="tpu_custom_call" | custom-call | flops 805306368 | bytes 12582912 | tf_op jit(solution)/shard_map/pallas_call | solution.py:96
  (40 shorter events, 16.6 us)
Async XLA Ops:
  0.0 12.1 %copy-start.2 = (s32[16,1,2]{0,2,1:T(2,128)S(1)}, s32[16,1,2]{0,2,1:T(2,128)}, u32[]{:S(2)}) copy-start(s32[16,1,2]{0,2,1:T(2,128)} %param.6) | copy-start | bytes 388
  0.0 12.2 %copy-start.4 = (bf16[16,1,2,128,128]{4,3,2,1,0:T(8,128)(2,1)S(1)}, bf16[16,1,2,128,128]{4,3,2,1,0:T(8,128)(2,1)}, u32[]{:S(2)}) copy-start(bf16[16,1,2,128,128]{4,3,2,1,0:T(8,128)(2,1)} %param.5) | copy-start | bytes 3145732
  1.2 23.5 %collective-permute-start.4 = (bf16[18,128,128]{2,1,0:T(8,128)(2,1)S(1)}, bf16[18,128,128]{2,1,0:T(8,128)(2,1)}, u32[]{:S(2)}, u32[]{:S(2)}) collective-permute-start(bf16[18,128,128]{2,1,0:T(8,128)(2,1)S(1)} %bitcast.44), channel_id=1, source_target_pairs={{128,0},{129,1},{130,2},{131,3},{132,4},{133,5},{134,6},{135,7},{3... | collective-permute-start | bytes 1769480 | tf_op jit(solution)/shard_map/ppermute | solution.py:172
  12.3 2.9 %copy-start.3 = (s32[1,32,2]{1,2,0:T(2,128)S(1)}, s32[1,32,2]{1,2,0:T(2,128)}, u32[]{:S(2)}) copy-start(s32[1,32,2]{1,2,0:T(2,128)} %param.8) | copy-start | bytes 772
  12.3 2.9 %slice-start = ((bf16[1,32,2,128,128]{4,3,2,1,0:T(8,128)(2,1)}), bf16[1,15,2,128,128]{4,3,2,1,0:T(8,128)(2,1)S(1)}, s32[]{:S(2)}) async-start(bf16[1,32,2,128,128]{4,3,2,1,0:T(8,128)(2,1)} %param.7), calls=%async_computation | async-start | bytes 1966080 | tf_op jit(solution)/shard_map/slice | solution.py:183
  12.3 38.2 %collective-permute-start.1 = (bf16[33,128,128]{2,1,0:T(8,128)(2,1)S(1)}, bf16[33,128,128]{2,1,0:T(8,128)(2,1)}, u32[]{:S(2)}, u32[]{:S(2)}) collective-permute-start(bf16[33,128,128]{2,1,0:T(8,128)(2,1)S(1)} %pad_maximum_fusion.refs_6_), channel_id=1, source_target_pairs={{2,0},{3,1},{4,2},{5,3},{6,4},{7,5},{8,6},{9,7},{10,8},{11,9},{12,... | collective-permute-start | bytes 3244040 | tf_op jit(solution)/shard_map/ppermute | solution.py:172
  15.3 35.2 %collective-permute-start.3 = (bf16[31,128,128]{2,1,0:T(8,128)(2,1)S(1)}, bf16[31,128,128]{2,1,0:T(8,128)(2,1)}, u32[]{:S(2)}, u32[]{:S(2)}) collective-permute-start(bf16[31,128,128]{2,1,0:T(8,128)(2,1)S(1)} %pad_maximum_fusion.1.refs_8_), channel_id=1, source_target_pairs={{16,0},{17,1},{18,2},{19,3},{20,4},{21,5},{22,6},{23,7},{24,8},{25... | collective-permute-start | bytes 3047432 | tf_op jit(solution)/shard_map/ppermute | solution.py:172
  25.8 28.0 %collective-permute-start.5 = (bf16[18,128,128]{2,1,0:T(8,128)(2,1)S(1)}, bf16[18,128,128]{2,1,0:T(8,128)(2,1)S(1)}, u32[]{:S(2)}, u32[]{:S(2)}) collective-permute-start(bf16[18,128,128]{2,1,0:T(8,128)(2,1)S(1)} %broadcast_select_fusion.1), channel_id=1, source_target_pairs={{16,0},{17,1},{18,2},{19,3},{20,4},{21,5},{22,6},{23,7},{24,8},{25... | collective-permute-start | bytes 1769480 | tf_op jit(solution)/shard_map/ppermute | solution.py:172
  28.9 85.9 %copy-start.5 = (s32[16,1,3]{0,1,2:T(1,128)S(1)}, s32[16,1,3]{0,1,2:T(1,128)}, u32[]{:S(2)}) copy-start(s32[16,1,3]{0,1,2:T(1,128)} %param.9) | copy-start | bytes 580
  28.9 21.6 %collective-permute-start.6 = (bf16[16,128,128]{2,1,0:T(8,128)(2,1)S(1)}, bf16[16,128,128]{2,1,0:T(8,128)(2,1)S(1)}, u32[]{:S(2)}, u32[]{:S(2)}) collective-permute-start(bf16[16,128,128]{2,1,0:T(8,128)(2,1)S(1)} %bitcast.46), channel_id=1, source_target_pairs={{96,0},{97,1},{98,2},{99,3},{100,4},{101,5},{102,6},{103,7},{104,8... | collective-permute-start | bytes 1572872 | tf_op jit(solution)/shard_map/ppermute | solution.py:172
  30.8 0.8 copy-start
  53.8 19.7 %collective-permute-start.8 = (bf16[18,128,128]{2,1,0:T(8,128)(2,1)S(1)}, bf16[18,128,128]{2,1,0:T(8,128)(2,1)S(1)}, u32[]{:S(2)}, u32[]{:S(2)}) collective-permute-start(bf16[18,128,128]{2,1,0:T(8,128)(2,1)S(1)} %collective-permute-done.5.refs_9_), channel_id=1, source_target_pairs={{128,0},{129,1},{130,2},{131,3},{132,4},{133,5},{134,6},{135,7},{3... | collective-permute-start | bytes 1769480 | tf_op jit(solution)/shard_map/ppermute | solution.py:172
  62.7 24.1 %collective-permute-start.10 = (bf16[16,128,128]{2,1,0:T(8,128)(2,1)S(1)}, bf16[16,128,128]{2,1,0:T(8,128)(2,1)S(1)}, u32[]{:S(2)}, u32[]{:S(2)}) collective-permute-start(bf16[16,128,128]{2,1,0:T(8,128)(2,1)S(1)} %collective-permute-done.6), channel_id=1, source_target_pairs={{96,0},{97,1},{98,2},{99,3},{100,4},{101,5},{102,6},{103,7},{104,8... | collective-permute-start | bytes 1572872 | tf_op jit(solution)/shard_map/ppermute | solution.py:172
  64.7 29.5 %collective-permute-start.7 = (bf16[31,128,128]{2,1,0:T(8,128)(2,1)}, bf16[31,128,128]{2,1,0:T(8,128)(2,1)}, u32[]{:S(2)}, u32[]{:S(2)}) collective-permute-start(bf16[31,128,128]{2,1,0:T(8,128)(2,1)} %collective-permute-done.3.refs_8_), channel_id=1, source_target_pairs={{16,0},{17,1},{18,2},{19,3},{20,4},{21,5},{22,6},{23,7},{24,8},{25... | collective-permute-start | bytes 3047432 | tf_op jit(solution)/shard_map/ppermute | solution.py:172
  73.5 31.1 %collective-permute-start.9 = (bf16[18,128,128]{2,1,0:T(8,128)(2,1)S(1)}, bf16[18,128,128]{2,1,0:T(8,128)(2,1)}, u32[]{:S(2)}, u32[]{:S(2)}) collective-permute-start(bf16[18,128,128]{2,1,0:T(8,128)(2,1)S(1)} %broadcast_select_fusion), channel_id=1, source_target_pairs={{16,0},{17,1},{18,2},{19,3},{20,4},{21,5},{22,6},{23,7},{24,8},{25... | collective-permute-start | bytes 1769480 | tf_op jit(solution)/shard_map/ppermute | solution.py:172
  75.5 49.4 %collective-permute-start = (bf16[33,128,128]{2,1,0:T(8,128)(2,1)S(1)}, bf16[33,128,128]{2,1,0:T(8,128)(2,1)}, u32[]{:S(2)}, u32[]{:S(2)}) collective-permute-start(bf16[33,128,128]{2,1,0:T(8,128)(2,1)S(1)} %pad_maximum_fusion.refs_6_), channel_id=1, source_target_pairs={{1,0},{4,1},{3,2},{6,3},{5,4},{8,5},{7,6},{10,7},{9,8},{12,9},{11,... | collective-permute-start | bytes 3244040 | tf_op jit(solution)/shard_map/ppermute | solution.py:172
  77.4 47.5 %collective-permute-start.2 = (bf16[33,128,128]{2,1,0:T(8,128)(2,1)}, bf16[33,128,128]{2,1,0:T(8,128)(2,1)}, u32[]{:S(2)}, u32[]{:S(2)}) collective-permute-start(bf16[33,128,128]{2,1,0:T(8,128)(2,1)} %collective-permute-done.1.refs_7_), channel_id=1, source_target_pairs={{1,0},{0,1},{3,2},{2,3},{5,4},{4,5},{7,6},{6,7},{9,8},{8,9},{11,10... | collective-permute-start | bytes 3244040 | tf_op jit(solution)/shard_map/ppermute | solution.py:172
  86.8 17.8 %collective-permute-start.12 = (bf16[16,128,128]{2,1,0:T(8,128)(2,1)S(1)}, bf16[16,128,128]{2,1,0:T(8,128)(2,1)}, u32[]{:S(2)}, u32[]{:S(2)}) collective-permute-start(bf16[16,128,128]{2,1,0:T(8,128)(2,1)S(1)} %collective-permute-done.10), channel_id=1, source_target_pairs={{112,0},{113,1},{114,2},{115,3},{116,4},{117,5},{118,6},{119,7},{1... | collective-permute-start | bytes 1572872 | tf_op jit(solution)/shard_map/ppermute | solution.py:172
  104.6 18.3 %collective-permute-start.13 = (bf16[16,128,128]{2,1,0:T(8,128)(2,1)}, bf16[16,128,128]{2,1,0:T(8,128)(2,1)}, u32[]{:S(2)}, u32[]{:S(2)}) collective-permute-start(bf16[16,128,128]{2,1,0:T(8,128)(2,1)} %collective-permute-done.12.refs_13_), channel_id=1, source_target_pairs={{496,0},{497,1},{498,2},{499,3},{500,4},{501,5},{502,6},{503,7},{2... | collective-permute-start | bytes 1572872 | tf_op jit(solution)/shard_map/ppermute | solution.py:172
  106.6 31.4 %collective-permute-start.11 = (bf16[31,128,128]{2,1,0:T(8,128)(2,1)}, bf16[31,128,128]{2,1,0:T(8,128)(2,1)}, u32[]{:S(2)}, u32[]{:S(2)}) collective-permute-start(bf16[31,128,128]{2,1,0:T(8,128)(2,1)} %collective-permute-done.7.refs_11_), channel_id=1, source_target_pairs={{16,0},{17,1},{18,2},{19,3},{20,4},{21,5},{22,6},{23,7},{24,8},{25... | collective-permute-start | bytes 3047432 | tf_op jit(solution)/shard_map/ppermute | solution.py:172
  116.1 31.2 %collective-permute-start.15 = (bf16[18,128,128]{2,1,0:T(8,128)(2,1)}, bf16[18,128,128]{2,1,0:T(8,128)(2,1)S(1)}, u32[]{:S(2)}, u32[]{:S(2)}) collective-permute-start(bf16[18,128,128]{2,1,0:T(8,128)(2,1)} %collective-permute-done.9.refs_12_), channel_id=1, source_target_pairs={{16,0},{17,1},{18,2},{19,3},{20,4},{21,5},{22,6},{23,7},{24,8},{25... | collective-permute-start | bytes 1769480 | tf_op jit(solution)/shard_map/ppermute | solution.py:172
  122.9 24.4 %collective-permute-start.14 = (bf16[16,128,128]{2,1,0:T(8,128)(2,1)}, bf16[16,128,128]{2,1,0:T(8,128)(2,1)S(1)}, u32[]{:S(2)}, u32[]{:S(2)}) collective-permute-start(bf16[16,128,128]{2,1,0:T(8,128)(2,1)} %collective-permute-done.13.refs_13_), channel_id=1, source_target_pairs={{496,0},{497,1},{498,2},{499,3},{500,4},{501,5},{502,6},{503,7},{2... | collective-permute-start | bytes 1572872 | tf_op jit(solution)/shard_map/ppermute | solution.py:172
  126.2 1.0 copy-start.1
